TPU v7x, 32 devices: a whole 2x2x4 slice. The times are simulated.
32 devices in a mesh: section: 2 (over x), ctx: 8 (over z, core), tp: 2 (over y).
Axes of the slice: x: 2, y: 2, z: 4, core: 2. Of those that a mesh axis runs over, the one named last changes fastest.
Arguments:
- inputs: bfloat16 [2, 1024, 1024], P(None, 'ctx'), may hold values from -6 to 6
- cotangent: bfloat16 [2, 1024, 1024], P(None, 'ctx'), may hold values from -6 to 6
- ln1_gain: bfloat16 [2, 1024], P('section'), may hold values from 0.25 to 1.75
- ln1_bias: bfloat16 [2, 1024], P('section'), may hold values from -1.75 to 1.75
- ln2_gain: bfloat16 [2, 1024], P('section'), may hold values from 0.25 to 1.75
- ln2_bias: bfloat16 [2, 1024], P('section'), may hold values from -1.75 to 1.75
- qkv_weight: bfloat16 [2, 3, 1024, 1024], P('section', None, None, 'tp'), may hold values from -0.1875 to 0.1875
- qkv_bias: bfloat16 [2, 3, 1024], P('section', None, 'tp'), may hold values from -3 to 3
- out_weight: bfloat16 [2, 1024, 1024], P('section', 'tp'), may hold values from -0.75 to 0.75
- up_weight: bfloat16 [2, 1024, 4096], P('section', None, 'tp'), may hold values from -0.1875 to 0.1875
- up_bias: bfloat16 [2, 4096], P('section', 'tp'), may hold values from -3 to 3
- down_weight: bfloat16 [2, 4096, 1024], P('section', 'tp'), may hold values from -0.09375 to 0.09375
- branch_bias: bfloat16 [2, 1024], P('section'), may hold values from -3 to 3
Outputs:
- acts: bfloat16 [2, 2, 1024, 1024], P('section', None, 'ctx')
- in_grads: bfloat16 [2, 2, 1024, 1024], P('section', None, 'ctx')
- ln1_gain_grad: float32 [2, 1024], P('section')
- ln1_bias_grad: float32 [2, 1024], P('section')
- ln2_gain_grad: float32 [2, 1024], P('section')
- ln2_bias_grad: float32 [2, 1024], P('section')
- qkv_weight_grad: float32 [2, 3, 1024, 1024], P('section', None, 'ctx', 'tp')
- qkv_bias_grad: float32 [2, 3, 1024], P('section', None, 'tp')
- out_weight_grad: float32 [2, 1024, 1024], P('section', 'tp', 'ctx')
- up_weight_grad: float32 [2, 1024, 4096], P('section', 'ctx', 'tp')
- up_bias_grad: float32 [2, 4096], P('section', 'tp')
- down_weight_grad: float32 [2, 4096, 1024], P('section', 'tp', 'ctx')
- branch_bias_grad: float32 [2, 1024], P('section')
All inputs are finite; a program needn't handle non-finite values.
Results may differ from a plain program's by a relative error of at most 0.015.
Values may be sent and summed in bfloat16 or wider, within the bound.
No kernel may reach another device: no remote copies, remote signals or barrier semaphores. Data moves between devices by JAX's collectives and lax.ppermute only.
A program may use at most 320 MiB of HBM per device.

v0:
```python
import math

import jax
import jax.numpy as jnp
from jax import lax
from jax.experimental import pallas as pl
from jax.experimental.pallas import tpu as pltpu
from jax.sharding import PartitionSpec as P

HD = 64
ROT = 16


def shifted(shard, axis, by):
    peers = lax.axis_size(axis)
    pairs = [(i, i + by) for i in range(peers) if 0 <= i + by < peers]
    return lax.ppermute(shard, axis, pairs)


def tables(positions):
    freqs = 1.0 / 10000.0 ** (jnp.arange(0, ROT, 2).astype(jnp.float32) / ROT)
    angles = positions.astype(jnp.float32)[:, None] * freqs[None, :]
    return (jnp.cos(angles)[:, None, :], jnp.sin(angles)[:, None, :])


def rotate(field, cosine, sine):
    half_rot = ROT // 2
    front = field[..., :half_rot]
    second = field[..., half_rot:ROT]
    return jnp.concatenate(
        [front * cosine - second * sine, second * cosine + front * sine, field[..., ROT:]], axis=-1
    )


def norms(hidden, gain_one, shift_one, gain_two, shift_two):
    centre = hidden - jnp.mean(hidden, axis=-1, keepdims=True)
    normed = centre * lax.rsqrt(jnp.mean(centre * centre, axis=-1, keepdims=True) + 1e-05)
    return (normed * gain_one + shift_one, normed * gain_two + shift_two)


def gelu_exact(value):
    return jax.nn.gelu(value, approximate=False)


def scores_of(queries, keys, query_pos, score_scale):
    raw = jnp.einsum("qhd,khd->hqk", queries, keys, preferred_element_type=jnp.float32)
    key_pos = jnp.arange(keys.shape[0], dtype=jnp.int32)
    return jnp.where(
        key_pos[None, None, :] <= query_pos[None, :, None], raw * score_scale, -1000000000.0
    )


def forward_layer(layer_in, weights, query_pos, cosine, sine):
    gains, w_qkv, b_qkv, w_out, w_up, b_up, w_down, b_branch = weights
    hidden = layer_in.astype(jnp.float32)
    attn_norm, mlp_norm = norms(hidden, gains[0], gains[1], gains[2], gains[3])
    attn_in = attn_norm.astype(jnp.bfloat16)
    mlp_in = mlp_norm.astype(jnp.bfloat16)
    projected = (
        jnp.einsum("td,cdf->tcf", attn_in, w_qkv, preferred_element_type=jnp.float32) + b_qkv
    )
    row_count = hidden.shape[0]
    feat_width = projected.shape[2]
    head_count = feat_width // HD
    queries = rotate(projected[:, 0].reshape(row_count, head_count, HD), cosine, sine).astype(
        jnp.bfloat16
    )
    key_flat = (
        rotate(projected[:, 1].reshape(row_count, head_count, HD), cosine, sine)
        .astype(jnp.bfloat16)
        .reshape(row_count, feat_width)
    )
    value_flat = projected[:, 2].astype(jnp.bfloat16)
    all_keys, all_values = (
        lax.all_gather(key_flat, "ctx", axis=0, tiled=True),
        lax.all_gather(value_flat, "ctx", axis=0, tiled=True),
    )
    key_count = all_keys.shape[0]
    score_scale = 1.0 / math.sqrt(HD)
    scores = scores_of(queries, all_keys.reshape(key_count, head_count, HD), query_pos, score_scale)
    row_max = jnp.max(scores, axis=-1, keepdims=True)
    exponent = jnp.exp(scores - row_max)
    summed = jnp.sum(exponent, axis=-1, keepdims=True)
    probability = (exponent / summed).astype(jnp.bfloat16)
    log_total = row_max + jnp.log(summed)
    mixed = jnp.einsum(
        "hqk,khd->qhd",
        probability,
        all_values.reshape(key_count, head_count, HD),
        preferred_element_type=jnp.float32,
    )
    mixed = mixed.reshape(row_count, feat_width).astype(jnp.bfloat16)
    partial_out = jnp.dot(mixed, w_out, preferred_element_type=jnp.float32)
    up_value = jnp.dot(mlp_in, w_up, preferred_element_type=jnp.float32) + b_up
    active = gelu_exact(up_value).astype(jnp.bfloat16)
    partial_out = partial_out + jnp.dot(active, w_down, preferred_element_type=jnp.float32)
    branches = lax.psum(partial_out, "tp")
    layer_out = (hidden + branches + b_branch).astype(jnp.bfloat16)
    stored = (key_flat, value_flat)
    saved = (layer_in, queries, stored, log_total, mixed, up_value, active)
    return (layer_out, saved)


def backward_layer(grad_out, saved, weights, query_pos, cosine, sine):
    gains, w_qkv, b_qkv, w_out, w_up, b_up, w_down, b_branch = weights
    layer_in, queries, stored, log_total, mixed, up_value, active = saved
    grad_full = grad_out.astype(jnp.float32)
    row_count, feat_width = mixed.shape
    head_count = feat_width // HD
    hidden = layer_in.astype(jnp.float32)
    norm_pair, norm_back = jax.vjp(norms, hidden, gains[0], gains[1], gains[2], gains[3])
    attn_in = norm_pair[0].astype(jnp.bfloat16)
    mlp_in = norm_pair[1].astype(jnp.bfloat16)
    active_grad = jnp.einsum("td,fd->tf", grad_out, w_down, preferred_element_type=jnp.float32)
    grad_down = jnp.einsum("tf,td->fd", active, grad_out, preferred_element_type=jnp.float32)
    gelu_back = jax.vjp(gelu_exact, up_value)[1]
    up_grad = gelu_back(active_grad)[0].astype(jnp.bfloat16)
    grad_up_bias = jnp.sum(up_grad.astype(jnp.float32), axis=0)
    grad_up = jnp.einsum("td,tf->df", mlp_in, up_grad, preferred_element_type=jnp.float32)
    mlp_in_grad = jnp.einsum("tf,df->td", up_grad, w_up, preferred_element_type=jnp.float32)
    mixed_grad = jnp.einsum(
        "td,fd->tf", grad_out, w_out, preferred_element_type=jnp.float32
    ).astype(jnp.bfloat16)
    grad_out_weight = jnp.einsum("tf,td->fd", mixed, grad_out, preferred_element_type=jnp.float32)
    all_keys, all_values = (
        lax.all_gather(stored[0], "ctx", axis=0, tiled=True),
        lax.all_gather(stored[1], "ctx", axis=0, tiled=True),
    )
    key_count = all_keys.shape[0]
    keys_heads = all_keys.reshape(key_count, head_count, HD)
    values_heads = all_values.reshape(key_count, head_count, HD)
    score_scale = 1.0 / math.sqrt(HD)
    scores = scores_of(queries, keys_heads, query_pos, score_scale)
    probability = jnp.exp(scores - log_total)
    heads_grad = mixed_grad.reshape(row_count, head_count, HD)
    prob_grad = jnp.einsum(
        "qhd,khd->hqk", heads_grad, values_heads, preferred_element_type=jnp.float32
    )
    centre = jnp.sum(probability * prob_grad, axis=-1, keepdims=True)
    score_grad = (score_scale * probability * (prob_grad - centre)).astype(jnp.bfloat16)
    query_grad = jnp.einsum(
        "hqk,khd->qhd", score_grad, keys_heads, preferred_element_type=jnp.float32
    )
    value_terms = jnp.einsum(
        "hqk,qhd->khd",
        probability.astype(jnp.bfloat16),
        heads_grad,
        preferred_element_type=jnp.float32,
    )
    key_terms = jnp.einsum("hqk,qhd->khd", score_grad, queries, preferred_element_type=jnp.float32)
    key_grad, value_grad = (
        lax.psum_scatter(
            key_terms.reshape(key_count, feat_width), "ctx", scatter_dimension=0, tiled=True
        ),
        lax.psum_scatter(
            value_terms.reshape(key_count, feat_width), "ctx", scatter_dimension=0, tiled=True
        ),
    )
    query_grad = rotate(query_grad, cosine, -sine).reshape(row_count, feat_width)
    key_grad = rotate(key_grad.reshape(row_count, head_count, HD), cosine, -sine).reshape(
        row_count, feat_width
    )
    qkv_grad = jnp.stack([query_grad, key_grad, value_grad], axis=1).astype(jnp.bfloat16)
    grad_qkv_bias = jnp.sum(qkv_grad.astype(jnp.float32), axis=0)
    grad_qkv = jnp.einsum("td,tcf->cdf", attn_in, qkv_grad, preferred_element_type=jnp.float32)
    attn_in_grad = jnp.einsum("tcf,cdf->td", qkv_grad, w_qkv, preferred_element_type=jnp.float32)
    attn_in_grad, mlp_in_grad = lax.psum((attn_in_grad, mlp_in_grad), "tp")
    hidden_grad, gain_one_grad, shift_one_grad, gain_two_grad, shift_two_grad = norm_back(
        (attn_in_grad, mlp_in_grad)
    )
    input_grad = (grad_full + hidden_grad).astype(jnp.bfloat16)
    grad_branch = jnp.sum(grad_full, axis=0)
    grads = (
        gain_one_grad,
        shift_one_grad,
        gain_two_grad,
        shift_two_grad,
        grad_qkv,
        grad_qkv_bias,
        grad_out_weight,
        grad_up,
        grad_up_bias,
        grad_down,
        grad_branch,
    )
    return (input_grad, grads)


def per_device(
    inputs,
    cotangent,
    ln1_gain,
    ln1_bias,
    ln2_gain,
    ln2_bias,
    qkv_weight,
    qkv_bias,
    out_weight,
    up_weight,
    up_bias,
    down_weight,
    branch_bias,
):
    gains = (
        ln1_gain[0].astype(jnp.float32),
        ln1_bias[0].astype(jnp.float32),
        ln2_gain[0].astype(jnp.float32),
        ln2_bias[0].astype(jnp.float32),
    )
    weights = (
        gains,
        qkv_weight[0],
        qkv_bias[0].astype(jnp.float32),
        out_weight[0],
        up_weight[0],
        up_bias[0].astype(jnp.float32),
        down_weight[0],
        branch_bias[0].astype(jnp.float32),
    )
    micro_count = inputs.shape[0]
    row_count = inputs.shape[1]
    query_pos = lax.axis_index("ctx") * row_count + jnp.arange(row_count, dtype=jnp.int32)
    cosine, sine = tables(query_pos)
    at_first = lax.axis_index("section") == 0
    blank = jnp.zeros_like(inputs[0])
    received = blank
    outputs_list = []
    saved_list = []
    for step_index in range(micro_count + 1):
        fresh = inputs[step_index] if step_index < micro_count else blank
        layer_in = jnp.where(at_first, fresh, received)
        layer_out, saved = forward_layer(layer_in, weights, query_pos, cosine, sine)
        outputs_list.append(layer_out)
        saved_list.append(saved)
        if step_index < micro_count:
            received = shifted(layer_out, "section", 1)
    returned = blank
    grad_list = []
    sums = None
    for back_index in range(micro_count + 1):
        batch_index = micro_count - 1 - back_index
        given = cotangent[batch_index] if batch_index >= 0 else blank
        grad_in = jnp.where(at_first, returned, given)
        input_grad, grads = backward_layer(
            grad_in, saved_list[micro_count - back_index], weights, query_pos, cosine, sine
        )
        sums = grads if sums is None else jax.tree.map(jnp.add, sums, grads)
        grad_list.append(input_grad)
        if back_index < micro_count:
            returned = shifted(input_grad, "section", -1)
    acts = jnp.stack(
        [jnp.where(at_first, outputs_list[j], outputs_list[j + 1]) for j in range(micro_count)]
    )[None]
    in_grads = jnp.stack(
        [
            jnp.where(at_first, grad_list[micro_count - j], grad_list[micro_count - 1 - j])
            for j in range(micro_count)
        ]
    )[None]
    (
        gain_one_grad,
        shift_one_grad,
        gain_two_grad,
        shift_two_grad,
        grad_qkv,
        grad_qkv_bias,
        grad_out_weight,
        grad_up,
        grad_up_bias,
        grad_down,
        grad_branch,
    ) = sums
    qkv_part, out_part, up_part, down_part = (
        lax.psum_scatter(
            grad_qkv[None].astype(jnp.bfloat16), "ctx", scatter_dimension=2, tiled=True
        ).astype(jnp.float32),
        lax.psum_scatter(
            grad_out_weight[None].astype(jnp.bfloat16), "ctx", scatter_dimension=2, tiled=True
        ).astype(jnp.float32),
        lax.psum_scatter(
            grad_up[None].astype(jnp.bfloat16), "ctx", scatter_dimension=1, tiled=True
        ).astype(jnp.float32),
        lax.psum_scatter(
            grad_down[None].astype(jnp.bfloat16), "ctx", scatter_dimension=2, tiled=True
        ).astype(jnp.float32),
    )
    small_sums = (
        lax.psum(gain_one_grad[None].astype(jnp.bfloat16), "ctx").astype(jnp.float32),
        lax.psum(shift_one_grad[None].astype(jnp.bfloat16), "ctx").astype(jnp.float32),
        lax.psum(gain_two_grad[None].astype(jnp.bfloat16), "ctx").astype(jnp.float32),
        lax.psum(shift_two_grad[None].astype(jnp.bfloat16), "ctx").astype(jnp.float32),
        lax.psum(grad_qkv_bias[None].astype(jnp.bfloat16), "ctx").astype(jnp.float32),
        lax.psum(grad_up_bias[None].astype(jnp.bfloat16), "ctx").astype(jnp.float32),
        lax.psum(grad_branch[None].astype(jnp.bfloat16), "ctx").astype(jnp.float32),
    )
    return (
        acts,
        in_grads,
        small_sums[0],
        small_sums[1],
        small_sums[2],
        small_sums[3],
        qkv_part,
        small_sums[4],
        out_part,
        up_part,
        small_sums[5],
        down_part,
        small_sums[6],
    )


ALL = ("section", "ctx", "tp")
SECTION, HALF, NEAR, CORE, SIDE = 16, 8, 4, 2, 1
CHIPS = (0, SIDE, NEAR, NEAR | SIDE, SECTION, SECTION | SIDE, SECTION | NEAR, SECTION | NEAR | SIDE)
F32, B16 = jnp.float32, jnp.bfloat16
ONE = 128
S_SECTION, S_HALF, S_NEAR, S_CORE, S_SIDE, S_CHIP, S_OWN, S_GIVE = range(8)


def swapped(array, mask, section=None):
    pairs = [(i, i ^ mask) for i in range(32) if section is None or i // 16 == section]
    return lax.ppermute(array, ALL, pairs)


def after(array, *earlier):
    return lax.optimization_barrier((array,) + earlier)[0]


def where_am_i():
    section = lax.axis_index("section")
    ctx = lax.axis_index("ctx")
    side = lax.axis_index("tp")
    half, near, core = ctx // 4, (ctx // 2) % 2, ctx % 2
    chip = 4 * section + 2 * near + side
    own, give = 2 * section + near, 2 * (1 - section) + near
    return jnp.stack([section, half, near, core, side, chip, own, give]).astype(jnp.int32)


def in_hbm(arrays):
    return [pltpu.with_memory_space_constraint(a, pltpu.HBM) for a in arrays]


def kernel_call(body, outs, at, *arrays, hbm=(), scratch=(), flops=0, exps=0, name=None, keep=True):
    moved = sum(a.size * a.dtype.itemsize for a in arrays)
    moved += sum(math.prod(s) * jnp.dtype(d).itemsize for s, d in outs)
    return pl.pallas_call(
        body,
        name=name,
        out_shape=[(pltpu.VMEM if keep else jax.ShapeDtypeStruct)(s, d) for s, d in outs],
        in_specs=[pl.BlockSpec(memory_space=pltpu.SMEM)]
        + [pl.BlockSpec(memory_space=pltpu.VMEM)] * len(arrays)
        + [pl.BlockSpec(memory_space=pltpu.HBM)] * len(hbm),
        out_specs=[pl.BlockSpec(memory_space=pltpu.VMEM)] * len(outs),
        scratch_shapes=list(scratch),
        compiler_params=pltpu.CompilerParams(vmem_limit_bytes=VMEM_BYTES),
        cost_estimate=pl.CostEstimate(flops=0, bytes_accessed=0, transcendentals=0),
    )(at, *arrays, *in_hbm(hbm))


VMEM_BYTES = 12 * 1024 * 1024


def kernel_call_named(name, *args, **kwargs):
    return kernel_call(*args, name=name, **kwargs)


def by_rows(rows, step, do):
    def one(i, _):
        do(pl.ds(pl.multiple_of(i * step, step), step))
        return 0

    lax.fori_loop(0, rows // step, one, 0)


def nn(a, b):
    return jnp.dot(a, b, preferred_element_type=F32)


def nt(a, b):
    return lax.dot_general(a, b, (((1,), (1,)), ((), ())), preferred_element_type=F32)


def tn(a, b):
    return lax.dot_general(a, b, (((0,), (0,)), ((), ())), preferred_element_type=F32)


def copy_kernel(name, body, outs, at, arrays, scratch):
    return pl.pallas_call(
        body,
        name=name,
        out_shape=[jax.ShapeDtypeStruct(s, B16) for s in outs],
        in_specs=[pl.BlockSpec(memory_space=pltpu.SMEM)]
        + [pl.BlockSpec(memory_space=pltpu.HBM)] * len(arrays),
        out_specs=[pl.BlockSpec(memory_space=pltpu.HBM)] * len(outs),
        scratch_shapes=list(scratch),
        compiler_params=pltpu.CompilerParams(vmem_limit_bytes=VMEM_BYTES),
        cost_estimate=pl.CostEstimate(flops=0, bytes_accessed=0, transcendentals=0),
    )(at, *in_hbm(arrays))


def token_copies(at, array, mine, strip, sems):
    width = strip.shape[1]
    lanes = pl.ds(pl.multiple_of(at[S_SIDE] * width, width), width)
    return [
        pltpu.make_async_copy(array.at[at[S_HALF]], mine, sems.at[0]),
        pltpu.make_async_copy(array.at[1 - at[S_HALF], :, lanes], strip, sems.at[1]),
    ]


def token_shapes(array):
    _, rows, dim = array.shape
    return [(rows, dim), (rows, dim // 2)]


def send_tokens(mine, strip):
    near = swapped(mine, NEAR)
    far = swapped(strip, HALF)
    far_near = swapped(strip, HALF | NEAR)
    return mine, near, far, far_near, swapped(far, SIDE), swapped(far_near, SIDE)


def start_loader(at, refs):
    mine, near, far, far_near, far_rest, far_near_rest = refs
    first = at[S_SIDE] == 0
    index = 2 * at[S_HALF] + at[S_NEAR]

    def whole(strip, rest):
        a, b = strip[...], rest[...]
        return jnp.concatenate([jnp.where(first, a, b), jnp.where(first, b, a)], axis=1)

    yield index, mine[...]
    yield index ^ 1, near[...]
    yield index ^ 2, whole(far, far_rest)
    yield index ^ 3, whole(far_near, far_near_rest)


def piece_loader(at, refs):
    for step, ref in zip(STEPS, refs):
        for i in range(2):
            yield at[S_CHIP] ^ (step | 2 * i), ref[i]


def run_copies(copies):
    for copy in copies:
        copy.start()
    for copy in copies:
        copy.wait()


def pack_first(at, tokens, vectors, w_qkv):
    _, three, dim, wide = w_qkv.shape
    heads, side = wide // 4, dim // 2
    count = len(vectors)

    def body(at, tokens, w_qkv, *refs):
        lines = refs[:count]
        mine, strip, packed, table, rounded, sems = refs[count : count + 6]
        held = refs[count + 6 :]
        rows = pl.ds(pl.multiple_of(at[S_CORE] * side, side), side)
        lanes = pl.ds(pl.multiple_of(at[S_GIVE] * heads, heads), heads)
        copies = token_copies(at, tokens, mine, strip, sems)
        for i in range(three):
            copies.append(
                pltpu.make_async_copy(
                    w_qkv.at[0, i, rows, lanes], packed.at[i * side : (i + 1) * side], sems.at[2 + i]
                )
            )
        loads = [
            pltpu.make_async_copy(line, hold, sems.at[6 + i])
            for i, (line, hold) in enumerate(zip(lines, held))
        ]
        for copy in copies:
            copy.start()
        run_copies(loads)
        fill_table(table, at[S_GIVE], held)
        rounded[...] = table[...].astype(B16)
        run_copies([pltpu.make_async_copy(rounded, packed.at[three * side :], sems.at[5])])
        for copy in copies:
            copy.wait()

    return copy_kernel(
        "pack_first", body, token_shapes(tokens) + [(three * side + TABLE, ONE)], at,
        [tokens, w_qkv, *vectors],
        [pltpu.VMEM((TABLE, ONE), F32), pltpu.VMEM((TABLE, ONE), B16), pltpu.SemaphoreType.DMA((6 + count,))]
        + [pltpu.VMEM(v.shape, B16) for v in vectors],
    )


def pack_second(at, tokens, w_up, w_out, w_down):
    dim, units, heads = w_up.shape[1], w_up.shape[2] // 4, w_out.shape[1] // 4
    side = dim // 2

    def body(at, tokens, w_up, w_out, w_down, mine, strip, up, down, sems):
        copies = token_copies(at, tokens, mine, strip, sems)
        rows = pl.ds(pl.multiple_of(at[S_CORE] * side, side), side)
        lanes = pl.ds(pl.multiple_of(at[S_GIVE] * units, units), units)
        copies.append(pltpu.make_async_copy(w_up.at[0, rows, lanes], up, sems.at[2]))
        part = 2 * at[S_GIVE] + at[S_CORE]
        for i, (source, size, start) in enumerate(
            ((w_down, units // 2, 0), (w_out, heads // 2, units // 2))
        ):
            rows = pl.ds(pl.multiple_of(part * size, size), size)
            copies.append(
                pltpu.make_async_copy(
                    source.at[0, rows], down.at[start : start + size], sems.at[3 + i]
                )
            )
        run_copies(copies)

    return copy_kernel(
        "pack_second", body, token_shapes(tokens) + [(side, units), ((units + heads) // 2, dim)], at,
        [tokens, w_up, w_out, w_down], [pltpu.SemaphoreType.DMA((5,))],
    )


def fill_table(table, index, vectors):
    *lines, b_up, b_qkv = vectors
    units, heads = b_up.shape[1] // 4, b_qkv.shape[2] // 4
    table[...] = jnp.zeros_like(table)
    row = 0
    for line in lines:
        for i in range(line.shape[1] // ONE):
            table[row : row + 1] = line[:, i * ONE : (i + 1) * ONE].astype(F32)
            row += 1
    for i in range(units // ONE):
        lanes = pl.ds(pl.multiple_of(index * units + i * ONE, ONE), ONE)
        table[row : row + 1] = b_up[:, lanes].astype(F32)
        row += 1
    few = b_qkv[0, :, pl.ds(pl.multiple_of(index * heads, ONE), heads)].astype(F32)
    table[row : row + few.shape[0]] = few


TABLE = 48


def vector_rows(at, vectors, got):
    dim = vectors[0].shape[1]
    units, few = vectors[5].shape[1] // 4, vectors[6].shape[1]

    def body(at, *refs):
        *lines, got, rows0, rows1, table = refs
        fill_table(table, at[S_OWN], lines)
        taken = got[got.shape[0] - TABLE :].astype(F32)
        is_first = at[S_SECTION] == 0
        for rows, lines in (
            (rows0, jnp.where(is_first, table[...], taken)),
            (rows1, jnp.where(is_first, taken, table[...])),
        ):
            rows[...] = jnp.zeros_like(rows)
            line = 0
            for r, tiles in enumerate([dim // ONE] * 5 + [units // ONE, few]):
                for i in range(tiles):
                    rows[r : r + 1, i * ONE : (i + 1) * ONE] = lines[line : line + 1]
                    line += 1

    return kernel_call_named(
        "vector_rows", body, [((8, dim), F32)] * 2, at, *vectors, got,
        scratch=[pltpu.VMEM((TABLE, ONE), F32)],
    )


def half_rows(at, which, size):
    return pl.ds(pl.multiple_of((at[S_CORE] ^ which) * size, size), size)


def qkv_copies(at, own, got, rest, target):
    three, heads = own.shape[1], own.shape[3] // 4
    side = own.shape[2] // 2
    lanes = pl.ds(pl.multiple_of(at[S_OWN] * heads, heads), heads)
    mine, halves = [], []
    for i in range(three):
        tile = slice(i * heads, (i + 1) * heads)
        mine.append((own.at[0, i, :, lanes], target[0].at[:, tile]))
        for which, source in ((0, got), (1, rest)):
            halves.append(
                (
                    source.at[i * side : (i + 1) * side],
                    target[1].at[half_rows(at, which, side), tile],
                )
            )
    return mine + halves


def up_copies(at, own, got, rest, target):
    side, units = got.shape
    lanes = pl.ds(pl.multiple_of(at[S_OWN] * units, units), units)
    return [(own.at[0, :, lanes], target[0])] + [
        (source, target[1].at[half_rows(at, which, side)])
        for which, source in ((0, got), (1, rest))
    ]


def row_copies(at, own, got, rest, target, start):
    size = target[0].shape[0]
    side = size // 2
    rows = pl.ds(pl.multiple_of(at[S_OWN] * size, size), size)
    return [(own.at[0, rows], target[0])] + [
        (source.at[start : start + side], target[1].at[half_rows(at, which, side)])
        for which, source in ((0, got), (1, rest))
    ]


def choose_weights(name, at, owns, got, rest, shapes, make):
    count = len(owns)

    def body(at, *refs):
        own, (got, rest), targets, sems = refs[:count], refs[count : count + 2], refs[count + 2 : -1], refs[-1]
        for section in range(2):

            @pl.when(at[S_SECTION] == section)
            def _():
                pairs = make(
                    at, own, got, rest,
                    [(targets[2 * i + section], targets[2 * i + 1 - section]) for i in range(count)],
                )
                run_copies(
                    [
                        pltpu.make_async_copy(source, target, sems.at[i])
                        for i, (source, target) in enumerate(pairs)
                    ]
                )

    outs = [(shape, B16) for shape in shapes for _ in range(2)]
    return kernel_call(
        body, outs, at, hbm=[*owns, got, rest],
        scratch=[pltpu.SemaphoreType.DMA((9,))], name=name,
    )


def weights_call(name, body, outs, at, arrays, weights, scratch=(), flops=0, exps=0):
    first, count = len(arrays), len(weights)

    def wrapped(at, *refs):
        given, chosen, rest = refs[:first], refs[first : first + count], refs[first + count :]
        made, own = rest[: len(outs)], rest[len(outs) :]
        body(at, *given, *made, *chosen, *own)

    return kernel_call(
        wrapped, outs, at, *arrays, *weights, scratch=scratch, flops=flops, exps=exps, name=name
    )


def first_weights(at, vectors, w_qkv, sent):
    _, three, dim, wide = w_qkv.shape
    got = swapped(sent, SECTION)
    qkv = choose_weights(
        "choose_qkv", at, [w_qkv], got, swapped(got, CORE), [(dim, three * (wide // 4))],
        lambda at, own, got, rest, to: qkv_copies(at, own[0], got, rest, to[0]),
    )
    return got, [dict(qkv=q, rows=r) for q, r in zip(qkv, vector_rows(at, vectors, got))]


def up_weights(at, w_up, got, rest):
    return choose_weights(
        "choose_up", at, [w_up], got, rest, [(w_up.shape[1], w_up.shape[2] // 4)],
        lambda at, own, got, rest, to: up_copies(at, own[0], got, rest, to[0]),
    )


def row_weights(at, w_down, w_out, got, rest):
    _, tall, dim = w_down.shape
    units, heads = tall // 4, w_out.shape[1] // 4
    return choose_weights(
        "choose_rows", at, [w_down, w_out], got, rest, [(units, dim), (heads, dim)],
        lambda at, own, got, rest, to: row_copies(at, own[0], got, rest, to[0], 0)
        + row_copies(at, own[1], got, rest, to[1], units // 2),
    )


def turn_tables(at, rows):
    half_rot = ROT // 2
    place = lax.broadcasted_iota(jnp.int32, (rows, ONE), 0)
    lane = lax.broadcasted_iota(jnp.int32, (rows, ONE), 1) % HD
    positions = (2 * (place // ONE) + at[S_CORE]) * ONE + place % ONE
    freqs = 1.0 / 10000.0 ** ((2 * (lane % half_rot)).astype(F32) / ROT)
    angles = positions.astype(F32) * freqs
    sine = jnp.sin(angles)
    return (
        jnp.where(lane < ROT, jnp.cos(angles), 1.0),
        jnp.where((lane >= half_rot) & (lane < ROT), sine, 0.0),
        jnp.where(lane < half_rot, -sine, 0.0),
    )


def keep_blocks(at, source, blocks):
    mine, give = blocks
    place = (2 * at[S_HALF] + at[S_NEAR]) * ONE
    mine[...] = source[pl.ds(pl.multiple_of(place, ONE), ONE)]
    size = give.shape[0]
    place = (2 * (1 - at[S_HALF]) + at[S_NEAR]) * ONE + at[S_SIDE] * size
    give[...] = source[pl.ds(pl.multiple_of(place, size), size)]


def keep_piece(at, source, piece):
    size = piece.shape[0]
    piece[...] = source[pl.ds(pl.multiple_of(at[S_CHIP] * size, size), size)]


def front(at, loader, sources, w, turns, with_piece):
    dim = w["qkv"].shape[0]
    rows = turns[0].shape[0]
    count = len(sources)

    def body(at, *refs):
        given = refs[:count]
        vectors, *turns = refs[count : count + 4]
        attn_in, mlp_in, normed_out, q, kv = refs[count + 4 : count + 9]
        *kept, qkv, ordered = refs[count + 9 :]
        gains = [vectors[i : i + 1] for i in range(4)]
        for place, block in loader(at, given):
            size = block.shape[0]
            ordered[pl.ds(pl.multiple_of(place * size, size), size)] = block
        if with_piece:
            keep_piece(at, ordered, kept[0])
        else:
            keep_blocks(at, ordered, kept)
        bias = vectors[6:7, : 3 * ONE]

        def norm(span):
            hidden = ordered[span].astype(F32)
            mean = jnp.sum(hidden, axis=1, keepdims=True) * (1.0 / dim)
            centre = hidden - mean
            var = jnp.sum(centre * centre, axis=1, keepdims=True) * (1.0 / dim)
            normed = centre * lax.rsqrt(var + 1e-05)
            attn_in[span] = (normed * gains[0] + gains[1]).astype(B16)
            mlp_in[span] = (normed * gains[2] + gains[3]).astype(B16)
            normed_out[span] = normed.astype(B16)

        def project(span):
            projected = nn(attn_in[span], qkv[...]) + bias
            cosine, second, first_half = [table[span] for table in turns]
            for i, target in ((0, q), (1, kv.at[0])):
                flat = projected[:, i * ONE : (i + 1) * ONE]
                flat = (
                    flat * cosine
                    + pltpu.roll(flat, ROT // 2, 1) * second
                    + pltpu.roll(flat, ONE - ROT // 2, 1) * first_half
                )
                target[span] = flat.astype(B16)
            kv[1, span] = projected[:, 2 * ONE :].astype(B16)

        by_rows(rows, 128, norm)
        by_rows(rows, 256, project)

    outs = [((rows, dim), B16)] * 3 + [((rows, ONE), B16), ((2, rows, ONE), B16)]
    outs += [((rows // 8, dim), B16)] if with_piece else [((n, dim), B16) for n in (ONE, ONE // 2)]
    return weights_call(
        "front", body, outs, at, [*sources, w["rows"], *turns], [w["qkv"]],
        scratch=[pltpu.VMEM((rows, dim), B16)],
        flops=2 * rows * dim * 3 * ONE + 20 * rows * dim,
    )


def units_forward(at, mlp_in, w):
    rows, dim = mlp_in.shape
    units = w["units"]

    def body(at, mlp_in, vectors, active, slope, up):
        bias = vectors[5:6, :units]

        def gelu(span):
            value = nn(mlp_in[span], up[...]) + bias
            cdf = 0.5 + 0.5 * lax.erf(value * (1.0 / math.sqrt(2.0)))
            pdf = jnp.exp(value * value * -0.5) * (1.0 / math.sqrt(2.0 * math.pi))
            active[span] = (value * cdf).astype(B16)
            slope[span] = (cdf + value * pdf).astype(B16)

        by_rows(rows, 128, gelu)

    return weights_call(
        "units_forward", body, [((rows, units), B16)] * 2, at, [mlp_in, w["rows"]], [w["up"]],
        flops=2 * rows * dim * units + 40 * rows * units, exps=rows * units,
    )


def head_lanes():
    return lax.broadcasted_iota(jnp.int32, (1, ONE), 1) < HD


def allowed_keys(at, first, step, count):
    row = lax.broadcasted_iota(jnp.int32, (step, count), 0) + first
    column = lax.broadcasted_iota(jnp.int32, (step, count), 1)
    return column <= row, column < (row // ONE + at[S_CORE]) * ONE


STEPS = (0, 1, 4, 5)
STEP_CHIPS = (0, SIDE, SECTION, SECTION | SIDE)


def pieces_out(at, total, pieces):
    size = total.shape[0] // 8
    for step, piece in zip(STEPS, pieces):
        for i in range(2):
            place = (at[S_CHIP] ^ (step | 2 * i)) * size
            piece[i] = total[pl.ds(pl.multiple_of(place, size), size)].astype(piece.dtype)


def piece_shapes(rows, dim):
    return [((2, rows // 8, dim), F32)] + [((2, rows // 8, dim), B16)] * 3


def fold(at, pieces):
    _, rows, dim = pieces[0].shape

    def body(at, *refs):
        *given, keep, give = refs
        for i, target in ((0, keep), (1, give)):
            total = given[0][i]
            for piece in given[1:]:
                total = total + piece[i].astype(F32)
            target[...] = total.astype(target.dtype)

    return kernel_call_named("fold", body, [((rows, dim), F32), ((rows, dim), B16)], at, *pieces)


def exchanged(pieces):
    return [pieces[0]] + [swapped(p, m) for p, m in zip(pieces[1:], STEP_CHIPS[1:])]


def gathered(piece, near):
    pair = jnp.stack([piece, near])
    return [pair] + [swapped(pair, mask) for mask in STEP_CHIPS[1:]]


def attention_forward(at, q, kv, kv_other, active, w):
    rows = q.shape[0]
    units, dim = w["down"].shape
    scale = 1.0 / math.sqrt(HD)

    def body(at, q, kv, kv_other, active, mixed, lse, *rest):
        pieces, (out, down, total) = rest[:4], rest[4:]
        first_head = head_lanes()
        step = 256
        for first in range(0, rows, step):
            span = slice(first, first + step)
            count = first + step
            queries = q[span]
            masks = allowed_keys(at, first, step, count)
            results, totals = [], []
            for head in range(2):
                lanes = first_head if head == 0 else jnp.logical_not(first_head)
                one = jnp.where(lanes, queries, jnp.zeros_like(queries))
                scores = [
                    jnp.where(mask, nt(one, keys[0, :count]) * scale, -1e9)
                    for mask, keys in zip(masks, (kv, kv_other))
                ]
                most = jnp.maximum(
                    jnp.max(scores[0], axis=1, keepdims=True),
                    jnp.max(scores[1], axis=1, keepdims=True),
                )
                exponents = [jnp.exp(s - most) for s in scores]
                summed = jnp.sum(exponents[0], axis=1, keepdims=True) + jnp.sum(
                    exponents[1], axis=1, keepdims=True
                )
                inverse = 1.0 / summed
                results.append(
                    nn((exponents[0] * inverse).astype(B16), kv[1, :count])
                    + nn((exponents[1] * inverse).astype(B16), kv_other[1, :count])
                )
                totals.append(most + jnp.log(summed))
            mixed[span] = jnp.where(first_head, results[0], results[1]).astype(B16)
            lse[span] = jnp.where(first_head, totals[0], totals[1])
            total[span] = nn(mixed[span], out[...]) + nn(active[span], down[...])
        pieces_out(at, total, pieces)

    outs = [((rows, ONE), B16), ((rows, ONE), F32)] + piece_shapes(rows, dim)
    return weights_call(
        "attention_forward", body, outs, at, [q, kv, kv_other, active], [w["out"], w["down"]],
        scratch=[pltpu.VMEM((rows, dim), F32)],
        flops=2 * rows * dim * (units + ONE) + 8 * rows * rows * ONE * 2,
        exps=2 * rows * rows * 2,
    )


def units_backward(at, loader, sources, slope, w, with_piece):
    rows, units = slope.shape
    dim = w["up"].shape[0]
    count = len(sources)

    def body(at, *refs):
        given = refs[:count]
        slope, g, up_grad, mixed_grad = refs[count : count + 4]
        *kept, down, out = refs[count + 4 :]
        for place, block in loader(at, given):
            size = block.shape[0]
            g[pl.ds(pl.multiple_of(place * size, size), size)] = block
        if with_piece:
            keep_piece(at, g, kept[0])
        else:
            keep_blocks(at, g, kept)

        def back(span):
            up_grad[span] = (nt(g[span], down[...]) * slope[span].astype(F32)).astype(B16)
            mixed_grad[span] = nt(g[span], out[...]).astype(B16)

        by_rows(rows, 256, back)

    outs = [((rows, dim), B16), ((rows, units), B16), ((rows, ONE), B16)]
    outs += [((rows // 8, dim), B16)] if with_piece else [((n, dim), B16) for n in (ONE, ONE // 2)]
    return weights_call(
        "units_backward", body, outs, at, [*sources, slope], [w["down"], w["out"]],
        flops=2 * rows * dim * (units + ONE),
    )


def attention_backward(at, q, kv, kv_other, lse, mixed_grad):
    rows = q.shape[0]
    scale = 1.0 / math.sqrt(HD)

    def body(at, q, kv, kv_other, lse, mixed_grad, dq, dkv, dkv_other):
        first_head = head_lanes()
        step = 256
        dkv[...] = jnp.zeros_like(dkv)
        dkv_other[...] = jnp.zeros_like(dkv_other)
        for first in range(0, rows, step):
            span = slice(first, first + step)
            count = first + step
            queries, back = q[span], mixed_grad[span]
            masks = allowed_keys(at, first, step, count)
            sides = ((masks[0], kv, dkv), (masks[1], kv_other, dkv_other))
            results = []
            for head in range(2):
                lanes = first_head if head == 0 else jnp.logical_not(first_head)
                one = jnp.where(lanes, queries, jnp.zeros_like(queries))
                one_back = jnp.where(lanes, back, jnp.zeros_like(back))
                level = lse[span, head * HD : head * HD + 1]
                probs, grads = [], []
                for mask, keys, _ in sides:
                    scores = nt(one, keys[0, :count]) * scale
                    probs.append(jnp.exp(jnp.where(mask, scores, -1e9) - level))
                    grads.append(nt(one_back, keys[1, :count]))
                delta = jnp.sum(probs[0] * grads[0], axis=1, keepdims=True) + jnp.sum(
                    probs[1] * grads[1], axis=1, keepdims=True
                )
                result = 0.0
                for (_, keys, target), prob, grad in zip(sides, probs, grads):
                    score_grad = (prob * (grad - delta) * scale).astype(B16)
                    result = result + nn(score_grad, keys[0, :count])
                    target[0, :count] += tn(score_grad, one)
                    target[1, :count] += tn(prob.astype(B16), one_back)
                results.append(result)
            dq[span] = jnp.where(first_head, results[0], results[1])

    return kernel_call_named(
        "attention_backward",
        body, [((rows, ONE), F32), ((2, rows, ONE), F32), ((2, rows, ONE), F32)],
        at, q, kv, kv_other, lse, mixed_grad,
        flops=20 * rows * rows * ONE * 2, exps=2 * rows * rows * 2,
    )


def inputs_backward(at, dq, dkv, dkv_got, up_grad, normed, g, turns, w):
    rows, dim = normed.shape
    units = up_grad.shape[1]

    def body(at, dq, dkv, dkv_got, up_grad, normed, g, *rest):
        turns, vectors, rest = rest[:3], rest[3], rest[4:]
        qkv_grad, table = rest[:2]
        pieces, (qkv, up, total, lines) = rest[2:6], rest[6:]
        gain_one, gain_two = vectors[0:1], vectors[2:3]
        step = 128

        def one(i, sums):
            span = pl.ds(pl.multiple_of(i * step, step), step)
            cosine, second, first_half = [table[span] for table in turns]
            parts = []
            for flat in (dq[span], dkv[0, span] + dkv_got[0, span]):
                parts.append(
                    flat * cosine
                    - pltpu.roll(flat, ROT // 2, 1) * second
                    - pltpu.roll(flat, ONE - ROT // 2, 1) * first_half
                )
            parts.append(dkv[1, span] + dkv_got[1, span])
            both = jnp.concatenate([p.astype(B16) for p in parts], axis=1)
            qkv_grad[span] = both
            attn = nt(both, qkv[...])
            mlp = nt(up_grad[span], up[...])
            total[span] = attn * gain_one + mlp * gain_two
            unit = normed[span].astype(F32)
            new = [
                jnp.sum(v, axis=0, keepdims=True)
                for v in (
                    attn * unit, attn, mlp * unit, mlp, g[span].astype(F32),
                    up_grad[span].astype(F32), both.astype(F32),
                )
            ]
            return tuple(a + b for a, b in zip(sums, new))

        widths = (dim,) * 5 + (units, 3 * ONE)
        sums = lax.fori_loop(
            0, rows // step, one, tuple(jnp.zeros((1, width), F32) for width in widths)
        )
        pieces_out(at, total, pieces)
        lines[...] = jnp.zeros_like(lines)
        line = 0
        for value in sums:
            for i in range(value.shape[1] // ONE):
                lines[line : line + 1] = value[:, i * ONE : (i + 1) * ONE]
                line += 1
        table[...] = lines[...].astype(B16)

    outs = [((rows, 3 * ONE), B16), ((LINES, ONE), B16)] + piece_shapes(rows, dim)
    return weights_call(
        "inputs_backward", body, outs, at,
        [dq, dkv, dkv_got, up_grad, normed, g, *turns, w["rows"]], [w["qkv"], w["up"]],
        scratch=[pltpu.VMEM((rows, dim), F32), pltpu.VMEM((LINES, ONE), F32)],
        flops=2 * rows * dim * (units + 3 * ONE) + 12 * rows * dim,
    )


LINES = 64


def join_forward(at, x_piece, parts, w):
    def body(at, x, vectors, own, *rest):
        total = x[...].astype(F32) + own[...].astype(F32) + vectors[4:5]
        for piece in rest[:-1]:
            total = total + piece[...].astype(F32)
        rest[-1][...] = total.astype(B16)

    return kernel_call_named("join_forward", body, [(x_piece.shape, B16)], at, x_piece, w["rows"], *parts)[0]


def join_backward(at, g_piece, x_piece, parts):
    dim = x_piece.shape[1]

    def body(at, g, x, own, *rest):
        total = own[...]
        for piece in rest[:-1]:
            total = total + piece[...].astype(F32)
        hidden = x[...].astype(F32)
        centre = hidden - jnp.sum(hidden, axis=1, keepdims=True) * (1.0 / dim)
        var = jnp.sum(centre * centre, axis=1, keepdims=True) * (1.0 / dim)
        scale = lax.rsqrt(var + 1e-05)
        normed = centre * scale
        inner = (
            total
            - jnp.sum(total, axis=1, keepdims=True) * (1.0 / dim)
            - normed * (jnp.sum(total * normed, axis=1, keepdims=True) * (1.0 / dim))
        )
        rest[-1][...] = (g[...].astype(F32) + scale * inner).astype(B16)

    return kernel_call_named("join_backward", body, [(x_piece.shape, B16)], at, g_piece, x_piece, *parts)[0]


def columns(at, ref, core, high):
    which = at[S_CORE] ^ core
    return jnp.concatenate(
        [
            ref[:, pl.ds(pl.multiple_of((4 * high + 2 * low + which) * ONE, ONE), ONE)]
            for low in range(2)
        ],
        axis=1,
    )


def early_grads(at, active, mixed, mlp_in, up_grad, g):
    rows, dim = g.shape
    units = active.shape[1]
    tiles = units // ONE

    def body(at, active, mixed, mlp_in, up_grad, g, keep, give):
        for core, target in ((0, keep), (1, give)):
            for high in range(2):
                strip = columns(at, g, core, high)
                down = tn(active[...], strip).astype(B16)
                out = tn(mixed[...], strip).astype(B16)
                up = tn(columns(at, mlp_in, core, high), up_grad[...]).astype(B16)
                for low in range(2):
                    lanes = slice(low * ONE, (low + 1) * ONE)
                    where = (at[S_HALF] ^ high, at[S_NEAR] ^ low)
                    target[where[0], where[1], :units] = down[:, lanes]
                    target[where[0], where[1], units : units + ONE] = out[:, lanes]
                    for i in range(tiles):
                        base = units + (1 + i) * ONE
                        target[where[0], where[1], base : base + ONE] = up[
                            lanes, i * ONE : (i + 1) * ONE
                        ]

    shape = (2, 2, 2 * units + ONE, ONE)
    return kernel_call_named(
        "early_grads",
        body, [(shape, B16)] * 2, at, active, mixed, mlp_in, up_grad, g,
        flops=2 * rows * dim * (2 * units + ONE),
    )


def late_grads(at, attn_in, qkv_grad, table, table_side):
    rows, dim = attn_in.shape

    def body(at, attn_in, qkv_grad, table, table_side, keep, give):
        lines = lax.broadcasted_iota(jnp.int32, table.shape, 0) < 4 * dim // ONE
        other = jnp.where(lines, table_side[...].astype(F32), 0.0)
        joined = (table[...].astype(F32) + other).astype(B16)
        for core, target in ((0, keep), (1, give)):
            for high in range(2):
                qkv = tn(columns(at, attn_in, core, high), qkv_grad[...]).astype(B16)
                for low in range(2):
                    where = (at[S_HALF] ^ high, at[S_NEAR] ^ low)
                    for i in range(3):
                        target[where[0], where[1], i * ONE : (i + 1) * ONE] = qkv[
                            low * ONE : (low + 1) * ONE, i * ONE : (i + 1) * ONE
                        ]
                    target[where[0], where[1], 3 * ONE :] = joined

    shape = (2, 2, 3 * ONE + LINES, ONE)
    return kernel_call_named(
        "late_grads",
        body, [(shape, B16)] * 2, at, attn_in, qkv_grad, table, table_side,
        flops=2 * rows * dim * 3 * ONE,
    )


def plus(a, b):
    return (a.astype(F32) + b.astype(F32)).astype(B16)


def summed_cores(keep, give):
    got = swapped(give, CORE)
    return (
        [plus(keep[0, i], got[0, i]) for i in range(2)],
        [plus(keep[1, i], got[1, i]) for i in range(2)],
    )


def unpack_grads(at, early, late, sizes):
    dim_part, units, heads = ONE, sizes["units"], ONE

    def body(at, *refs):
        early, late = refs[:4], refs[4:8]
        qkv, out, up, down, lines, b_qkv, b_up, branch = refs[8:]
        index = at[S_OWN]
        total = 0.0
        for j, (wide, narrow) in enumerate(zip(early, late)):
            source = index ^ (2 * (j % 2) + j // 2)
            place = pl.multiple_of(source * units, units)
            small = pl.multiple_of(source * ONE, ONE)
            down[pl.ds(place, units)] = wide[:units].astype(F32)
            out[pl.ds(small, ONE)] = wide[units : units + ONE].astype(F32)
            for i in range(units // ONE):
                base = units + (1 + i) * ONE
                up[:, pl.ds(place + i * ONE, ONE)] = wide[base : base + ONE].astype(F32)
            for i in range(3):
                qkv[i, :, pl.ds(small, ONE)] = narrow[i * ONE : (i + 1) * ONE].astype(F32)
            table = narrow[3 * ONE :].astype(F32)
            total = total + table[:32]
            for i in range(units // ONE):
                b_up[:, pl.ds(place + i * ONE, ONE)] = table[40 + i : 41 + i]
            for i in range(3):
                b_qkv[i : i + 1, pl.ds(small, ONE)] = table[40 + units // ONE + i :][:1]
            if j == 0:
                branch[...] = table[32:40]
        lines[...] = total

    outs = [
        ((3, dim_part, 4 * heads), F32),
        ((4 * heads, dim_part), F32),
        ((dim_part, 4 * units), F32),
        ((4 * units, dim_part), F32),
        ((32, ONE), F32),
        ((3, 4 * heads), F32),
        ((1, 4 * units), F32),
        ((8, ONE), F32),
    ]
    return kernel_call_named("unpack_grads", body, outs, at, *early, *late, keep=False)


def cube_device(
    inputs, cotangent, ln1_gain, ln1_bias, ln2_gain, ln2_bias, qkv_weight, qkv_bias,
    out_weight, up_weight, up_bias, down_weight, branch_bias,
):
    at = where_am_i()
    section, half, side = [lax.axis_index("section"), lax.axis_index("ctx") // 4, lax.axis_index("tp")]
    at, is_first, is_low, is_left, is_near = lax.optimization_barrier(
        (at, section == 0, half == 0, side == 0, section == half)
    )
    dim = inputs.shape[2]
    rows = 4 * inputs.shape[1]
    vectors = (ln1_gain, ln1_bias, ln2_gain, ln2_bias, branch_bias, up_bias, qkv_bias)

    mine, strip, sent_qkv = pack_first(at, inputs, vectors, qkv_weight)
    g_mine, g_strip, sent_up, sent_down = pack_second(
        at, cotangent, up_weight, out_weight, down_weight
    )
    x_parts = send_tokens(mine, strip)
    got_qkv, layers = first_weights(at, vectors, qkv_weight, sent_qkv)
    got_up = swapped(after(sent_up, got_qkv, x_parts[1]), SECTION)
    got_down = swapped(after(sent_down, got_up, *x_parts[4:]), SECTION)
    g_parts = send_tokens(after(g_mine, *x_parts[4:]), after(g_strip, *x_parts[4:]))
    first, second = layers
    turns = turn_tables(at, rows)

    def bring_rest(q):
        up = up_weights(at, up_weight, got_up, swapped(after(got_up, q), CORE))
        tall = row_weights(
            at, down_weight, out_weight, got_down,
            swapped(after(got_down, q, up[0], *g_parts[1:4]), CORE),
        )
        for i, layer in enumerate(layers):
            layer.update(up=up[i], down=tall[i], out=tall[2 + i], units=up[i].shape[1])

    def forward(loader, sources, w, with_piece):
        got = front(at, loader, sources, w, turns, with_piece)
        attn_in, mlp_in, normed, q, kv = got[:5]
        kv_other = swapped(kv, CORE)
        if "up" not in w:
            bring_rest(q)
        active, slope = units_forward(at, mlp_in, w)
        made = attention_forward(at, q, kv, kv_other, active, w)
        mixed, lse, pieces = made[0], made[1], made[2:]
        saved = dict(
            attn_in=attn_in, mlp_in=mlp_in, normed=normed, q=q, kv=kv, kv_other=kv_other,
            active=active, slope=slope, mixed=mixed, lse=lse,
        )
        return pieces, saved, got[5:]

    def backward(loader, sources, saved, w, with_piece, earlier=()):
        made = units_backward(at, loader, sources, saved["slope"], w, with_piece)
        g, up_grad, mixed_grad = made[:3]
        early = early_grads(at, saved["active"], saved["mixed"], saved["mlp_in"], up_grad, g)
        dq, dkv, dkv_other = attention_backward(
            at, saved["q"], saved["kv"], saved["kv_other"], saved["lse"],
            after(mixed_grad, early[0], *earlier),
        )
        dkv_got = swapped(dkv_other, CORE)
        return early, (dq, dkv, dkv_got, up_grad, saved["normed"], g), made[3:]

    def backward_end(given, saved, w):
        out = inputs_backward(at, *given, turns, w)
        qkv_grad, table, pieces = out[0], out[1], out[2:]
        late = late_grads(at, saved["attn_in"], qkv_grad, table, swapped(table, SIDE))
        return exchanged(pieces), late

    parts, saved_first, (x_piece,) = forward(start_loader, x_parts, first, True)
    keep, give = fold(at, exchanged(parts))
    piece = join_forward(at, x_piece, [keep, swapped(give, NEAR)], first)
    middle = gathered(piece, after(swapped(piece, NEAR), *g_parts[4:]))

    parts_last, saved_second, blocks = forward(piece_loader, middle, second, False)
    acts_mine, acts_give = blocks

    early, given, (g_piece,) = backward(start_loader, g_parts, saved_second, second, True)
    early_keep, early_give = summed_cores(*early)
    given = (after(given[0], *early_give),) + given[1:]
    parts, late = backward_end(given, saved_second, second)
    far_second = swapped(early_give[1], HALF)
    parts[0] = after(parts[0], far_second, *late)
    keep, give = fold(at, parts)
    late_keep, late_give = summed_cores(*late)
    late_got = swapped(after(jnp.stack(late_give), give), HALF)
    back = join_backward(at, g_piece, piece, [keep, swapped(give, NEAR)])
    near = after(swapped(back, NEAR), late_got)
    g_middle = gathered(back, near)
    close_second = swapped(after(early_give[0], near), HALF)
    g_middle[0] = after(g_middle[0], close_second)

    parts_last = exchanged([after(p, *g_middle) for p in parts_last])
    early, given, blocks = backward(piece_loader, g_middle, saved_first, first, False)
    in_mine, in_give = blocks
    early_second = [plus(a, b) for a, b in zip(early_keep, (close_second, far_second))]
    late_second = [plus(a, b) for a, b in zip(late_keep, late_got)]
    early_keep, early_give = summed_cores(*early)
    keep_last, give_last = fold(at, parts_last)
    given = (after(given[0], *early_give, give_last),) + given[1:]
    parts, late = backward_end(given, saved_first, first)
    far_first = swapped(early_give[1], HALF)
    parts[0] = after(parts[0], far_first, *late)
    keep, give = fold(at, parts)
    close_first = swapped(early_give[0], HALF)
    back_last = join_backward(at, back, x_piece, [keep, swapped(give, NEAR)])
    last = join_forward(at, piece, [keep_last, swapped(give_last, NEAR)], second)
    early_first = [plus(a, b) for a, b in zip(early_keep, (close_first, far_first))]
    late_keep, late_give = summed_cores(*late)
    late_got = swapped(jnp.stack(late_give), HALF)
    late_first = [plus(a, b) for a, b in zip(late_keep, late_got)]
    known_got = swapped(jnp.where(is_first, acts_give, in_give), HALF)
    known_rest = swapped(known_got, SIDE)

    def owned(one, two):
        return jnp.where(is_first, one, two), swapped(jnp.where(is_first, two, one), SECTION)

    far_own, far_got = owned(early_first[1], early_second[1])
    far = swapped(jnp.stack([far_own, far_got]), NEAR)
    close_own, close_got = owned(early_first[0], early_second[0])
    late_own, late_got = owned(jnp.stack(late_first), jnp.stack(late_second))
    late_near = swapped(jnp.stack([late_own[1], late_got[1]]), NEAR)
    sizes = dict(units=up_weight.shape[2] // 4)
    qkv, out, up, down, lines, b_qkv, b_up, branch = unpack_grads(
        at,
        (close_own, close_got, far[0], far[1]),
        (late_own[0], late_got[0], late_near[0], late_near[1]),
        sizes,
    )

    known_mine = jnp.where(is_first, acts_mine, in_mine)
    known_other = jnp.where(
        is_left,
        jnp.concatenate([known_got, known_rest], axis=0),
        jnp.concatenate([known_rest, known_got], axis=0),
    )
    known = jnp.where(
        is_low, jnp.stack([known_mine, known_other]), jnp.stack([known_other, known_mine])
    )
    mine = jnp.where(is_first, back_last, last)
    got = swapped(jnp.where(is_first, last, back_last), SECTION)
    stay = jnp.where(is_near, mine, got)
    other = swapped(jnp.where(is_near, got, mine), HALF)
    own = jnp.where(is_low, jnp.stack([stay, other]), jnp.stack([other, stay]))
    rest = swapped(own, SIDE)
    new = jnp.where(
        is_left, jnp.concatenate([own, rest], axis=1), jnp.concatenate([rest, own], axis=1)
    )
    acts = jnp.where(is_first, known, new)
    in_grads = jnp.where(is_first, new, known)

    lines = lines.reshape(4, dim)
    return (
        acts[None],
        in_grads[None],
        lines[0:1],
        lines[1:2],
        lines[2:3],
        lines[3:4],
        qkv[None],
        b_qkv[None],
        out[None],
        up[None],
        b_up,
        down[None],
        branch.reshape(1, dim),
    )


def placed_program(mesh, device_program):
    placed = (
        P(None, "ctx", None),
        P(None, "ctx", None),
        P("section", None),
        P("section", None),
        P("section", None),
        P("section", None),
        P("section", None, None, "tp"),
        P("section", None, "tp"),
        P("section", "tp", None),
        P("section", None, "tp"),
        P("section", "tp"),
        P("section", "tp", None),
        P("section", None),
    )
    return jax.shard_map(
        device_program,
        mesh=mesh,
        in_specs=placed,
        out_specs=(
            P("section", None, "ctx", None),
            P("section", None, "ctx", None),
            P("section", None),
            P("section", None),
            P("section", None),
            P("section", None),
            P("section", None, "ctx", "tp"),
            P("section", None, "tp"),
            P("section", "tp", "ctx"),
            P("section", "ctx", "tp"),
            P("section", "tp"),
            P("section", "tp", "ctx"),
            P("section", None),
        ),
        check_vma=False,
    )


def solution(mesh):
    sizes = dict(mesh.shape)
    if sizes["section"] == 2 and sizes["tp"] == 2 and sizes["ctx"] == 8:
        return placed_program(mesh, cube_device)
    return placed_program(mesh, per_device)
```

profile of v0, /device:TPU:0, one launch (start us, length us, event | category | flops | bytes accessed | tf_op | source)
XLA Modules:
  0.0 273.8 jit_solution(5324660007166378739)
XLA Ops:
  2.6 3.0 %collective-permute-start.5 = (bf16[1584,128]{1,0:T(8,128)(2,1)S(1)}, bf16[1584,128]{1,0:T(8,128)(2,1)S(1)}, u32[]{:S(2)}, u32[]{:S(2)}) collective-permute-start(bf16[1584,128]{1,0:T(8,128)(2,1)S(1)} %get-tuple-element.141), channel_id=1, source_target_pairs={{0,16},{1,17},{2,18},{3,19},{4,20},{5,21},{6,22},{7,23},{8,24},{9,... | collective-permute-start | bytes 1216520 | tf_op jit(solution)/shard_map/ppermute | solution.py:323
  7.2 2.5 collective-permute-start.2
  11.9 6.0 %collective-permute-done.refs_1_ = bf16[128,1024]{1,0:T(8,128)(2,1)S(1)} collective-permute-done((bf16[128,1024]{1,0:T(8,128)(2,1)S(1)}, bf16[128,1024]{1,0:T(8,128)(2,1)S(1)}, u32[]{:S(2)}, u32[]{:S(2)}) %collective-permute-start) | collective-permute-done | bytes 262176 | tf_op jit(solution)/shard_map/ppermute | solution.py:323
  26.2 2.9 %collective-permute-done.8.refs_1_ = bf16[512,512]{1,0:T(8,128)(2,1)S(1)} collective-permute-done((bf16[512,512]{1,0:T(8,128)(2,1)S(1)}, bf16[512,512]{1,0:T(8,128)(2,1)S(1)}, u32[]{:S(2)}, u32[]{:S(2)}) %collective-permute-start.8) | collective-permute-done | bytes 524320 | tf_op jit(solution)/shard_map/ppermute | solution.py:323
  35.4 3.1 %front.2 = (bf16[512,1024]{1,0:T(8,128)(2,1)S(1)}, bf16[512,1024]{1,0:T(8,128)(2,1)S(1)}, bf16[512,1024]{1,0:T(8,128)(2,1)S(1)}, bf16[512,128]{1,0:T(8,128)(2,1)...) custom-call(s32[8]{0:T(128)S(1)} %stack.113.at, bf16[128,1024]{1,0:T(8,128)(2,1)S(1)} %get-tuple-element.139.refs_0_, ...), custom_call_target="tpu_custom_call" | custom-call | tf_op jit(solution)/shard_map/front/pallas_call | solution.py:347
  39.5 2.8 %collective-permute-start.13 = (bf16[128,512]{1,0:T(8,128)(2,1)S(1)}, bf16[128,512]{1,0:T(8,128)(2,1)S(1)}, u32[]{:S(2)}, u32[]{:S(2)}) collective-permute-start(bf16[128,512]{1,0:T(8,128)(2,1)S(1)} %get-tuple-element.158), channel_id=1, source_target_pairs={{0,12},{1,13},{2,14},{3,15},{4,8},{5,9},{6,10},{7,11},{8,4},{9,5},... | collective-permute-start | bytes 393224 | tf_op jit(solution)/shard_map/ppermute | solution.py:323
  43.6 2.1 choose_up.1
  45.8 6.5 %collective-permute-done.13.refs_3_ = bf16[128,512]{1,0:T(8,128)(2,1)S(1)} collective-permute-done((bf16[128,512]{1,0:T(8,128)(2,1)S(1)}, bf16[128,512]{1,0:T(8,128)(2,1)S(1)}, u32[]{:S(2)}, u32[]{:S(2)}) %collective-permute-start.13) | collective-permute-done | bytes 131104 | tf_op jit(solution)/shard_map/ppermute | solution.py:323
  52.3 2.8 %collective-permute-done.12.refs_2_ = bf16[128,512]{1,0:T(8,128)(2,1)S(1)} collective-permute-done((bf16[128,512]{1,0:T(8,128)(2,1)S(1)}, bf16[128,512]{1,0:T(8,128)(2,1)S(1)}, u32[]{:S(2)}, u32[]{:S(2)}) %collective-permute-start.12) | collective-permute-done | bytes 131104 | tf_op jit(solution)/shard_map/ppermute | solution.py:323
  55.7 2.2 units_forward.2
  58.7 2.3 choose_rows.1
  61.0 3.7 %attention_forward.2 = (bf16[512,128]{1,0:T(8,128)(2,1)S(1)}, f32[512,128]{1,0:T(8,128)S(1)}, f32[2,64,1024]{2,1,0:T(8,128)S(1)}, bf16[2,64,1024]{2,1,0:T(8,128)...) custom-call(s32[8]{0:T(128)S(1)} %stack.113.at, ...), custom_call_target="tpu_custom_call" | custom-call | tf_op jit(solution)/shard_map/attention_forward/pallas_call | solution.py:347
  68.3 4.8 %collective-permute-done.15.refs_1_ = bf16[2,64,1024]{2,1,0:T(8,128)(2,1)S(1)} collective-permute-done((bf16[2,64,1024]{2,1,0:T(8,128)(2,1)S(1)}, bf16[2,64,1024]{2,1,0:T(8,128)(2,1)S(1)}, u32[]{:S(2)}, u32[]{:S(2)}) %collective-permute-start.15) | collective-permute-done | bytes 262176 | tf_op jit(solution)/shard_map/ppermute | solution.py:323
  73.1 2.4 collective-permute-done.16.refs_2_
  75.6 4.4 %collective-permute-done.17.refs_3_ = bf16[2,64,1024]{2,1,0:T(8,128)(2,1)S(1)} collective-permute-done((bf16[2,64,1024]{2,1,0:T(8,128)(2,1)S(1)}, bf16[2,64,1024]{2,1,0:T(8,128)(2,1)S(1)}, u32[]{:S(2)}, u32[]{:S(2)}) %collective-permute-start.17) | collective-permute-done | bytes 262176 | tf_op jit(solution)/shard_map/ppermute | solution.py:323
  83.0 2.6 collective-permute-done.18.rest_0_
  87.9 3.4 %collective-permute-done.19 = bf16[64,1024]{1,0:T(8,128)(2,1)S(1)} collective-permute-done((bf16[64,1024]{1,0:T(8,128)(2,1)S(1)}, bf16[64,1024]{1,0:T(8,128)(2,1)S(1)}, u32[]{:S(2)}, u32[]{:S(2)}) %collective-permute-start.19) | collective-permute-done | bytes 131104 | tf_op jit(solution)/shard_map/ppermute | solution.py:323
  91.3 2.6 collective-permute-start.24
  94.9 5.3 %collective-permute-done.24.refs_3_ = bf16[2,64,1024]{2,1,0:T(8,128)(2,1)S(1)} collective-permute-done((bf16[2,64,1024]{2,1,0:T(8,128)(2,1)S(1)}, bf16[2,64,1024]{2,1,0:T(8,128)(2,1)S(1)}, u32[]{:S(2)}, u32[]{:S(2)}) %collective-permute-start.24) | collective-permute-done | bytes 262176 | tf_op jit(solution)/shard_map/ppermute | solution.py:323
  100.1 2.8 %collective-permute-done.23.refs_2_ = bf16[2,64,1024]{2,1,0:T(8,128)(2,1)S(1)} collective-permute-done((bf16[2,64,1024]{2,1,0:T(8,128)(2,1)S(1)}, bf16[2,64,1024]{2,1,0:T(8,128)(2,1)S(1)}, u32[]{:S(2)}, u32[]{:S(2)}) %collective-permute-start.23) | collective-permute-done | bytes 262176 | tf_op jit(solution)/shard_map/ppermute | solution.py:323
  103.0 3.1 %front.3 = (bf16[512,1024]{1,0:T(8,128)(2,1)S(1)}, bf16[512,1024]{1,0:T(8,128)(2,1)S(1)}, bf16[512,1024]{1,0:T(8,128)(2,1)S(1)}, bf16[512,128]{1,0:T(8,128)(2,1)...) custom-call(s32[8]{0:T(128)S(1)} %stack.113.at, ...), custom_call_target="tpu_custom_call" | custom-call | tf_op jit(solution)/shard_map/front/pallas_call | solution.py:347
  106.1 2.2 units_forward.3
  110.3 3.7 %attention_forward.3 = (bf16[512,128]{1,0:T(8,128)(2,1)S(1)}, f32[512,128]{1,0:T(8,128)S(1)}, f32[2,64,1024]{2,1,0:T(8,128)S(1)}, bf16[2,64,1024]{2,1,0:T(8,128)...) custom-call(s32[8]{0:T(128)S(1)} %stack.113.at, ...), custom_call_target="tpu_custom_call" | custom-call | tf_op jit(solution)/shard_map/attention_forward/pallas_call | solution.py:347
  114.1 2.2 early_grads.2
  116.8 4.0 %attention_backward.2 = (f32[512,128]{1,0:T(8,128)S(1)}, f32[2,512,128]{2,1,0:T(8,128)S(1)}, f32[2,512,128]{2,1,0:T(8,128)S(1)}) custom-call(s32[8]{0:T(128)S(1)} %stack.113.at, bf16[512,128]{1,0:T(8,128)(2,1)S(1)} %get-tuple-element.178.refs_0_.q, bf16[2,512,128]{2,1,0:T(8,128)(2,1)S(1)} %get-tuple-element.179.refs_1_.kv, ...), custom_call_target="tpu_custom_call" | custom-call | tf_op jit(solution)/shard_map/attention_backward/pallas_call | solution.py:347
  122.8 4.0 %inputs_backward.2 = (bf16[512,384]{1,0:T(8,128)(2,1)S(1)}, bf16[64,128]{1,0:T(8,128)(2,1)S(1)}, f32[2,64,1024]{2,1,0:T(8,128)S(1)}, bf16[2,64,1024]{2,1,0:T(8,1...) custom-call(s32[8]{0:T(128)S(1)} %stack.113.at, ...), custom_call_target="tpu_custom_call" | custom-call | tf_op jit(solution)/shard_map/inputs_backward/pallas_call | solution.py:347
  128.2 2.4 collective-permute-done.29.table_side
  137.1 11.4 %collective-permute-done.28 = bf16[1152,128]{1,0:T(8,128)(2,1)S(1)} collective-permute-done((bf16[1152,128]{1,0:T(8,128)(2,1)S(1)}, bf16[1152,128]{1,0:T(8,128)(2,1)S(1)}, u32[]{:S(2)}, u32[]{:S(2)}) %collective-permute-start.28) | collective-permute-done | bytes 294944 | tf_op jit(solution)/shard_map/ppermute | solution.py:323
  152.6 4.2 %collective-permute-done.33.rest_0_ = bf16[64,1024]{1,0:T(8,128)(2,1)S(1)} collective-permute-done((bf16[64,1024]{1,0:T(8,128)(2,1)S(1)}, bf16[64,1024]{1,0:T(8,128)(2,1)S(1)}, u32[]{:S(2)}, u32[]{:S(2)}) %collective-permute-start.33) | collective-permute-done | bytes 131104 | tf_op jit(solution)/shard_map/ppermute | solution.py:323
  158.1 6.7 %collective-permute-done.34 = bf16[64,1024]{1,0:T(8,128)(2,1)S(1)} collective-permute-done((bf16[64,1024]{1,0:T(8,128)(2,1)S(1)}, bf16[64,1024]{1,0:T(8,128)(2,1)S(1)}, u32[]{:S(2)}, u32[]{:S(2)}) %collective-permute-start.34) | collective-permute-done | bytes 131104 | tf_op jit(solution)/shard_map/ppermute | solution.py:323
  165.4 2.5 collective-permute-start.40
  168.9 9.0 %collective-permute-done.37 = bf16[1152,128]{1,0:T(8,128)(2,1)S(1)} collective-permute-done((bf16[1152,128]{1,0:T(8,128)(2,1)S(1)}, bf16[1152,128]{1,0:T(8,128)(2,1)S(1)}, u32[]{:S(2)}, u32[]{:S(2)}) %collective-permute-start.37) | collective-permute-done | bytes 294944 | tf_op jit(solution)/shard_map/ppermute | solution.py:323
  178.7 2.1 units_backward.3
  180.8 2.1 early_grads.3
  187.2 4.0 %attention_backward.3 = (f32[512,128]{1,0:T(8,128)S(1)}, f32[2,512,128]{2,1,0:T(8,128)S(1)}, f32[2,512,128]{2,1,0:T(8,128)S(1)}) custom-call(s32[8]{0:T(128)S(1)} %stack.113.at, bf16[512,128]{1,0:T(8,128)(2,1)S(1)} %get-tuple-element.145.refs_0_.q, bf16[2,512,128]{2,1,0:T(8,128)(2,1)S(1)} %get-tuple-element.146.refs_1_.kv, ...), custom_call_target="tpu_custom_call" | custom-call | tf_op jit(solution)/shard_map/attention_backward/pallas_call | solution.py:347
  194.4 4.7 %collective-permute-done.46.refs_3_ = bf16[2,64,1024]{2,1,0:T(8,128)(2,1)S(1)} collective-permute-done((bf16[2,64,1024]{2,1,0:T(8,128)(2,1)S(1)}, bf16[2,64,1024]{2,1,0:T(8,128)(2,1)S(1)}, u32[]{:S(2)}, u32[]{:S(2)}) %collective-permute-start.46) | collective-permute-done | bytes 262176 | tf_op jit(solution)/shard_map/ppermute | solution.py:323
  199.7 2.6 collective-permute-start.54
  202.4 2.6 collective-permute-start.48
  205.0 4.0 %inputs_backward.3 = (bf16[512,384]{1,0:T(8,128)(2,1)S(1)}, bf16[64,128]{1,0:T(8,128)(2,1)S(1)}, f32[2,64,1024]{2,1,0:T(8,128)S(1)}, bf16[2,64,1024]{2,1,0:T(8,1...) custom-call(s32[8]{0:T(128)S(1)} %stack.113.at, ...), custom_call_target="tpu_custom_call" | custom-call | tf_op jit(solution)/shard_map/inputs_backward/pallas_call | solution.py:347
  214.7 3.4 %collective-permute-done.49.table_side = bf16[64,128]{1,0:T(8,128)(2,1)S(1)} collective-permute-done((bf16[64,128]{1,0:T(8,128)(2,1)S(1)}, bf16[64,128]{1,0:T(8,128)(2,1)S(1)}, u32[]{:S(2)}, u32[]{:S(2)}) %collective-permute-start.49) | collective-permute-done | bytes 16416 | tf_op jit(solution)/shard_map/ppermute | solution.py:323
  223.2 2.1 collective-permute-start.53
  227.1 2.9 %collective-permute-done.58 = bf16[1152,128]{1,0:T(8,128)(2,1)S(1)} collective-permute-done((bf16[1152,128]{1,0:T(8,128)(2,1)S(1)}, bf16[1152,128]{1,0:T(8,128)(2,1)S(1)}, u32[]{:S(2)}, u32[]{:S(2)}) %collective-permute-start.58) | collective-permute-done | bytes 294944 | tf_op jit(solution)/shard_map/ppermute | solution.py:323
  235.8 8.1 %collective-permute-done.55 = bf16[64,1024]{1,0:T(8,128)(2,1)S(1)} collective-permute-done((bf16[64,1024]{1,0:T(8,128)(2,1)S(1)}, bf16[64,1024]{1,0:T(8,128)(2,1)S(1)}, u32[]{:S(2)}, u32[]{:S(2)}) %collective-permute-start.55) | collective-permute-done | bytes 131104 | tf_op jit(solution)/shard_map/ppermute | solution.py:323
  243.9 3.6 %collective-permute-start.56 = (bf16[64,1024]{1,0:T(8,128)(2,1)S(1)}, bf16[64,1024]{1,0:T(8,128)(2,1)S(1)}, u32[]{:S(2)}, u32[]{:S(2)}) collective-permute-start(bf16[64,1024]{1,0:T(8,128)(2,1)S(1)} %get-tuple-element.295), channel_id=1, source_target_pairs={{0,8},{1,9},{2,10},{3,11},{4,12},{5,13},{6,14},{7,15},{8,0},{9,1},... | collective-permute-start | bytes 393224 | tf_op jit(solution)/shard_map/ppermute | solution.py:323
  247.9 6.0 %collective-permute-done.56 = bf16[64,1024]{1,0:T(8,128)(2,1)S(1)} collective-permute-done((bf16[64,1024]{1,0:T(8,128)(2,1)S(1)}, bf16[64,1024]{1,0:T(8,128)(2,1)S(1)}, u32[]{:S(2)}, u32[]{:S(2)}) %collective-permute-start.56) | collective-permute-done | bytes 131104 | tf_op jit(solution)/shard_map/ppermute | solution.py:323
  256.8 5.6 %collective-permute-done.64 = bf16[2,448,128]{2,1,0:T(8,128)(2,1)S(1)} collective-permute-done((bf16[2,448,128]{2,1,0:T(8,128)(2,1)S(1)}, bf16[2,448,128]{2,1,0:T(8,128)(2,1)S(1)}, u32[]{:S(2)}, u32[]{:S(2)}) %collective-permute-start.64) | collective-permute-done | bytes 229408 | tf_op jit(solution)/shard_map/ppermute | solution.py:323
  263.8 6.2 %collective-permute-done.65 = bf16[2,448,128]{2,1,0:T(8,128)(2,1)S(1)} collective-permute-done((bf16[2,448,128]{2,1,0:T(8,128)(2,1)S(1)}, bf16[2,448,128]{2,1,0:T(8,128)(2,1)S(1)}, u32[]{:S(2)}, u32[]{:S(2)}) %collective-permute-start.65) | collective-permute-done | bytes 229408 | tf_op jit(solution)/shard_map/ppermute | solution.py:323
  270.1 2.5 unpack_grads.1
  (178 shorter events, 86.7 us)
Async XLA Ops:
  2.6 15.3 %collective-permute-start.5 = (bf16[1584,128]{1,0:T(8,128)(2,1)S(1)}, bf16[1584,128]{1,0:T(8,128)(2,1)S(1)}, u32[]{:S(2)}, u32[]{:S(2)}) collective-permute-start(bf16[1584,128]{1,0:T(8,128)(2,1)S(1)} %get-tuple-element.141), channel_id=1, source_target_pairs={{0,16},{1,17},{2,18},{3,19},{4,20},{5,21},{6,22},{7,23},{8,24},{9,... | collective-permute-start | bytes 1216520 | tf_op jit(solution)/shard_map/ppermute | solution.py:323
  5.6 12.3 %collective-permute-start = (bf16[128,1024]{1,0:T(8,128)(2,1)S(1)}, bf16[128,1024]{1,0:T(8,128)(2,1)S(1)}, u32[]{:S(2)}, u32[]{:S(2)}) collective-permute-start(bf16[128,1024]{1,0:T(8,128)(2,1)S(1)} %get-tuple-element.139.refs_0_), channel_id=1, source_target_pairs={{0,4},{1,5},{2,6},{3,7},{4,0},{5,1},{6,2},{7,3},{8,12},{9,13},{10,... | collective-permute-start | bytes 786440 | tf_op jit(solution)/shard_map/ppermute | solution.py:323
  7.2 12.5 %collective-permute-start.2 = (bf16[128,512]{1,0:T(8,128)(2,1)S(1)}, bf16[128,512]{1,0:T(8,128)(2,1)S(1)}, u32[]{:S(2)}, u32[]{:S(2)}) collective-permute-start(bf16[128,512]{1,0:T(8,128)(2,1)S(1)} %get-tuple-element.140), channel_id=1, source_target_pairs={{0,12},{1,13},{2,14},{3,15},{4,8},{5,9},{6,10},{7,11},{8,4},{9,5},... | collective-permute-start | bytes 393224 | tf_op jit(solution)/shard_map/ppermute | solution.py:323
  9.8 11.5 %collective-permute-start.1 = (bf16[128,512]{1,0:T(8,128)(2,1)S(1)}, bf16[128,512]{1,0:T(8,128)(2,1)S(1)}, u32[]{:S(2)}, u32[]{:S(2)}) collective-permute-start(bf16[128,512]{1,0:T(8,128)(2,1)S(1)} %get-tuple-element.140), channel_id=1, source_target_pairs={{0,8},{1,9},{2,10},{3,11},{4,12},{5,13},{6,14},{7,15},{8,0},{9,1},... | collective-permute-start | bytes 393224 | tf_op jit(solution)/shard_map/ppermute | solution.py:323
  17.9 11.2 %collective-permute-start.8 = (bf16[512,512]{1,0:T(8,128)(2,1)S(1)}, bf16[512,512]{1,0:T(8,128)(2,1)S(1)}, u32[]{:S(2)}, u32[]{:S(2)}) collective-permute-start(bf16[512,512]{1,0:T(8,128)(2,1)S(1)} %get-tuple-element.149), channel_id=1, source_target_pairs={{0,16},{1,17},{2,18},{3,19},{4,20},{5,21},{6,22},{7,23},{8,24},{9,... | collective-permute-start | bytes 1572872 | tf_op jit(solution)/shard_map/ppermute | solution.py:323
  22.8 9.9 %collective-permute-start.6 = (bf16[1584,128]{1,0:T(8,128)(2,1)S(1)}, bf16[1584,128]{1,0:T(8,128)(2,1)S(1)}, u32[]{:S(2)}, u32[]{:S(2)}) collective-permute-start(bf16[1584,128]{1,0:T(8,128)(2,1)S(1)} %collective-permute-done.5.refs_7_.refs_1_), channel_id=1, source_target_pairs={{0,2},{1,3},{2,0},{3,1},{4,6},{5,7},{6,4},{7,5},{8,10},{9,11},{10,... | collective-permute-start | bytes 1216520 | tf_op jit(solution)/shard_map/ppermute | solution.py:323
  29.1 26.0 %collective-permute-start.10 = (bf16[320,1024]{1,0:T(8,128)(2,1)S(1)}, bf16[320,1024]{1,0:T(8,128)(2,1)S(1)}, u32[]{:S(2)}, u32[]{:S(2)}) collective-permute-start(bf16[320,1024]{1,0:T(8,128)(2,1)S(1)} %get-tuple-element.154), channel_id=1, source_target_pairs={{0,16},{1,17},{2,18},{3,19},{4,20},{5,21},{6,22},{7,23},{8,24},{9,... | collective-permute-start | bytes 1966088 | tf_op jit(solution)/shard_map/ppermute | solution.py:323
  38.6 16.5 %collective-permute-start.11 = (bf16[128,1024]{1,0:T(8,128)(2,1)S(1)}, bf16[128,1024]{1,0:T(8,128)(2,1)S(1)}, u32[]{:S(2)}, u32[]{:S(2)}) collective-permute-start(bf16[128,1024]{1,0:T(8,128)(2,1)S(1)} %get-tuple-element.156.refs_0_), channel_id=1, source_target_pairs={{0,4},{1,5},{2,6},{3,7},{4,0},{5,1},{6,2},{7,3},{8,12},{9,13},{10,... | collective-permute-start | bytes 786440 | tf_op jit(solution)/shard_map/ppermute | solution.py:323
  39.5 12.8 %collective-permute-start.13 = (bf16[128,512]{1,0:T(8,128)(2,1)S(1)}, bf16[128,512]{1,0:T(8,128)(2,1)S(1)}, u32[]{:S(2)}, u32[]{:S(2)}) collective-permute-start(bf16[128,512]{1,0:T(8,128)(2,1)S(1)} %get-tuple-element.158), channel_id=1, source_target_pairs={{0,12},{1,13},{2,14},{3,15},{4,8},{5,9},{6,10},{7,11},{8,4},{9,5},... | collective-permute-start | bytes 393224 | tf_op jit(solution)/shard_map/ppermute | solution.py:323
  42.3 12.8 %collective-permute-start.12 = (bf16[128,512]{1,0:T(8,128)(2,1)S(1)}, bf16[128,512]{1,0:T(8,128)(2,1)S(1)}, u32[]{:S(2)}, u32[]{:S(2)}) collective-permute-start(bf16[128,512]{1,0:T(8,128)(2,1)S(1)} %get-tuple-element.158), channel_id=1, source_target_pairs={{0,8},{1,9},{2,10},{3,11},{4,12},{5,13},{6,14},{7,15},{8,0},{9,1},... | collective-permute-start | bytes 393224 | tf_op jit(solution)/shard_map/ppermute | solution.py:323
  64.8 8.4 %collective-permute-start.15 = (bf16[2,64,1024]{2,1,0:T(8,128)(2,1)S(1)}, bf16[2,64,1024]{2,1,0:T(8,128)(2,1)S(1)}, u32[]{:S(2)}, u32[]{:S(2)}) collective-permute-start(bf16[2,64,1024]{2,1,0:T(8,128)(2,1)S(1)} %get-tuple-element.163), channel_id=1, source_target_pairs={{0,1},{1,0},{2,3},{3,2},{4,5},{5,4},{6,7},{7,6},{8,9},{9,8},{10,11... | collective-permute-start | bytes 786440 | tf_op jit(solution)/shard_map/ppermute | solution.py:323
  66.4 9.2 %collective-permute-start.16 = (bf16[2,64,1024]{2,1,0:T(8,128)(2,1)S(1)}, bf16[2,64,1024]{2,1,0:T(8,128)(2,1)S(1)}, u32[]{:S(2)}, u32[]{:S(2)}) collective-permute-start(bf16[2,64,1024]{2,1,0:T(8,128)(2,1)S(1)} %get-tuple-element.164), channel_id=1, source_target_pairs={{0,16},{1,17},{2,18},{3,19},{4,20},{5,21},{6,22},{7,23},{8,24},{9,... | collective-permute-start | bytes 786440 | tf_op jit(solution)/shard_map/ppermute | solution.py:323
  67.9 12.0 %collective-permute-start.17 = (bf16[2,64,1024]{2,1,0:T(8,128)(2,1)S(1)}, bf16[2,64,1024]{2,1,0:T(8,128)(2,1)S(1)}, u32[]{:S(2)}, u32[]{:S(2)}) collective-permute-start(bf16[2,64,1024]{2,1,0:T(8,128)(2,1)S(1)} %get-tuple-element.165), channel_id=1, source_target_pairs={{0,17},{1,16},{2,19},{3,18},{4,21},{5,20},{6,23},{7,22},{8,25},{9,... | collective-permute-start | bytes 786440 | tf_op jit(solution)/shard_map/ppermute | solution.py:323
  91.3 8.8 %collective-permute-start.24 = (bf16[2,64,1024]{2,1,0:T(8,128)(2,1)S(1)}, bf16[2,64,1024]{2,1,0:T(8,128)(2,1)S(1)}, u32[]{:S(2)}, u32[]{:S(2)}) collective-permute-start(bf16[2,64,1024]{2,1,0:T(8,128)(2,1)S(1)} %pad_maximum_fusion.1.refs_0_), channel_id=1, source_target_pairs={{0,17},{1,16},{2,19},{3,18},{4,21},{5,20},{6,23},{7,22},{8,25},{9,... | collective-permute-start | bytes 786440 | tf_op jit(solution)/shard_map/ppermute | solution.py:323
  93.9 9.1 %collective-permute-start.23 = (bf16[2,64,1024]{2,1,0:T(8,128)(2,1)S(1)}, bf16[2,64,1024]{2,1,0:T(8,128)(2,1)S(1)}, u32[]{:S(2)}, u32[]{:S(2)}) collective-permute-start(bf16[2,64,1024]{2,1,0:T(8,128)(2,1)S(1)} %pad_maximum_fusion.1.refs_0_), channel_id=1, source_target_pairs={{0,16},{1,17},{2,18},{3,19},{4,20},{5,21},{6,22},{7,23},{8,24},{9,... | collective-permute-start | bytes 786440 | tf_op jit(solution)/shard_map/ppermute | solution.py:323
  94.3 8.6 %collective-permute-start.22 = (bf16[2,64,1024]{2,1,0:T(8,128)(2,1)S(1)}, bf16[2,64,1024]{2,1,0:T(8,128)(2,1)S(1)}, u32[]{:S(2)}, u32[]{:S(2)}) collective-permute-start(bf16[2,64,1024]{2,1,0:T(8,128)(2,1)S(1)} %pad_maximum_fusion.1.refs_0_), channel_id=1, source_target_pairs={{0,1},{1,0},{2,3},{3,2},{4,5},{5,4},{6,7},{7,6},{8,9},{9,8},{10,11... | collective-permute-start | bytes 786440 | tf_op jit(solution)/shard_map/ppermute | solution.py:323
  131.9 19.2 %collective-permute-start.35 = (bf16[2,2,448,128]{3,2,1,0:T(8,128)(2,1)S(1)}, bf16[2,2,448,128]{3,2,1,0:T(8,128)(2,1)S(1)}, u32[]{:S(2)}, u32[]{:S(2)}) collective-permute-start(bf16[2,2,448,128]{3,2,1,0:T(8,128)(2,1)S(1)} %get-tuple-element.199), channel_id=1, source_target_pairs={{0,2},{1,3},{2,0},{3,1},{4,6},{5,7},{6,4},{7,5},{8,10},{9,11},{10,... | collective-permute-start | bytes 1376264 | tf_op jit(solution)/shard_map/ppermute | solution.py:323
  132.0 16.6 %collective-permute-start.28 = (bf16[1152,128]{1,0:T(8,128)(2,1)S(1)}, bf16[1152,128]{1,0:T(8,128)(2,1)S(1)}, u32[]{:S(2)}, u32[]{:S(2)}) collective-permute-start(bf16[1152,128]{1,0:T(8,128)(2,1)S(1)} %get-tuple-element.278), channel_id=1, source_target_pairs={{0,8},{1,9},{2,10},{3,11},{4,12},{5,13},{6,14},{7,15},{8,0},{9,1},... | collective-permute-start | bytes 884744 | tf_op jit(solution)/shard_map/ppermute | solution.py:323
  133.6 14.9 %collective-permute-start.30 = (bf16[2,64,1024]{2,1,0:T(8,128)(2,1)S(1)}, bf16[2,64,1024]{2,1,0:T(8,128)(2,1)S(1)}, u32[]{:S(2)}, u32[]{:S(2)}) collective-permute-start(bf16[2,64,1024]{2,1,0:T(8,128)(2,1)S(1)} %get-tuple-element.201), channel_id=1, source_target_pairs={{0,1},{1,0},{2,3},{3,2},{4,5},{5,4},{6,7},{7,6},{8,9},{9,8},{10,11... | collective-permute-start | bytes 786440 | tf_op jit(solution)/shard_map/ppermute | solution.py:323
  135.0 13.5 %collective-permute-start.31 = (bf16[2,64,1024]{2,1,0:T(8,128)(2,1)S(1)}, bf16[2,64,1024]{2,1,0:T(8,128)(2,1)S(1)}, u32[]{:S(2)}, u32[]{:S(2)}) collective-permute-start(bf16[2,64,1024]{2,1,0:T(8,128)(2,1)S(1)} %get-tuple-element.202), channel_id=1, source_target_pairs={{0,16},{1,17},{2,18},{3,19},{4,20},{5,21},{6,22},{7,23},{8,24},{9,... | collective-permute-start | bytes 786440 | tf_op jit(solution)/shard_map/ppermute | solution.py:323
  136.5 12.2 %collective-permute-start.32 = (bf16[2,64,1024]{2,1,0:T(8,128)(2,1)S(1)}, bf16[2,64,1024]{2,1,0:T(8,128)(2,1)S(1)}, u32[]{:S(2)}, u32[]{:S(2)}) collective-permute-start(bf16[2,64,1024]{2,1,0:T(8,128)(2,1)S(1)} %get-tuple-element.203), channel_id=1, source_target_pairs={{0,17},{1,16},{2,19},{3,18},{4,21},{5,20},{6,23},{7,22},{8,25},{9,... | collective-permute-start | bytes 786440 | tf_op jit(solution)/shard_map/ppermute | solution.py:323
  151.2 13.6 %collective-permute-start.36 = (bf16[2,448,128]{2,1,0:T(8,128)(2,1)S(1)}, bf16[2,448,128]{2,1,0:T(8,128)(2,1)S(1)}, u32[]{:S(2)}, u32[]{:S(2)}) collective-permute-start(bf16[2,448,128]{2,1,0:T(8,128)(2,1)S(1)} %pad_maximum_fusion.3), channel_id=1, source_target_pairs={{0,8},{1,9},{2,10},{3,11},{4,12},{5,13},{6,14},{7,15},{8,0},{9,1},... | collective-permute-start | bytes 688136 | tf_op jit(solution)/shard_map/ppermute | solution.py:323
  164.7 13.2 %collective-permute-start.37 = (bf16[1152,128]{1,0:T(8,128)(2,1)S(1)}, bf16[1152,128]{1,0:T(8,128)(2,1)S(1)}, u32[]{:S(2)}, u32[]{:S(2)}) collective-permute-start(bf16[1152,128]{1,0:T(8,128)(2,1)S(1)} %get-tuple-element.208), channel_id=1, source_target_pairs={{0,8},{1,9},{2,10},{3,11},{4,12},{5,13},{6,14},{7,15},{8,0},{9,1},... | collective-permute-start | bytes 884744 | tf_op jit(solution)/shard_map/ppermute | solution.py:323
  165.4 12.5 %collective-permute-start.40 = (bf16[2,64,1024]{2,1,0:T(8,128)(2,1)S(1)}, bf16[2,64,1024]{2,1,0:T(8,128)(2,1)S(1)}, u32[]{:S(2)}, u32[]{:S(2)}) collective-permute-start(bf16[2,64,1024]{2,1,0:T(8,128)(2,1)S(1)} %pad_maximum_fusion.2.refs_0_), channel_id=1, source_target_pairs={{0,17},{1,16},{2,19},{3,18},{4,21},{5,20},{6,23},{7,22},{8,25},{9,... | collective-permute-start | bytes 786440 | tf_op jit(solution)/shard_map/ppermute | solution.py:323
  167.8 10.9 %collective-permute-start.39 = (bf16[2,64,1024]{2,1,0:T(8,128)(2,1)S(1)}, bf16[2,64,1024]{2,1,0:T(8,128)(2,1)S(1)}, u32[]{:S(2)}, u32[]{:S(2)}) collective-permute-start(bf16[2,64,1024]{2,1,0:T(8,128)(2,1)S(1)} %pad_maximum_fusion.2.refs_0_), channel_id=1, source_target_pairs={{0,16},{1,17},{2,18},{3,19},{4,20},{5,21},{6,22},{7,23},{8,24},{9,... | collective-permute-start | bytes 786440 | tf_op jit(solution)/shard_map/ppermute | solution.py:323
  168.3 10.4 %collective-permute-start.38 = (bf16[2,64,1024]{2,1,0:T(8,128)(2,1)S(1)}, bf16[2,64,1024]{2,1,0:T(8,128)(2,1)S(1)}, u32[]{:S(2)}, u32[]{:S(2)}) collective-permute-start(bf16[2,64,1024]{2,1,0:T(8,128)(2,1)S(1)} %pad_maximum_fusion.2.refs_0_), channel_id=1, source_target_pairs={{0,1},{1,0},{2,3},{3,2},{4,5},{5,4},{6,7},{7,6},{8,9},{9,8},{10,11... | collective-permute-start | bytes 786440 | tf_op jit(solution)/shard_map/ppermute | solution.py:323
  183.0 19.3 %collective-permute-start.43 = (bf16[2,2,1152,128]{3,2,1,0:T(8,128)(2,1)S(1)}, bf16[2,2,1152,128]{3,2,1,0:T(8,128)(2,1)S(1)}, u32[]{:S(2)}, u32[]{:S(2)}) collective-permute-start(bf16[2,2,1152,128]{3,2,1,0:T(8,128)(2,1)S(1)} %get-tuple-element.224), channel_id=1, source_target_pairs={{0,2},{1,3},{2,0},{3,1},{4,6},{5,7},{6,4},{7,5},{8,10},{9,11},{10,... | collective-permute-start | bytes 3538952 | tf_op jit(solution)/shard_map/ppermute | solution.py:323
  183.1 9.7 %collective-permute-start.41 = (bf16[64,1024]{1,0:T(8,128)(2,1)S(1)}, bf16[64,1024]{1,0:T(8,128)(2,1)S(1)}, u32[]{:S(2)}, u32[]{:S(2)}) collective-permute-start(bf16[64,1024]{1,0:T(8,128)(2,1)S(1)} %broadcast_select_fusion.10), channel_id=1, source_target_pairs={{0,8},{1,9},{2,10},{3,11},{4,12},{5,13},{6,14},{7,15},{8,0},{9,1},... | collective-permute-start | bytes 393224 | tf_op jit(solution)/shard_map/ppermute | solution.py:323
  183.7 9.2 %collective-permute-start.44 = (bf16[2,64,1024]{2,1,0:T(8,128)(2,1)S(1)}, bf16[2,64,1024]{2,1,0:T(8,128)(2,1)S(1)}, u32[]{:S(2)}, u32[]{:S(2)}) collective-permute-start(bf16[2,64,1024]{2,1,0:T(8,128)(2,1)S(1)} %get-tuple-element.228), channel_id=1, source_target_pairs={{0,1},{1,0},{2,3},{3,2},{4,5},{5,4},{6,7},{7,6},{8,9},{9,8},{10,11... | collective-permute-start | bytes 786440 | tf_op jit(solution)/shard_map/ppermute | solution.py:323
  185.1 9.3 %collective-permute-start.45 = (bf16[2,64,1024]{2,1,0:T(8,128)(2,1)S(1)}, bf16[2,64,1024]{2,1,0:T(8,128)(2,1)S(1)}, u32[]{:S(2)}, u32[]{:S(2)}) collective-permute-start(bf16[2,64,1024]{2,1,0:T(8,128)(2,1)S(1)} %get-tuple-element.230), channel_id=1, source_target_pairs={{0,16},{1,17},{2,18},{3,19},{4,20},{5,21},{6,22},{7,23},{8,24},{9,... | collective-permute-start | bytes 786440 | tf_op jit(solution)/shard_map/ppermute | solution.py:323
  186.6 12.4 %collective-permute-start.46 = (bf16[2,64,1024]{2,1,0:T(8,128)(2,1)S(1)}, bf16[2,64,1024]{2,1,0:T(8,128)(2,1)S(1)}, u32[]{:S(2)}, u32[]{:S(2)}) collective-permute-start(bf16[2,64,1024]{2,1,0:T(8,128)(2,1)S(1)} %get-tuple-element.232), channel_id=1, source_target_pairs={{0,17},{1,16},{2,19},{3,18},{4,21},{5,20},{6,23},{7,22},{8,25},{9,... | collective-permute-start | bytes 786440 | tf_op jit(solution)/shard_map/ppermute | solution.py:323
  192.8 12.2 %collective-permute-start.47 = (f32[2,512,128]{2,1,0:T(8,128)S(1)}, f32[2,512,128]{2,1,0:T(8,128)S(1)}, u32[]{:S(2)}, u32[]{:S(2)}) collective-permute-start(f32[2,512,128]{2,1,0:T(8,128)S(1)} %get-tuple-element.236), channel_id=1, source_target_pairs={{0,2},{1,3},{2,0},{3,1},{4,6},{5,7},{6,4},{7,5},{8,10},{9,11},{10,... | collective-permute-start | bytes 1572872 | tf_op jit(solution)/shard_map/ppermute | solution.py:323
  192.9 19.1 %collective-permute-start.42 = (bf16[64,1024]{1,0:T(8,128)(2,1)S(1)}, bf16[64,1024]{1,0:T(8,128)(2,1)S(1)}, u32[]{:S(2)}, u32[]{:S(2)}) collective-permute-start(bf16[64,1024]{1,0:T(8,128)(2,1)S(1)} %collective-permute-done.41), channel_id=1, source_target_pairs={{0,1},{1,0},{2,3},{3,2},{4,5},{5,4},{6,7},{7,6},{8,9},{9,8},{10,11... | collective-permute-start | bytes 393224 | tf_op jit(solution)/shard_map/ppermute | solution.py:323
  199.7 12.9 %collective-permute-start.54 = (bf16[64,1024]{1,0:T(8,128)(2,1)S(1)}, bf16[64,1024]{1,0:T(8,128)(2,1)S(1)}, u32[]{:S(2)}, u32[]{:S(2)}) collective-permute-start(bf16[64,1024]{1,0:T(8,128)(2,1)S(1)} %get-tuple-element.233), channel_id=1, source_target_pairs={{0,4},{1,5},{2,6},{3,7},{4,0},{5,1},{6,2},{7,3},{8,12},{9,13},{10,... | collective-permute-start | bytes 393224 | tf_op jit(solution)/shard_map/ppermute | solution.py:323
  202.4 18.3 %collective-permute-start.48 = (bf16[1152,128]{1,0:T(8,128)(2,1)S(1)}, bf16[1152,128]{1,0:T(8,128)(2,1)S(1)}, u32[]{:S(2)}, u32[]{:S(2)}) collective-permute-start(bf16[1152,128]{1,0:T(8,128)(2,1)S(1)} %get-tuple-element.276), channel_id=1, source_target_pairs={{0,8},{1,9},{2,10},{3,11},{4,12},{5,13},{6,14},{7,15},{8,0},{9,1},... | collective-permute-start | bytes 884744 | tf_op jit(solution)/shard_map/ppermute | solution.py:323
  209.0 11.7 %collective-permute-start.50 = (bf16[2,64,1024]{2,1,0:T(8,128)(2,1)S(1)}, bf16[2,64,1024]{2,1,0:T(8,128)(2,1)S(1)}, u32[]{:S(2)}, u32[]{:S(2)}) collective-permute-start(bf16[2,64,1024]{2,1,0:T(8,128)(2,1)S(1)} %get-tuple-element.245), channel_id=1, source_target_pairs={{0,1},{1,0},{2,3},{3,2},{4,5},{5,4},{6,7},{7,6},{8,9},{9,8},{10,11... | collective-permute-start | bytes 786440 | tf_op jit(solution)/shard_map/ppermute | solution.py:323
  210.4 10.2 %collective-permute-start.51 = (bf16[2,64,1024]{2,1,0:T(8,128)(2,1)S(1)}, bf16[2,64,1024]{2,1,0:T(8,128)(2,1)S(1)}, u32[]{:S(2)}, u32[]{:S(2)}) collective-permute-start(bf16[2,64,1024]{2,1,0:T(8,128)(2,1)S(1)} %get-tuple-element.246), channel_id=1, source_target_pairs={{0,16},{1,17},{2,18},{3,19},{4,20},{5,21},{6,22},{7,23},{8,24},{9,... | collective-permute-start | bytes 786440 | tf_op jit(solution)/shard_map/ppermute | solution.py:323
  212.0 10.5 %collective-permute-start.52 = (bf16[2,64,1024]{2,1,0:T(8,128)(2,1)S(1)}, bf16[2,64,1024]{2,1,0:T(8,128)(2,1)S(1)}, u32[]{:S(2)}, u32[]{:S(2)}) collective-permute-start(bf16[2,64,1024]{2,1,0:T(8,128)(2,1)S(1)} %get-tuple-element.247), channel_id=1, source_target_pairs={{0,17},{1,16},{2,19},{3,18},{4,21},{5,20},{6,23},{7,22},{8,25},{9,... | collective-permute-start | bytes 786440 | tf_op jit(solution)/shard_map/ppermute | solution.py:323
  218.1 12.0 %collective-permute-start.58 = (bf16[1152,128]{1,0:T(8,128)(2,1)S(1)}, bf16[1152,128]{1,0:T(8,128)(2,1)S(1)}, u32[]{:S(2)}, u32[]{:S(2)}) collective-permute-start(bf16[1152,128]{1,0:T(8,128)(2,1)S(1)} %get-tuple-element.277), channel_id=1, source_target_pairs={{0,8},{1,9},{2,10},{3,11},{4,12},{5,13},{6,14},{7,15},{8,0},{9,1},... | collective-permute-start | bytes 884744 | tf_op jit(solution)/shard_map/ppermute | solution.py:323
  220.7 14.6 %collective-permute-start.62 = (bf16[2,2,448,128]{3,2,1,0:T(8,128)(2,1)S(1)}, bf16[2,2,448,128]{3,2,1,0:T(8,128)(2,1)S(1)}, u32[]{:S(2)}, u32[]{:S(2)}) collective-permute-start(bf16[2,2,448,128]{3,2,1,0:T(8,128)(2,1)S(1)} %get-tuple-element.243), channel_id=1, source_target_pairs={{0,2},{1,3},{2,0},{3,1},{4,6},{5,7},{6,4},{7,5},{8,10},{9,11},{10,... | collective-permute-start | bytes 1376264 | tf_op jit(solution)/shard_map/ppermute | solution.py:323
  223.2 9.6 %collective-permute-start.53 = (bf16[64,1024]{1,0:T(8,128)(2,1)S(1)}, bf16[64,1024]{1,0:T(8,128)(2,1)S(1)}, u32[]{:S(2)}, u32[]{:S(2)}) collective-permute-start(bf16[64,1024]{1,0:T(8,128)(2,1)S(1)} %get-tuple-element.249), channel_id=1, source_target_pairs={{0,4},{1,5},{2,6},{3,7},{4,0},{5,1},{6,2},{7,3},{8,12},{9,13},{10,... | collective-permute-start | bytes 393224 | tf_op jit(solution)/shard_map/ppermute | solution.py:323
  225.6 21.9 %collective-permute-start.60 = (bf16[1152,128]{1,0:T(8,128)(2,1)S(1)}, bf16[1152,128]{1,0:T(8,128)(2,1)S(1)}, u32[]{:S(2)}, u32[]{:S(2)}) collective-permute-start(bf16[1152,128]{1,0:T(8,128)(2,1)S(1)} %get-tuple-element.273), channel_id=1, source_target_pairs={{0,16},{1,17},{2,18},{3,19},{4,20},{5,21},{6,22},{7,23},{8,24},{9,... | collective-permute-start | bytes 884744 | tf_op jit(solution)/shard_map/ppermute | solution.py:323
  230.3 39.8 %collective-permute-start.59 = (bf16[1152,128]{1,0:T(8,128)(2,1)S(1)}, bf16[1152,128]{1,0:T(8,128)(2,1)S(1)}, u32[]{:S(2)}, u32[]{:S(2)}) collective-permute-start(bf16[1152,128]{1,0:T(8,128)(2,1)S(1)} %get-tuple-element.274), channel_id=1, source_target_pairs={{0,16},{1,17},{2,18},{3,19},{4,20},{5,21},{6,22},{7,23},{8,24},{9,... | collective-permute-start | bytes 884744 | tf_op jit(solution)/shard_map/ppermute | solution.py:323
  233.6 10.2 %collective-permute-start.55 = (bf16[64,1024]{1,0:T(8,128)(2,1)S(1)}, bf16[64,1024]{1,0:T(8,128)(2,1)S(1)}, u32[]{:S(2)}, u32[]{:S(2)}) collective-permute-start(bf16[64,1024]{1,0:T(8,128)(2,1)S(1)} %broadcast_select_fusion.8), channel_id=1, source_target_pairs={{0,16},{1,17},{2,18},{3,19},{4,20},{5,21},{6,22},{7,23},{8,24},{9,... | collective-permute-start | bytes 393224 | tf_op jit(solution)/shard_map/ppermute | solution.py:323
  235.4 19.6 %collective-permute-start.63 = (bf16[2,448,128]{2,1,0:T(8,128)(2,1)S(1)}, bf16[2,448,128]{2,1,0:T(8,128)(2,1)S(1)}, u32[]{:S(2)}, u32[]{:S(2)}) collective-permute-start(bf16[2,448,128]{2,1,0:T(8,128)(2,1)S(1)} %pad_maximum_fusion.4), channel_id=1, source_target_pairs={{0,8},{1,9},{2,10},{3,11},{4,12},{5,13},{6,14},{7,15},{8,0},{9,1},... | collective-permute-start | bytes 688136 | tf_op jit(solution)/shard_map/ppermute | solution.py:323
  243.9 10.0 %collective-permute-start.56 = (bf16[64,1024]{1,0:T(8,128)(2,1)S(1)}, bf16[64,1024]{1,0:T(8,128)(2,1)S(1)}, u32[]{:S(2)}, u32[]{:S(2)}) collective-permute-start(bf16[64,1024]{1,0:T(8,128)(2,1)S(1)} %get-tuple-element.295), channel_id=1, source_target_pairs={{0,8},{1,9},{2,10},{3,11},{4,12},{5,13},{6,14},{7,15},{8,0},{9,1},... | collective-permute-start | bytes 393224 | tf_op jit(solution)/shard_map/ppermute | solution.py:323
  247.6 22.5 %collective-permute-start.61 = (bf16[2,1152,128]{2,1,0:T(8,128)(2,1)S(1)}, bf16[2,1152,128]{2,1,0:T(8,128)(2,1)S(1)}, u32[]{:S(2)}, u32[]{:S(2)}) collective-permute-start(bf16[2,1152,128]{2,1,0:T(8,128)(2,1)S(1)} %pad_maximum_fusion), channel_id=1, source_target_pairs={{0,4},{1,5},{2,6},{3,7},{4,0},{5,1},{6,2},{7,3},{8,12},{9,13},{10,... | collective-permute-start | bytes 1769480 | tf_op jit(solution)/shard_map/ppermute | solution.py:323
  254.0 8.6 %collective-permute-start.57 = (bf16[2,64,1024]{2,1,0:T(8,128)(2,1)S(1)}, bf16[2,64,1024]{2,1,0:T(8,128)(2,1)S(1)}, u32[]{:S(2)}, u32[]{:S(2)}) collective-permute-start(bf16[2,64,1024]{2,1,0:T(8,128)(2,1)S(1)} %maximum_select_fusion.3), channel_id=1, source_target_pairs={{0,1},{1,0},{2,3},{3,2},{4,5},{5,4},{6,7},{7,6},{8,9},{9,8},{10,11... | collective-permute-start | bytes 786440 | tf_op jit(solution)/shard_map/ppermute | solution.py:323
  (31 other events, 296.4 us)
where the time goes:
time: 274 us
  waiting for transfers between devices  128 us (47%)
  starting transfers between devices  71.7 us (26%)
  Pallas kernels  63.6 us (23%)
  other arithmetic  4.7 us (2%)
  local copies, waits for them, and re-layouts  4.38 us (2%)
    ppermute x66, waiting for transfers between devices, swapped(): return lax.ppermute(array, ALL, pairs)  128 us
    ppermute x66, starting transfers between devices, swapped(): return lax.ppermute(array, ALL, pairs)  71.7 us
    pallas_call x29, Pallas kernels, kernel_call(): pl.pallas_call(body, name=name, out_shape=[(pltpu.VMEM if keep else jax.S...  59.9 us
  transfers between devices with their start and end apart: 66, of which 34 were waited for; matrix products, arithmetic and copies ran while one was open for 2% of the time, Pallas kernels for 13%

commit v1 on v0

--- a/solution.py
+++ b/solution.py
@@ -413,11 +413,8 @@
     return [(rows, dim), (rows, dim // 2)]
 
 
-def send_tokens(mine, strip):
-    near = swapped(mine, NEAR)
-    far = swapped(strip, HALF)
-    far_near = swapped(strip, HALF | NEAR)
-    return mine, near, far, far_near, swapped(far, SIDE), swapped(far_near, SIDE)
+def send_strips(strip):
+    return swapped(strip, HALF), swapped(strip, HALF | NEAR)
 
 
 def start_loader(at, refs):
@@ -823,13 +820,11 @@
     return [pair] + [swapped(pair, mask) for mask in STEP_CHIPS[1:]]
 
 
-def attention_forward(at, q, kv, kv_other, active, w):
+def attention_forward(at, q, kv, kv_other):
     rows = q.shape[0]
-    units, dim = w["down"].shape
     scale = 1.0 / math.sqrt(HD)
 
-    def body(at, q, kv, kv_other, active, mixed, lse, *rest):
-        pieces, (out, down, total) = rest[:4], rest[4:]
+    def body(at, q, kv, kv_other, mixed, lse):
         first_head = head_lanes()
         step = 256
         for first in range(0, rows, step):
@@ -861,15 +856,30 @@
                 totals.append(most + jnp.log(summed))
             mixed[span] = jnp.where(first_head, results[0], results[1]).astype(B16)
             lse[span] = jnp.where(first_head, totals[0], totals[1])
+
+    return kernel_call_named(
+        "attention_forward", body, [((rows, ONE), B16), ((rows, ONE), F32)], at, q, kv, kv_other,
+        flops=8 * rows * rows * ONE * 2, exps=2 * rows * rows * 2,
+    )
+
+
+def outputs_forward(at, mixed, active, w):
+    rows = mixed.shape[0]
+    units, dim = w["down"].shape
+
+    def body(at, mixed, active, *rest):
+        pieces, (out, down, total) = rest[:4], rest[4:]
+
+        def one(span):
             total[span] = nn(mixed[span], out[...]) + nn(active[span], down[...])
+
+        by_rows(rows, 256, one)
         pieces_out(at, total, pieces)
 
-    outs = [((rows, ONE), B16), ((rows, ONE), F32)] + piece_shapes(rows, dim)
     return weights_call(
-        "attention_forward", body, outs, at, [q, kv, kv_other, active], [w["out"], w["down"]],
-        scratch=[pltpu.VMEM((rows, dim), F32)],
-        flops=2 * rows * dim * (units + ONE) + 8 * rows * rows * ONE * 2,
-        exps=2 * rows * rows * 2,
+        "outputs_forward", body, piece_shapes(rows, dim), at, [mixed, active],
+        [w["out"], w["down"]], scratch=[pltpu.VMEM((rows, dim), F32)],
+        flops=2 * rows * dim * (units + ONE),
     )
 
 
@@ -1086,13 +1096,12 @@
     )
 
 
-def late_grads(at, attn_in, qkv_grad, table, table_side):
+def late_grads(at, attn_in, qkv_grad, tables):
     rows, dim = attn_in.shape
-
-    def body(at, attn_in, qkv_grad, table, table_side, keep, give):
-        lines = lax.broadcasted_iota(jnp.int32, table.shape, 0) < 4 * dim // ONE
-        other = jnp.where(lines, table_side[...].astype(F32), 0.0)
-        joined = (table[...].astype(F32) + other).astype(B16)
+    count = len(tables)
+
+    def body(at, attn_in, qkv_grad, *refs):
+        tables, (keep, give) = refs[:count], refs[count:]
         for core, target in ((0, keep), (1, give)):
             for high in range(2):
                 qkv = tn(columns(at, attn_in, core, high), qkv_grad[...]).astype(B16)
@@ -1102,12 +1111,13 @@
                         target[where[0], where[1], i * ONE : (i + 1) * ONE] = qkv[
                             low * ONE : (low + 1) * ONE, i * ONE : (i + 1) * ONE
                         ]
-                    target[where[0], where[1], 3 * ONE :] = joined
-
-    shape = (2, 2, 3 * ONE + LINES, ONE)
+                    for i, table in enumerate(tables):
+                        base = 3 * ONE + i * LINES
+                        target[where[0], where[1], base : base + LINES] = table[...]
+
+    shape = (2, 2, 3 * ONE + count * LINES, ONE)
     return kernel_call_named(
-        "late_grads",
-        body, [(shape, B16)] * 2, at, attn_in, qkv_grad, table, table_side,
+        "late_grads", body, [(shape, B16)] * 2, at, attn_in, qkv_grad, *tables,
         flops=2 * rows * dim * 3 * ONE,
     )
 
@@ -1116,22 +1126,32 @@
     return (a.astype(F32) + b.astype(F32)).astype(B16)
 
 
-def summed_cores(keep, give):
-    got = swapped(give, CORE)
+def summed_cores(keep, give, *earlier):
+    got = swapped(after(give, *earlier), CORE)
     return (
         [plus(keep[0, i], got[0, i]) for i in range(2)],
         [plus(keep[1, i], got[1, i]) for i in range(2)],
     )
 
 
+def sum_lines(at, late):
+    def body(at, *refs):
+        *late, lines = refs
+        total = 0.0
+        for part in late:
+            total = total + part[3 * ONE : 3 * ONE + lines.shape[0]].astype(F32)
+        lines[...] = total
+
+    return kernel_call_named("sum_lines", body, [((32, ONE), F32)], at, *late)[0]
+
+
 def unpack_grads(at, early, late, sizes):
     dim_part, units, heads = ONE, sizes["units"], ONE
 
     def body(at, *refs):
         early, late = refs[:4], refs[4:8]
-        qkv, out, up, down, lines, b_qkv, b_up, branch = refs[8:]
+        qkv, out, up, down, b_qkv, b_up, branch = refs[8:]
         index = at[S_OWN]
-        total = 0.0
         for j, (wide, narrow) in enumerate(zip(early, late)):
             source = index ^ (2 * (j % 2) + j // 2)
             place = pl.multiple_of(source * units, units)
@@ -1144,21 +1164,18 @@
             for i in range(3):
                 qkv[i, :, pl.ds(small, ONE)] = narrow[i * ONE : (i + 1) * ONE].astype(F32)
             table = narrow[3 * ONE :].astype(F32)
-            total = total + table[:32]
             for i in range(units // ONE):
                 b_up[:, pl.ds(place + i * ONE, ONE)] = table[40 + i : 41 + i]
             for i in range(3):
                 b_qkv[i : i + 1, pl.ds(small, ONE)] = table[40 + units // ONE + i :][:1]
             if j == 0:
                 branch[...] = table[32:40]
-        lines[...] = total
 
     outs = [
         ((3, dim_part, 4 * heads), F32),
         ((4 * heads, dim_part), F32),
         ((dim_part, 4 * units), F32),
         ((4 * units, dim_part), F32),
-        ((32, ONE), F32),
         ((3, 4 * heads), F32),
         ((1, 4 * units), F32),
         ((8, ONE), F32),
@@ -1183,133 +1200,156 @@
     g_mine, g_strip, sent_up, sent_down = pack_second(
         at, cotangent, up_weight, out_weight, down_weight
     )
-    x_parts = send_tokens(mine, strip)
+    strips = send_strips(strip)
+    turns = turn_tables(at, rows)
+    sides = [swapped(after(part, turns[0]), SIDE) for part in strips]
+    x_parts = (mine, swapped(mine, NEAR), *strips, *sides)
     got_qkv, layers = first_weights(at, vectors, qkv_weight, sent_qkv)
-    got_up = swapped(after(sent_up, got_qkv, x_parts[1]), SECTION)
-    got_down = swapped(after(sent_down, got_up, *x_parts[4:]), SECTION)
-    g_parts = send_tokens(after(g_mine, *x_parts[4:]), after(g_strip, *x_parts[4:]))
+    got_up = swapped(after(sent_up, got_qkv), SECTION)
     first, second = layers
-    turns = turn_tables(at, rows)
-
-    def bring_rest(q):
-        up = up_weights(at, up_weight, got_up, swapped(after(got_up, q), CORE))
+    got_down = swapped(
+        after(sent_down, got_up, *x_parts[4:], first["qkv"], first["rows"]), SECTION
+    )
+
+    def bring_up(*earlier):
+        up = up_weights(at, up_weight, got_up, swapped(after(got_up, *earlier), CORE))
+        for i, layer in enumerate(layers):
+            layer.update(up=up[i], units=up[i].shape[1])
+
+    def bring_rows(*earlier):
         tall = row_weights(
-            at, down_weight, out_weight, got_down,
-            swapped(after(got_down, q, up[0], *g_parts[1:4]), CORE),
+            at, down_weight, out_weight, got_down, swapped(after(got_down, *earlier), CORE)
         )
         for i, layer in enumerate(layers):
-            layer.update(up=up[i], down=tall[i], out=tall[2 + i], units=up[i].shape[1])
+            layer.update(down=tall[i], out=tall[2 + i])
 
     def forward(loader, sources, w, with_piece):
         got = front(at, loader, sources, w, turns, with_piece)
         attn_in, mlp_in, normed, q, kv = got[:5]
         kv_other = swapped(kv, CORE)
-        if "up" not in w:
-            bring_rest(q)
+        is_start = "up" not in w
+        if is_start:
+            bring_up(q)
         active, slope = units_forward(at, mlp_in, w)
-        made = attention_forward(at, q, kv, kv_other, active, w)
-        mixed, lse, pieces = made[0], made[1], made[2:]
+        mixed, lse = attention_forward(at, q, kv, kv_other)
+        if is_start:
+            bring_rows(active, mixed)
+        pieces = outputs_forward(at, mixed, active, w)
         saved = dict(
             attn_in=attn_in, mlp_in=mlp_in, normed=normed, q=q, kv=kv, kv_other=kv_other,
             active=active, slope=slope, mixed=mixed, lse=lse,
         )
         return pieces, saved, got[5:]
 
-    def backward(loader, sources, saved, w, with_piece, earlier=()):
+    def backward(loader, sources, saved, w, with_piece):
         made = units_backward(at, loader, sources, saved["slope"], w, with_piece)
         g, up_grad, mixed_grad = made[:3]
-        early = early_grads(at, saved["active"], saved["mixed"], saved["mlp_in"], up_grad, g)
         dq, dkv, dkv_other = attention_backward(
-            at, saved["q"], saved["kv"], saved["kv_other"], saved["lse"],
-            after(mixed_grad, early[0], *earlier),
+            at, saved["q"], saved["kv"], saved["kv_other"], saved["lse"], mixed_grad
         )
         dkv_got = swapped(dkv_other, CORE)
-        return early, (dq, dkv, dkv_got, up_grad, saved["normed"], g), made[3:]
+        early = early_grads(
+            at, saved["active"], saved["mixed"], saved["mlp_in"], up_grad, after(g, dkv_other)
+        )
+        given = (after(dq, early[0]), dkv, dkv_got, up_grad, saved["normed"], g)
+        return early, given, made[3:]
 
     def backward_end(given, saved, w):
         out = inputs_backward(at, *given, turns, w)
-        qkv_grad, table, pieces = out[0], out[1], out[2:]
-        late = late_grads(at, saved["attn_in"], qkv_grad, table, swapped(table, SIDE))
-        return exchanged(pieces), late
+        return out[0], out[1], out[2:]
 
     parts, saved_first, (x_piece,) = forward(start_loader, x_parts, first, True)
-    keep, give = fold(at, exchanged(parts))
+    strips = send_strips(after(g_strip, parts[0]))
+    parts = exchanged(parts)
+    parts[0] = after(parts[0], *strips)
+    keep, give = fold(at, parts)
+    sides = [swapped(part, SIDE) for part in strips]
     piece = join_forward(at, x_piece, [keep, swapped(give, NEAR)], first)
-    middle = gathered(piece, after(swapped(piece, NEAR), *g_parts[4:]))
+    near = after(swapped(piece, NEAR), *sides)
+    middle = gathered(piece, near)
+    g_near = swapped(after(g_mine, near), NEAR)
+    middle[0] = after(middle[0], g_near)
+    g_parts = (g_mine, g_near, *strips, *sides)
 
     parts_last, saved_second, blocks = forward(piece_loader, middle, second, False)
     acts_mine, acts_give = blocks
 
     early, given, (g_piece,) = backward(start_loader, g_parts, saved_second, second, True)
-    early_keep, early_give = summed_cores(*early)
-    given = (after(given[0], *early_give),) + given[1:]
-    parts, late = backward_end(given, saved_second, second)
+    early_keep, early_give = summed_cores(*early, given[2])
+    qkv_grad, table_second, pieces = backward_end(given, saved_second, second)
+    late = late_grads(at, saved_second["attn_in"], qkv_grad, ())
+    parts = exchanged(pieces)
     far_second = swapped(early_give[1], HALF)
     parts[0] = after(parts[0], far_second, *late)
     keep, give = fold(at, parts)
     late_keep, late_give = summed_cores(*late)
     late_got = swapped(after(jnp.stack(late_give), give), HALF)
+    parts_last = exchanged([after(p, give) for p in parts_last])
     back = join_backward(at, g_piece, piece, [keep, swapped(give, NEAR)])
-    near = after(swapped(back, NEAR), late_got)
+    near = after(swapped(back, NEAR), late_got, *parts_last)
     g_middle = gathered(back, near)
     close_second = swapped(after(early_give[0], near), HALF)
     g_middle[0] = after(g_middle[0], close_second)
-
-    parts_last = exchanged([after(p, *g_middle) for p in parts_last])
+    keep_last, give_last = fold(at, parts_last)
+
     early, given, blocks = backward(piece_loader, g_middle, saved_first, first, False)
     in_mine, in_give = blocks
     early_second = [plus(a, b) for a, b in zip(early_keep, (close_second, far_second))]
     late_second = [plus(a, b) for a, b in zip(late_keep, late_got)]
-    early_keep, early_give = summed_cores(*early)
-    keep_last, give_last = fold(at, parts_last)
-    given = (after(given[0], *early_give, give_last),) + given[1:]
-    parts, late = backward_end(given, saved_first, first)
+    early_keep, early_give = summed_cores(*early, given[2])
+    given = (after(given[0], *early_give),) + given[1:]
+    qkv_grad, table_first, pieces = backward_end(given, saved_first, first)
+    parts = exchanged(pieces)
     far_first = swapped(early_give[1], HALF)
-    parts[0] = after(parts[0], far_first, *late)
+    late = late_grads(at, saved_first["attn_in"], qkv_grad, (table_first, table_second))
+    parts[0] = after(parts[0], far_first)
     keep, give = fold(at, parts)
-    close_first = swapped(early_give[0], HALF)
-    back_last = join_backward(at, back, x_piece, [keep, swapped(give, NEAR)])
-    last = join_forward(at, piece, [keep_last, swapped(give_last, NEAR)], second)
+    close_first = swapped(after(early_give[0], give), HALF)
+    late_keep, late_give = summed_cores(*late)
+    late_got = swapped(after(jnp.stack(late_give), give), HALF)
+    back_last = join_backward(
+        at, back, x_piece, [keep, after(swapped(give, NEAR), close_first)]
+    )
+    last = join_forward(at, piece, [keep_last, swapped(after(give_last, give), NEAR)], second)
     early_first = [plus(a, b) for a, b in zip(early_keep, (close_first, far_first))]
-    late_keep, late_give = summed_cores(*late)
-    late_got = swapped(jnp.stack(late_give), HALF)
     late_first = [plus(a, b) for a, b in zip(late_keep, late_got)]
-    known_got = swapped(jnp.where(is_first, acts_give, in_give), HALF)
-    known_rest = swapped(known_got, SIDE)
-
-    def owned(one, two):
-        return jnp.where(is_first, one, two), swapped(jnp.where(is_first, two, one), SECTION)
-
-    far_own, far_got = owned(early_first[1], early_second[1])
-    far = swapped(jnp.stack([far_own, far_got]), NEAR)
-    close_own, close_got = owned(early_first[0], early_second[0])
-    late_own, late_got = owned(jnp.stack(late_first), jnp.stack(late_second))
-    late_near = swapped(jnp.stack([late_own[1], late_got[1]]), NEAR)
+    tall = 3 * ONE + LINES
+    late_second = [
+        jnp.concatenate([a, b[tall:]], axis=0) for a, b in zip(late_second, late_first)
+    ]
+    late_first = [a[:tall] for a in late_first]
+    def brought(close, far):
+        own = jnp.where(is_first, close[0], close[1])
+        near = swapped(jnp.where(is_first, far[0], far[1]), NEAR)
+        got = swapped(jnp.where(is_first, close[1], close[0]), SECTION)
+        cross = swapped(jnp.where(is_first, far[1], far[0]), SECTION | NEAR)
+        return own, got, near, cross
+
+    early, late = [
+        brought((one[0], two[0]), (one[1], two[1]))
+        for one, two in ((early_first, early_second), (late_first, late_second))
+    ]
+    lines = sum_lines(at, late)
+    lines = lines + swapped(lines, SIDE)
     sizes = dict(units=up_weight.shape[2] // 4)
-    qkv, out, up, down, lines, b_qkv, b_up, branch = unpack_grads(
-        at,
-        (close_own, close_got, far[0], far[1]),
-        (late_own[0], late_got[0], late_near[0], late_near[1]),
-        sizes,
-    )
-
-    known_mine = jnp.where(is_first, acts_mine, in_mine)
-    known_other = jnp.where(
-        is_left,
-        jnp.concatenate([known_got, known_rest], axis=0),
-        jnp.concatenate([known_rest, known_got], axis=0),
-    )
-    known = jnp.where(
-        is_low, jnp.stack([known_mine, known_other]), jnp.stack([known_other, known_mine])
-    )
+    qkv, out, up, down, b_qkv, b_up, branch = unpack_grads(at, early, late, sizes)
+
     mine = jnp.where(is_first, back_last, last)
     got = swapped(jnp.where(is_first, last, back_last), SECTION)
     stay = jnp.where(is_near, mine, got)
-    other = swapped(jnp.where(is_near, got, mine), HALF)
-    own = jnp.where(is_low, jnp.stack([stay, other]), jnp.stack([other, stay]))
+    known_give = jnp.where(is_first, acts_give, in_give)
+    other = swapped(jnp.stack([jnp.where(is_near, got, mine), known_give]), HALF)
+    own = jnp.stack(
+        [jnp.where(is_low, stay, other[0]), jnp.where(is_low, other[0], stay), other[1]]
+    )
     rest = swapped(own, SIDE)
-    new = jnp.where(
+    both = jnp.where(
         is_left, jnp.concatenate([own, rest], axis=1), jnp.concatenate([rest, own], axis=1)
+    )
+    new = both[:2]
+    known_mine = jnp.where(is_first, acts_mine, in_mine)
+    known = jnp.where(
+        is_low, jnp.stack([known_mine, both[2]]), jnp.stack([both[2], known_mine])
     )
     acts = jnp.where(is_first, known, new)
     in_grads = jnp.where(is_first, new, known)

time: 274 us -> 254 us (0.927)
  waiting for transfers between devices: 128 us -> 113 us
  starting transfers between devices: 71.7 us -> 64.8 us
    ppermute x66 -> x64, waiting for transfers between devices: 128 us -> 113 us  [swapped(): return lax.ppermute(array, ALL, pairs)]
    ppermute x66 -> x64, starting transfers between devices: 71.7 us -> 64.8 us  [swapped(): return lax.ppermute(array, ALL, pairs)]
    pallas_call x29 -> x32, Pallas kernels: 59.9 us -> 62.2 us  [kernel_call(): pl.pallas_call(body, name=name, out_shape=[(pltpu.VMEM if keep else jax.S...]
  transfers between devices with their start and end apart: 66 -> 64, of which waited for: 34 -> 35; matrix products, arithmetic and copies ran while one was open for 2% -> 2% of each run, Pallas kernels for 13% -> 17%
where the time goes in v1:
time: 254 us
  waiting for transfers between devices  113 us (44%)
  Pallas kernels  65.9 us (26%)
  starting transfers between devices  64.8 us (26%)
  other arithmetic  4.78 us (2%)
  local copies, waits for them, and re-layouts  4.33 us (2%)
    ppermute x64, waiting for transfers between devices, swapped(): return lax.ppermute(array, ALL, pairs)  113 us
    ppermute x64, starting transfers between devices, swapped(): return lax.ppermute(array, ALL, pairs)  64.8 us
    pallas_call x32, Pallas kernels, kernel_call(): pl.pallas_call(body, name=name, out_shape=[(pltpu.VMEM if keep else jax.S...  62.2 us
  transfers between devices with their start and end apart: 64, of which 35 were waited for; matrix products, arithmetic and copies ran while one was open for 2% of the time, Pallas kernels for 17%

profile of v1, /device:TPU:0, one launch (start us, length us, event | category | flops | bytes accessed | tf_op | source)
XLA Modules:
  0.0 254.0 jit_solution(448232415637243809)
XLA Ops:
  2.6 3.0 %collective-permute-start.5 = (bf16[1584,128]{1,0:T(8,128)(2,1)S(1)}, bf16[1584,128]{1,0:T(8,128)(2,1)S(1)}, u32[]{:S(2)}, u32[]{:S(2)}) collective-permute-start(bf16[1584,128]{1,0:T(8,128)(2,1)S(1)} %get-tuple-element.153), channel_id=1, source_target_pairs={{0,16},{1,17},{2,18},{3,19},{4,20},{5,21},{6,22},{7,23},{8,24},{9,... | collective-permute-start | bytes 1216520 | tf_op jit(solution)/shard_map/ppermute | solution.py:323
  5.6 3.6 %collective-permute-start.2 = (bf16[128,512]{1,0:T(8,128)(2,1)S(1)}, bf16[128,512]{1,0:T(8,128)(2,1)S(1)}, u32[]{:S(2)}, u32[]{:S(2)}) collective-permute-start(bf16[128,512]{1,0:T(8,128)(2,1)S(1)} %get-tuple-element.150), channel_id=1, source_target_pairs={{0,12},{1,13},{2,14},{3,15},{4,8},{5,9},{6,10},{7,11},{8,4},{9,5},... | collective-permute-start | bytes 393224 | tf_op jit(solution)/shard_map/ppermute | solution.py:323
  10.1 2.0 pack_second.1
  12.1 2.9 %collective-permute-done.5.refs_7_.refs_1_ = bf16[1584,128]{1,0:T(8,128)(2,1)S(1)} collective-permute-done((bf16[1584,128]{1,0:T(8,128)(2,1)S(1)}, bf16[1584,128]{1,0:T(8,128)(2,1)S(1)}, u32[]{:S(2)}, u32[]{:S(2)}) %collective-permute-start.5) | collective-permute-done | bytes 405536 | tf_op jit(solution)/shard_map/ppermute | solution.py:323
  23.1 2.0 choose_qkv.1
  25.5 2.4 collective-permute-done.3.refs_4_
  29.5 3.0 %front.2 = (bf16[512,1024]{1,0:T(8,128)(2,1)S(1)}, bf16[512,1024]{1,0:T(8,128)(2,1)S(1)}, bf16[512,1024]{1,0:T(8,128)(2,1)S(1)}, bf16[512,128]{1,0:T(8,128)(2,1)...) custom-call(s32[8]{0:T(128)S(1)} %stack.91.at, bf16[128,1024]{1,0:T(8,128)(2,1)S(1)} %get-tuple-element.149.refs_0_, ...), custom_call_target="tpu_custom_call" | custom-call | tf_op jit(solution)/shard_map/front/pallas_call | solution.py:347
  35.0 2.8 %attention_forward.2 = (bf16[512,128]{1,0:T(8,128)(2,1)S(1)}, f32[512,128]{1,0:T(8,128)S(1)}) custom-call(s32[8]{0:T(128)S(1)} %stack.91.at, bf16[512,128]{1,0:T(8,128)(2,1)S(1)} %get-tuple-element.157.q, bf16[2,512,128]{2,1,0:T(8,128)(2,1)S(1)} %get-tuple-element.158.kv, bf16[2,512,128]{2,1,0:T(8,128)(2,1)S(1)} %collective-permute-done.7.kv_other), custom_call_target="tpu_custom_call" | custom-call | tf_op jit(solution)/shard_map/attention_forward/pallas_call | solution.py:347
  38.5 2.1 choose_up.1
  40.7 2.2 units_forward.2
  44.3 2.1 collective-permute-done.11.refs_3_
  47.2 2.3 choose_rows.1
  54.8 3.6 %collective-permute-start.13 = (bf16[128,512]{1,0:T(8,128)(2,1)S(1)}, bf16[128,512]{1,0:T(8,128)(2,1)S(1)}, u32[]{:S(2)}, u32[]{:S(2)}) collective-permute-start(bf16[128,512]{1,0:T(8,128)(2,1)S(1)} %get-tuple-element.173), channel_id=1, source_target_pairs={{0,12},{1,13},{2,14},{3,15},{4,8},{5,9},{6,10},{7,11},{8,4},{9,5},... | collective-permute-start | bytes 393224 | tf_op jit(solution)/shard_map/ppermute | solution.py:323
  58.5 4.5 %collective-permute-done.13.refs_3_ = bf16[128,512]{1,0:T(8,128)(2,1)S(1)} collective-permute-done((bf16[128,512]{1,0:T(8,128)(2,1)S(1)}, bf16[128,512]{1,0:T(8,128)(2,1)S(1)}, u32[]{:S(2)}, u32[]{:S(2)}) %collective-permute-start.13) | collective-permute-done | bytes 131104 | tf_op jit(solution)/shard_map/ppermute | solution.py:323
  62.9 6.1 %collective-permute-done.12.refs_2_ = bf16[128,512]{1,0:T(8,128)(2,1)S(1)} collective-permute-done((bf16[128,512]{1,0:T(8,128)(2,1)S(1)}, bf16[128,512]{1,0:T(8,128)(2,1)S(1)}, u32[]{:S(2)}, u32[]{:S(2)}) %collective-permute-start.12) | collective-permute-done | bytes 131104 | tf_op jit(solution)/shard_map/ppermute | solution.py:323
  71.8 2.9 %collective-permute-done.17.rest_0_ = bf16[64,1024]{1,0:T(8,128)(2,1)S(1)} collective-permute-done((bf16[64,1024]{1,0:T(8,128)(2,1)S(1)}, bf16[64,1024]{1,0:T(8,128)(2,1)S(1)}, u32[]{:S(2)}, u32[]{:S(2)}) %collective-permute-start.17) | collective-permute-done | bytes 131104 | tf_op jit(solution)/shard_map/ppermute | solution.py:323
  77.1 3.7 %collective-permute-done.18 = bf16[64,1024]{1,0:T(8,128)(2,1)S(1)} collective-permute-done((bf16[64,1024]{1,0:T(8,128)(2,1)S(1)}, bf16[64,1024]{1,0:T(8,128)(2,1)S(1)}, u32[]{:S(2)}, u32[]{:S(2)}) %collective-permute-start.18) | collective-permute-done | bytes 131104 | tf_op jit(solution)/shard_map/ppermute | solution.py:323
  84.5 2.8 %collective-permute-done.21.refs_1_ = bf16[128,1024]{1,0:T(8,128)(2,1)S(1)} collective-permute-done((bf16[128,1024]{1,0:T(8,128)(2,1)S(1)}, bf16[128,1024]{1,0:T(8,128)(2,1)S(1)}, u32[]{:S(2)}, u32[]{:S(2)}) %collective-permute-start.21) | collective-permute-done | bytes 262176 | tf_op jit(solution)/shard_map/ppermute | solution.py:323
  87.2 2.3 collective-permute-done.24.refs_3_
  89.6 2.9 %collective-permute-done.23.refs_2_ = bf16[2,64,1024]{2,1,0:T(8,128)(2,1)S(1)} collective-permute-done((bf16[2,64,1024]{2,1,0:T(8,128)(2,1)S(1)}, bf16[2,64,1024]{2,1,0:T(8,128)(2,1)S(1)}, u32[]{:S(2)}, u32[]{:S(2)}) %collective-permute-start.23) | collective-permute-done | bytes 262176 | tf_op jit(solution)/shard_map/ppermute | solution.py:323
  92.4 3.1 %front.3 = (bf16[512,1024]{1,0:T(8,128)(2,1)S(1)}, bf16[512,1024]{1,0:T(8,128)(2,1)S(1)}, bf16[512,1024]{1,0:T(8,128)(2,1)S(1)}, bf16[512,128]{1,0:T(8,128)(2,1)...) custom-call(s32[8]{0:T(128)S(1)} %stack.91.at, ...), custom_call_target="tpu_custom_call" | custom-call | tf_op jit(solution)/shard_map/front/pallas_call | solution.py:347
  95.6 2.2 units_forward.3
  97.8 2.0 units_backward.2
  99.8 2.8 %attention_forward.3 = (bf16[512,128]{1,0:T(8,128)(2,1)S(1)}, f32[512,128]{1,0:T(8,128)S(1)}) custom-call(s32[8]{0:T(128)S(1)} %stack.91.at, bf16[512,128]{1,0:T(8,128)(2,1)S(1)} %get-tuple-element.193.q, bf16[2,512,128]{2,1,0:T(8,128)(2,1)S(1)} %get-tuple-element.194.kv, bf16[2,512,128]{2,1,0:T(8,128)(2,1)S(1)} %collective-permute-done.25.kv_other), custom_call_target="tpu_custom_call" | custom-call | tf_op jit(solution)/shard_map/attention_forward/pallas_call | solution.py:347
  102.6 4.0 %attention_backward.2 = (f32[512,128]{1,0:T(8,128)S(1)}, f32[2,512,128]{2,1,0:T(8,128)S(1)}, f32[2,512,128]{2,1,0:T(8,128)S(1)}) custom-call(s32[8]{0:T(128)S(1)} %stack.91.at, bf16[512,128]{1,0:T(8,128)(2,1)S(1)} %get-tuple-element.193.q, bf16[2,512,128]{2,1,0:T(8,128)(2,1)S(1)} %get-tuple-element.194.kv, ...), custom_call_target="tpu_custom_call" | custom-call | tf_op jit(solution)/shard_map/attention_backward/pallas_call | solution.py:347
  107.1 2.2 early_grads.2
  109.4 4.0 %inputs_backward.2 = (bf16[512,384]{1,0:T(8,128)(2,1)S(1)}, bf16[64,128]{1,0:T(8,128)(2,1)S(1)}, f32[2,64,1024]{2,1,0:T(8,128)S(1)}, bf16[2,64,1024]{2,1,0:T(8,1...) custom-call(s32[8]{0:T(128)S(1)} %stack.91.at, ...), custom_call_target="tpu_custom_call" | custom-call | tf_op jit(solution)/shard_map/inputs_backward/pallas_call | solution.py:347
  115.4 2.5 collective-permute-start.28
  123.3 8.4 %collective-permute-done.28 = bf16[1152,128]{1,0:T(8,128)(2,1)S(1)} collective-permute-done((bf16[1152,128]{1,0:T(8,128)(2,1)S(1)}, bf16[1152,128]{1,0:T(8,128)(2,1)S(1)}, u32[]{:S(2)}, u32[]{:S(2)}) %collective-permute-start.28) | collective-permute-done | bytes 294944 | tf_op jit(solution)/shard_map/ppermute | solution.py:323
  137.0 2.0 collective-permute-start.35
  140.4 6.3 %collective-permute-done.35 = bf16[2,384,128]{2,1,0:T(8,128)(2,1)S(1)} collective-permute-done((bf16[2,384,128]{2,1,0:T(8,128)(2,1)S(1)}, bf16[2,384,128]{2,1,0:T(8,128)(2,1)S(1)}, u32[]{:S(2)}, u32[]{:S(2)}) %collective-permute-start.35) | collective-permute-done | bytes 196640 | tf_op jit(solution)/shard_map/ppermute | solution.py:323
  152.3 9.0 %collective-permute-done.39 = bf16[1152,128]{1,0:T(8,128)(2,1)S(1)} collective-permute-done((bf16[1152,128]{1,0:T(8,128)(2,1)S(1)}, bf16[1152,128]{1,0:T(8,128)(2,1)S(1)}, u32[]{:S(2)}, u32[]{:S(2)}) %collective-permute-start.39) | collective-permute-done | bytes 294944 | tf_op jit(solution)/shard_map/ppermute | solution.py:323
  161.3 2.1 units_backward.3
  163.4 4.0 %attention_backward.3 = (f32[512,128]{1,0:T(8,128)S(1)}, f32[2,512,128]{2,1,0:T(8,128)S(1)}, f32[2,512,128]{2,1,0:T(8,128)S(1)}) custom-call(s32[8]{0:T(128)S(1)} %stack.91.at, bf16[512,128]{1,0:T(8,128)(2,1)S(1)} %get-tuple-element.157.q, bf16[2,512,128]{2,1,0:T(8,128)(2,1)S(1)} %get-tuple-element.158.kv, ...), custom_call_target="tpu_custom_call" | custom-call | tf_op jit(solution)/shard_map/attention_backward/pallas_call | solution.py:347
  167.5 2.2 early_grads.3
  170.3 2.5 collective-permute-done.44
  172.9 1.9 collective-permute-start.45
  174.8 4.0 %inputs_backward.3 = (bf16[512,384]{1,0:T(8,128)(2,1)S(1)}, bf16[64,128]{1,0:T(8,128)(2,1)S(1)}, f32[2,64,1024]{2,1,0:T(8,128)S(1)}, bf16[2,64,1024]{2,1,0:T(8,1...) custom-call(s32[8]{0:T(128)S(1)} %stack.91.at, ...), custom_call_target="tpu_custom_call" | custom-call | tf_op jit(solution)/shard_map/inputs_backward/pallas_call | solution.py:347
  184.6 4.9 %collective-permute-done.45 = bf16[1152,128]{1,0:T(8,128)(2,1)S(1)} collective-permute-done((bf16[1152,128]{1,0:T(8,128)(2,1)S(1)}, bf16[1152,128]{1,0:T(8,128)(2,1)S(1)}, u32[]{:S(2)}, u32[]{:S(2)}) %collective-permute-start.45) | collective-permute-done | bytes 294944 | tf_op jit(solution)/shard_map/ppermute | solution.py:323
  189.5 4.5 %collective-permute-done.48.refs_3_ = bf16[2,64,1024]{2,1,0:T(8,128)(2,1)S(1)} collective-permute-done((bf16[2,64,1024]{2,1,0:T(8,128)(2,1)S(1)}, bf16[2,64,1024]{2,1,0:T(8,128)(2,1)S(1)}, u32[]{:S(2)}, u32[]{:S(2)}) %collective-permute-start.48) | collective-permute-done | bytes 262176 | tf_op jit(solution)/shard_map/ppermute | solution.py:323
  198.9 9.9 %collective-permute-done.51.rest_0_ = bf16[64,1024]{1,0:T(8,128)(2,1)S(1)} collective-permute-done((bf16[64,1024]{1,0:T(8,128)(2,1)S(1)}, bf16[64,1024]{1,0:T(8,128)(2,1)S(1)}, u32[]{:S(2)}, u32[]{:S(2)}) %collective-permute-start.51) | collective-permute-done | bytes 131104 | tf_op jit(solution)/shard_map/ppermute | solution.py:323
  209.4 2.0 collective-permute-done.50
  213.3 4.0 %collective-permute-done.52 = bf16[64,1024]{1,0:T(8,128)(2,1)S(1)} collective-permute-done((bf16[64,1024]{1,0:T(8,128)(2,1)S(1)}, bf16[64,1024]{1,0:T(8,128)(2,1)S(1)}, u32[]{:S(2)}, u32[]{:S(2)}) %collective-permute-start.52) | collective-permute-done | bytes 131104 | tf_op jit(solution)/shard_map/ppermute | solution.py:323
  218.5 13.7 %collective-permute-done.56 = bf16[2,512,128]{2,1,0:T(8,128)(2,1)S(1)} collective-permute-done((bf16[2,512,128]{2,1,0:T(8,128)(2,1)S(1)}, bf16[2,512,128]{2,1,0:T(8,128)(2,1)S(1)}, u32[]{:S(2)}, u32[]{:S(2)}) %collective-permute-start.56) | collective-permute-done | bytes 262176 | tf_op jit(solution)/shard_map/ppermute | solution.py:323
  233.0 3.0 %collective-permute-start.58 = (bf16[448,128]{1,0:T(8,128)(2,1)S(1)}, bf16[448,128]{1,0:T(8,128)(2,1)S(1)}, u32[]{:S(2)}, u32[]{:S(2)}) collective-permute-start(bf16[448,128]{1,0:T(8,128)(2,1)S(1)} %get-tuple-element.315), channel_id=1, source_target_pairs={{0,4},{1,5},{2,6},{3,7},{4,0},{5,1},{6,2},{7,3},{8,12},{9,13},{10,... | collective-permute-start | bytes 344072 | tf_op jit(solution)/shard_map/ppermute | solution.py:323
  236.3 2.3 collective-permute-done.57.refs_1_.refs_5_
  246.7 2.5 unpack_grads.1
  250.4 2.2 collective-permute-done.54
  (178 shorter events, 79.6 us)
Async XLA Ops:
  2.6 12.4 %collective-permute-start.5 = (bf16[1584,128]{1,0:T(8,128)(2,1)S(1)}, bf16[1584,128]{1,0:T(8,128)(2,1)S(1)}, u32[]{:S(2)}, u32[]{:S(2)}) collective-permute-start(bf16[1584,128]{1,0:T(8,128)(2,1)S(1)} %get-tuple-element.153), channel_id=1, source_target_pairs={{0,16},{1,17},{2,18},{3,19},{4,20},{5,21},{6,22},{7,23},{8,24},{9,... | collective-permute-start | bytes 1216520 | tf_op jit(solution)/shard_map/ppermute | solution.py:323
  5.6 13.5 %collective-permute-start.2 = (bf16[128,512]{1,0:T(8,128)(2,1)S(1)}, bf16[128,512]{1,0:T(8,128)(2,1)S(1)}, u32[]{:S(2)}, u32[]{:S(2)}) collective-permute-start(bf16[128,512]{1,0:T(8,128)(2,1)S(1)} %get-tuple-element.150), channel_id=1, source_target_pairs={{0,12},{1,13},{2,14},{3,15},{4,8},{5,9},{6,10},{7,11},{8,4},{9,5},... | collective-permute-start | bytes 393224 | tf_op jit(solution)/shard_map/ppermute | solution.py:323
  9.2 11.5 %collective-permute-start.1 = (bf16[128,512]{1,0:T(8,128)(2,1)S(1)}, bf16[128,512]{1,0:T(8,128)(2,1)S(1)}, u32[]{:S(2)}, u32[]{:S(2)}) collective-permute-start(bf16[128,512]{1,0:T(8,128)(2,1)S(1)} %get-tuple-element.150), channel_id=1, source_target_pairs={{0,8},{1,9},{2,10},{3,11},{4,12},{5,13},{6,14},{7,15},{8,0},{9,1},... | collective-permute-start | bytes 393224 | tf_op jit(solution)/shard_map/ppermute | solution.py:323
  9.3 20.3 %collective-permute-start = (bf16[128,1024]{1,0:T(8,128)(2,1)S(1)}, bf16[128,1024]{1,0:T(8,128)(2,1)S(1)}, u32[]{:S(2)}, u32[]{:S(2)}) collective-permute-start(bf16[128,1024]{1,0:T(8,128)(2,1)S(1)} %get-tuple-element.149.refs_0_), channel_id=1, source_target_pairs={{0,4},{1,5},{2,6},{3,7},{4,0},{5,1},{6,2},{7,3},{8,12},{9,13},{10,... | collective-permute-start | bytes 786440 | tf_op jit(solution)/shard_map/ppermute | solution.py:323
  15.0 13.1 %collective-permute-start.8 = (bf16[512,512]{1,0:T(8,128)(2,1)S(1)}, bf16[512,512]{1,0:T(8,128)(2,1)S(1)}, u32[]{:S(2)}, u32[]{:S(2)}) collective-permute-start(bf16[512,512]{1,0:T(8,128)(2,1)S(1)} %get-tuple-element.162), channel_id=1, source_target_pairs={{0,16},{1,17},{2,18},{3,19},{4,20},{5,21},{6,22},{7,23},{8,24},{9,... | collective-permute-start | bytes 1572872 | tf_op jit(solution)/shard_map/ppermute | solution.py:323
  19.1 6.4 %collective-permute-start.4 = (bf16[128,512]{1,0:T(8,128)(2,1)S(1)}, bf16[128,512]{1,0:T(8,128)(2,1)S(1)}, u32[]{:S(2)}, u32[]{:S(2)}) collective-permute-start(bf16[128,512]{1,0:T(8,128)(2,1)S(1)} %collective-permute-done.2.refs_3_), channel_id=1, source_target_pairs={{0,1},{1,0},{2,3},{3,2},{4,5},{5,4},{6,7},{7,6},{8,9},{9,8},{10,11... | collective-permute-start | bytes 393224 | tf_op jit(solution)/shard_map/ppermute | solution.py:323
  20.7 7.2 %collective-permute-start.3 = (bf16[128,512]{1,0:T(8,128)(2,1)S(1)}, bf16[128,512]{1,0:T(8,128)(2,1)S(1)}, u32[]{:S(2)}, u32[]{:S(2)}) collective-permute-start(bf16[128,512]{1,0:T(8,128)(2,1)S(1)} %collective-permute-done.1.refs_2_), channel_id=1, source_target_pairs={{0,1},{1,0},{2,3},{3,2},{4,5},{5,4},{6,7},{7,6},{8,9},{9,8},{10,11... | collective-permute-start | bytes 393224 | tf_op jit(solution)/shard_map/ppermute | solution.py:323
  28.1 16.2 %collective-permute-start.10 = (bf16[320,1024]{1,0:T(8,128)(2,1)S(1)}, bf16[320,1024]{1,0:T(8,128)(2,1)S(1)}, u32[]{:S(2)}, u32[]{:S(2)}) collective-permute-start(bf16[320,1024]{1,0:T(8,128)(2,1)S(1)} %get-tuple-element.167), channel_id=1, source_target_pairs={{0,16},{1,17},{2,18},{3,19},{4,20},{5,21},{6,22},{7,23},{8,24},{9,... | collective-permute-start | bytes 1966088 | tf_op jit(solution)/shard_map/ppermute | solution.py:323
  51.3 17.7 %collective-permute-start.14 = (bf16[2,64,1024]{2,1,0:T(8,128)(2,1)S(1)}, bf16[2,64,1024]{2,1,0:T(8,128)(2,1)S(1)}, u32[]{:S(2)}, u32[]{:S(2)}) collective-permute-start(bf16[2,64,1024]{2,1,0:T(8,128)(2,1)S(1)} %get-tuple-element.175), channel_id=1, source_target_pairs={{0,1},{1,0},{2,3},{3,2},{4,5},{5,4},{6,7},{7,6},{8,9},{9,8},{10,11... | collective-permute-start | bytes 786440 | tf_op jit(solution)/shard_map/ppermute | solution.py:323
  52.9 16.1 %collective-permute-start.15 = (bf16[2,64,1024]{2,1,0:T(8,128)(2,1)S(1)}, bf16[2,64,1024]{2,1,0:T(8,128)(2,1)S(1)}, u32[]{:S(2)}, u32[]{:S(2)}) collective-permute-start(bf16[2,64,1024]{2,1,0:T(8,128)(2,1)S(1)} %get-tuple-element.176), channel_id=1, source_target_pairs={{0,16},{1,17},{2,18},{3,19},{4,20},{5,21},{6,22},{7,23},{8,24},{9,... | collective-permute-start | bytes 786440 | tf_op jit(solution)/shard_map/ppermute | solution.py:323
  53.4 15.6 %collective-permute-start.16 = (bf16[2,64,1024]{2,1,0:T(8,128)(2,1)S(1)}, bf16[2,64,1024]{2,1,0:T(8,128)(2,1)S(1)}, u32[]{:S(2)}, u32[]{:S(2)}) collective-permute-start(bf16[2,64,1024]{2,1,0:T(8,128)(2,1)S(1)} %get-tuple-element.177), channel_id=1, source_target_pairs={{0,17},{1,16},{2,19},{3,18},{4,21},{5,20},{6,23},{7,22},{8,25},{9,... | collective-permute-start | bytes 786440 | tf_op jit(solution)/shard_map/ppermute | solution.py:323
  54.8 8.1 %collective-permute-start.13 = (bf16[128,512]{1,0:T(8,128)(2,1)S(1)}, bf16[128,512]{1,0:T(8,128)(2,1)S(1)}, u32[]{:S(2)}, u32[]{:S(2)}) collective-permute-start(bf16[128,512]{1,0:T(8,128)(2,1)S(1)} %get-tuple-element.173), channel_id=1, source_target_pairs={{0,12},{1,13},{2,14},{3,15},{4,8},{5,9},{6,10},{7,11},{8,4},{9,5},... | collective-permute-start | bytes 393224 | tf_op jit(solution)/shard_map/ppermute | solution.py:323
  58.5 10.5 %collective-permute-start.12 = (bf16[128,512]{1,0:T(8,128)(2,1)S(1)}, bf16[128,512]{1,0:T(8,128)(2,1)S(1)}, u32[]{:S(2)}, u32[]{:S(2)}) collective-permute-start(bf16[128,512]{1,0:T(8,128)(2,1)S(1)} %get-tuple-element.173), channel_id=1, source_target_pairs={{0,8},{1,9},{2,10},{3,11},{4,12},{5,13},{6,14},{7,15},{8,0},{9,1},... | collective-permute-start | bytes 393224 | tf_op jit(solution)/shard_map/ppermute | solution.py:323
  80.9 6.4 %collective-permute-start.21 = (bf16[128,1024]{1,0:T(8,128)(2,1)S(1)}, bf16[128,1024]{1,0:T(8,128)(2,1)S(1)}, u32[]{:S(2)}, u32[]{:S(2)}) collective-permute-start(bf16[128,1024]{1,0:T(8,128)(2,1)S(1)} %get-tuple-element.182.refs_0_), channel_id=1, source_target_pairs={{0,4},{1,5},{2,6},{3,7},{4,0},{5,1},{6,2},{7,3},{8,12},{9,13},{10,... | collective-permute-start | bytes 786440 | tf_op jit(solution)/shard_map/ppermute | solution.py:323
  80.9 8.7 %collective-permute-start.24 = (bf16[2,64,1024]{2,1,0:T(8,128)(2,1)S(1)}, bf16[2,64,1024]{2,1,0:T(8,128)(2,1)S(1)}, u32[]{:S(2)}, u32[]{:S(2)}) collective-permute-start(bf16[2,64,1024]{2,1,0:T(8,128)(2,1)S(1)} %pad_maximum_fusion.1.refs_0_), channel_id=1, source_target_pairs={{0,17},{1,16},{2,19},{3,18},{4,21},{5,20},{6,23},{7,22},{8,25},{9,... | collective-permute-start | bytes 786440 | tf_op jit(solution)/shard_map/ppermute | solution.py:323
  82.5 9.9 %collective-permute-start.23 = (bf16[2,64,1024]{2,1,0:T(8,128)(2,1)S(1)}, bf16[2,64,1024]{2,1,0:T(8,128)(2,1)S(1)}, u32[]{:S(2)}, u32[]{:S(2)}) collective-permute-start(bf16[2,64,1024]{2,1,0:T(8,128)(2,1)S(1)} %pad_maximum_fusion.1.refs_0_), channel_id=1, source_target_pairs={{0,16},{1,17},{2,18},{3,19},{4,20},{5,21},{6,22},{7,23},{8,24},{9,... | collective-permute-start | bytes 786440 | tf_op jit(solution)/shard_map/ppermute | solution.py:323
  83.9 8.5 %collective-permute-start.22 = (bf16[2,64,1024]{2,1,0:T(8,128)(2,1)S(1)}, bf16[2,64,1024]{2,1,0:T(8,128)(2,1)S(1)}, u32[]{:S(2)}, u32[]{:S(2)}) collective-permute-start(bf16[2,64,1024]{2,1,0:T(8,128)(2,1)S(1)} %pad_maximum_fusion.1.refs_0_), channel_id=1, source_target_pairs={{0,1},{1,0},{2,3},{3,2},{4,5},{5,4},{6,7},{7,6},{8,9},{9,8},{10,11... | collective-permute-start | bytes 786440 | tf_op jit(solution)/shard_map/ppermute | solution.py:323
  114.7 8.5 %collective-permute-start.34 = (bf16[2,2,384,128]{3,2,1,0:T(8,128)(2,1)S(1)}, bf16[2,2,384,128]{3,2,1,0:T(8,128)(2,1)S(1)}, u32[]{:S(2)}, u32[]{:S(2)}) collective-permute-start(bf16[2,2,384,128]{3,2,1,0:T(8,128)(2,1)S(1)} %get-tuple-element.214), channel_id=1, source_target_pairs={{0,2},{1,3},{2,0},{3,1},{4,6},{5,7},{6,4},{7,5},{8,10},{9,11},{10,... | collective-permute-start | bytes 1179656 | tf_op jit(solution)/shard_map/ppermute | solution.py:323
  115.4 16.2 %collective-permute-start.28 = (bf16[1152,128]{1,0:T(8,128)(2,1)S(1)}, bf16[1152,128]{1,0:T(8,128)(2,1)S(1)}, u32[]{:S(2)}, u32[]{:S(2)}) collective-permute-start(bf16[1152,128]{1,0:T(8,128)(2,1)S(1)} %get-tuple-element.301), channel_id=1, source_target_pairs={{0,8},{1,9},{2,10},{3,11},{4,12},{5,13},{6,14},{7,15},{8,0},{9,1},... | collective-permute-start | bytes 884744 | tf_op jit(solution)/shard_map/ppermute | solution.py:323
  117.9 13.7 %collective-permute-start.29 = (bf16[2,64,1024]{2,1,0:T(8,128)(2,1)S(1)}, bf16[2,64,1024]{2,1,0:T(8,128)(2,1)S(1)}, u32[]{:S(2)}, u32[]{:S(2)}) collective-permute-start(bf16[2,64,1024]{2,1,0:T(8,128)(2,1)S(1)} %get-tuple-element.216), channel_id=1, source_target_pairs={{0,1},{1,0},{2,3},{3,2},{4,5},{5,4},{6,7},{7,6},{8,9},{9,8},{10,11... | collective-permute-start | bytes 786440 | tf_op jit(solution)/shard_map/ppermute | solution.py:323
  119.3 12.3 %collective-permute-start.30 = (bf16[2,64,1024]{2,1,0:T(8,128)(2,1)S(1)}, bf16[2,64,1024]{2,1,0:T(8,128)(2,1)S(1)}, u32[]{:S(2)}, u32[]{:S(2)}) collective-permute-start(bf16[2,64,1024]{2,1,0:T(8,128)(2,1)S(1)} %get-tuple-element.217), channel_id=1, source_target_pairs={{0,16},{1,17},{2,18},{3,19},{4,20},{5,21},{6,22},{7,23},{8,24},{9,... | collective-permute-start | bytes 786440 | tf_op jit(solution)/shard_map/ppermute | solution.py:323
  119.9 12.8 %collective-permute-start.31 = (bf16[2,64,1024]{2,1,0:T(8,128)(2,1)S(1)}, bf16[2,64,1024]{2,1,0:T(8,128)(2,1)S(1)}, u32[]{:S(2)}, u32[]{:S(2)}) collective-permute-start(bf16[2,64,1024]{2,1,0:T(8,128)(2,1)S(1)} %get-tuple-element.218), channel_id=1, source_target_pairs={{0,17},{1,16},{2,19},{3,18},{4,21},{5,20},{6,23},{7,22},{8,25},{9,... | collective-permute-start | bytes 786440 | tf_op jit(solution)/shard_map/ppermute | solution.py:323
  133.4 13.3 %collective-permute-start.36 = (bf16[2,64,1024]{2,1,0:T(8,128)(2,1)S(1)}, bf16[2,64,1024]{2,1,0:T(8,128)(2,1)S(1)}, u32[]{:S(2)}, u32[]{:S(2)}) collective-permute-start(bf16[2,64,1024]{2,1,0:T(8,128)(2,1)S(1)} %get-tuple-element.225), channel_id=1, source_target_pairs={{0,1},{1,0},{2,3},{3,2},{4,5},{5,4},{6,7},{7,6},{8,9},{9,8},{10,11... | collective-permute-start | bytes 786440 | tf_op jit(solution)/shard_map/ppermute | solution.py:323
  134.9 11.8 %collective-permute-start.37 = (bf16[2,64,1024]{2,1,0:T(8,128)(2,1)S(1)}, bf16[2,64,1024]{2,1,0:T(8,128)(2,1)S(1)}, u32[]{:S(2)}, u32[]{:S(2)}) collective-permute-start(bf16[2,64,1024]{2,1,0:T(8,128)(2,1)S(1)} %get-tuple-element.227), channel_id=1, source_target_pairs={{0,16},{1,17},{2,18},{3,19},{4,20},{5,21},{6,22},{7,23},{8,24},{9,... | collective-permute-start | bytes 786440 | tf_op jit(solution)/shard_map/ppermute | solution.py:323
  135.5 11.6 %collective-permute-start.38 = (bf16[2,64,1024]{2,1,0:T(8,128)(2,1)S(1)}, bf16[2,64,1024]{2,1,0:T(8,128)(2,1)S(1)}, u32[]{:S(2)}, u32[]{:S(2)}) collective-permute-start(bf16[2,64,1024]{2,1,0:T(8,128)(2,1)S(1)} %get-tuple-element.229), channel_id=1, source_target_pairs={{0,17},{1,16},{2,19},{3,18},{4,21},{5,20},{6,23},{7,22},{8,25},{9,... | collective-permute-start | bytes 786440 | tf_op jit(solution)/shard_map/ppermute | solution.py:323
  137.0 9.7 %collective-permute-start.35 = (bf16[2,384,128]{2,1,0:T(8,128)(2,1)S(1)}, bf16[2,384,128]{2,1,0:T(8,128)(2,1)S(1)}, u32[]{:S(2)}, u32[]{:S(2)}) collective-permute-start(bf16[2,384,128]{2,1,0:T(8,128)(2,1)S(1)} %pad_maximum_fusion.5), channel_id=1, source_target_pairs={{0,8},{1,9},{2,10},{3,11},{4,12},{5,13},{6,14},{7,15},{8,0},{9,1},... | collective-permute-start | bytes 589832 | tf_op jit(solution)/shard_map/ppermute | solution.py:323
  139.9 6.9 %collective-permute-start.33 = (bf16[64,1024]{1,0:T(8,128)(2,1)S(1)}, bf16[64,1024]{1,0:T(8,128)(2,1)S(1)}, u32[]{:S(2)}, u32[]{:S(2)}) collective-permute-start(bf16[64,1024]{1,0:T(8,128)(2,1)S(1)} %join_backward.2.g), channel_id=1, source_target_pairs={{0,4},{1,5},{2,6},{3,7},{4,0},{5,1},{6,2},{7,3},{8,12},{9,13},{10,... | collective-permute-start | bytes 393224 | tf_op jit(solution)/shard_map/ppermute | solution.py:323
  147.1 14.3 %collective-permute-start.39 = (bf16[1152,128]{1,0:T(8,128)(2,1)S(1)}, bf16[1152,128]{1,0:T(8,128)(2,1)S(1)}, u32[]{:S(2)}, u32[]{:S(2)}) collective-permute-start(bf16[1152,128]{1,0:T(8,128)(2,1)S(1)} %get-tuple-element.231), channel_id=1, source_target_pairs={{0,8},{1,9},{2,10},{3,11},{4,12},{5,13},{6,14},{7,15},{8,0},{9,1},... | collective-permute-start | bytes 884744 | tf_op jit(solution)/shard_map/ppermute | solution.py:323
  148.8 12.6 %collective-permute-start.42 = (bf16[2,64,1024]{2,1,0:T(8,128)(2,1)S(1)}, bf16[2,64,1024]{2,1,0:T(8,128)(2,1)S(1)}, u32[]{:S(2)}, u32[]{:S(2)}) collective-permute-start(bf16[2,64,1024]{2,1,0:T(8,128)(2,1)S(1)} %pad_maximum_fusion.2.refs_0_), channel_id=1, source_target_pairs={{0,17},{1,16},{2,19},{3,18},{4,21},{5,20},{6,23},{7,22},{8,25},{9,... | collective-permute-start | bytes 786440 | tf_op jit(solution)/shard_map/ppermute | solution.py:323
  150.3 11.1 %collective-permute-start.41 = (bf16[2,64,1024]{2,1,0:T(8,128)(2,1)S(1)}, bf16[2,64,1024]{2,1,0:T(8,128)(2,1)S(1)}, u32[]{:S(2)}, u32[]{:S(2)}) collective-permute-start(bf16[2,64,1024]{2,1,0:T(8,128)(2,1)S(1)} %pad_maximum_fusion.2.refs_0_), channel_id=1, source_target_pairs={{0,16},{1,17},{2,18},{3,19},{4,20},{5,21},{6,22},{7,23},{8,24},{9,... | collective-permute-start | bytes 786440 | tf_op jit(solution)/shard_map/ppermute | solution.py:323
  151.7 9.6 %collective-permute-start.40 = (bf16[2,64,1024]{2,1,0:T(8,128)(2,1)S(1)}, bf16[2,64,1024]{2,1,0:T(8,128)(2,1)S(1)}, u32[]{:S(2)}, u32[]{:S(2)}) collective-permute-start(bf16[2,64,1024]{2,1,0:T(8,128)(2,1)S(1)} %pad_maximum_fusion.2.refs_0_), channel_id=1, source_target_pairs={{0,1},{1,0},{2,3},{3,2},{4,5},{5,4},{6,7},{7,6},{8,9},{9,8},{10,11... | collective-permute-start | bytes 786440 | tf_op jit(solution)/shard_map/ppermute | solution.py:323
  172.9 16.6 %collective-permute-start.45 = (bf16[1152,128]{1,0:T(8,128)(2,1)S(1)}, bf16[1152,128]{1,0:T(8,128)(2,1)S(1)}, u32[]{:S(2)}, u32[]{:S(2)}) collective-permute-start(bf16[1152,128]{1,0:T(8,128)(2,1)S(1)} %get-tuple-element.298), channel_id=1, source_target_pairs={{0,8},{1,9},{2,10},{3,11},{4,12},{5,13},{6,14},{7,15},{8,0},{9,1},... | collective-permute-start | bytes 884744 | tf_op jit(solution)/shard_map/ppermute | solution.py:323
  178.8 10.6 %collective-permute-start.46 = (bf16[2,64,1024]{2,1,0:T(8,128)(2,1)S(1)}, bf16[2,64,1024]{2,1,0:T(8,128)(2,1)S(1)}, u32[]{:S(2)}, u32[]{:S(2)}) collective-permute-start(bf16[2,64,1024]{2,1,0:T(8,128)(2,1)S(1)} %get-tuple-element.253), channel_id=1, source_target_pairs={{0,1},{1,0},{2,3},{3,2},{4,5},{5,4},{6,7},{7,6},{8,9},{9,8},{10,11... | collective-permute-start | bytes 786440 | tf_op jit(solution)/shard_map/ppermute | solution.py:323
  180.3 9.2 %collective-permute-start.47 = (bf16[2,64,1024]{2,1,0:T(8,128)(2,1)S(1)}, bf16[2,64,1024]{2,1,0:T(8,128)(2,1)S(1)}, u32[]{:S(2)}, u32[]{:S(2)}) collective-permute-start(bf16[2,64,1024]{2,1,0:T(8,128)(2,1)S(1)} %get-tuple-element.254), channel_id=1, source_target_pairs={{0,16},{1,17},{2,18},{3,19},{4,20},{5,21},{6,22},{7,23},{8,24},{9,... | collective-permute-start | bytes 786440 | tf_op jit(solution)/shard_map/ppermute | solution.py:323
  180.9 13.1 %collective-permute-start.48 = (bf16[2,64,1024]{2,1,0:T(8,128)(2,1)S(1)}, bf16[2,64,1024]{2,1,0:T(8,128)(2,1)S(1)}, u32[]{:S(2)}, u32[]{:S(2)}) collective-permute-start(bf16[2,64,1024]{2,1,0:T(8,128)(2,1)S(1)} %get-tuple-element.255), channel_id=1, source_target_pairs={{0,17},{1,16},{2,19},{3,18},{4,21},{5,20},{6,23},{7,22},{8,25},{9,... | collective-permute-start | bytes 786440 | tf_op jit(solution)/shard_map/ppermute | solution.py:323
  184.5 28.4 %collective-permute-start.55 = (bf16[2,2,512,128]{3,2,1,0:T(8,128)(2,1)S(1)}, bf16[2,2,512,128]{3,2,1,0:T(8,128)(2,1)S(1)}, u32[]{:S(2)}, u32[]{:S(2)}) collective-permute-start(bf16[2,2,512,128]{3,2,1,0:T(8,128)(2,1)S(1)} %get-tuple-element.270), channel_id=1, source_target_pairs={{0,2},{1,3},{2,0},{3,1},{4,6},{5,7},{6,4},{7,5},{8,10},{9,11},{10,... | collective-permute-start | bytes 1572872 | tf_op jit(solution)/shard_map/ppermute | solution.py:323
  194.7 14.8 %collective-permute-start.49 = (bf16[64,1024]{1,0:T(8,128)(2,1)S(1)}, bf16[64,1024]{1,0:T(8,128)(2,1)S(1)}, u32[]{:S(2)}, u32[]{:S(2)}) collective-permute-start(bf16[64,1024]{1,0:T(8,128)(2,1)S(1)} %get-tuple-element.257), channel_id=1, source_target_pairs={{0,4},{1,5},{2,6},{3,7},{4,0},{5,1},{6,2},{7,3},{8,12},{9,13},{10,... | collective-permute-start | bytes 393224 | tf_op jit(solution)/shard_map/ppermute | solution.py:323
  195.1 13.7 %collective-permute-start.51 = (bf16[64,1024]{1,0:T(8,128)(2,1)S(1)}, bf16[64,1024]{1,0:T(8,128)(2,1)S(1)}, u32[]{:S(2)}, u32[]{:S(2)}) collective-permute-start(bf16[64,1024]{1,0:T(8,128)(2,1)S(1)} %get-tuple-element.262), channel_id=1, source_target_pairs={{0,4},{1,5},{2,6},{3,7},{4,0},{5,1},{6,2},{7,3},{8,12},{9,13},{10,... | collective-permute-start | bytes 393224 | tf_op jit(solution)/shard_map/ppermute | solution.py:323
  196.7 14.6 %collective-permute-start.50 = (bf16[1152,128]{1,0:T(8,128)(2,1)S(1)}, bf16[1152,128]{1,0:T(8,128)(2,1)S(1)}, u32[]{:S(2)}, u32[]{:S(2)}) collective-permute-start(bf16[1152,128]{1,0:T(8,128)(2,1)S(1)} %get-tuple-element.258), channel_id=1, source_target_pairs={{0,8},{1,9},{2,10},{3,11},{4,12},{5,13},{6,14},{7,15},{8,0},{9,1},... | collective-permute-start | bytes 884744 | tf_op jit(solution)/shard_map/ppermute | solution.py:323
  198.1 47.3 %collective-permute-start.63 = (bf16[1152,128]{1,0:T(8,128)(2,1)S(1)}, bf16[1152,128]{1,0:T(8,128)(2,1)S(1)}, u32[]{:S(2)}, u32[]{:S(2)}) collective-permute-start(bf16[1152,128]{1,0:T(8,128)(2,1)S(1)} %get-tuple-element.294), channel_id=1, source_target_pairs={{0,20},{1,21},{2,22},{3,23},{4,16},{5,17},{6,18},{7,19},{8,28},{9,... | collective-permute-start | bytes 884744 | tf_op jit(solution)/shard_map/ppermute | solution.py:323
  213.0 19.2 %collective-permute-start.56 = (bf16[2,512,128]{2,1,0:T(8,128)(2,1)S(1)}, bf16[2,512,128]{2,1,0:T(8,128)(2,1)S(1)}, u32[]{:S(2)}, u32[]{:S(2)}) collective-permute-start(bf16[2,512,128]{2,1,0:T(8,128)(2,1)S(1)} %pad_maximum_fusion.4), channel_id=1, source_target_pairs={{0,8},{1,9},{2,10},{3,11},{4,12},{5,13},{6,14},{7,15},{8,0},{9,1},... | collective-permute-start | bytes 786440 | tf_op jit(solution)/shard_map/ppermute | solution.py:323
  217.4 27.2 %collective-permute-start.53 = (bf16[2,64,1024]{2,1,0:T(8,128)(2,1)S(1)}, bf16[2,64,1024]{2,1,0:T(8,128)(2,1)S(1)}, u32[]{:S(2)}, u32[]{:S(2)}) collective-permute-start(bf16[2,64,1024]{2,1,0:T(8,128)(2,1)S(1)} %pad_maximum_fusion.3), channel_id=1, source_target_pairs={{0,8},{1,9},{2,10},{3,11},{4,12},{5,13},{6,14},{7,15},{8,0},{9,1},... | collective-permute-start | bytes 786440 | tf_op jit(solution)/shard_map/ppermute | solution.py:323
  232.9 7.0 %collective-permute-start.59 = (bf16[448,128]{1,0:T(8,128)(2,1)S(1)}, bf16[448,128]{1,0:T(8,128)(2,1)S(1)}, u32[]{:S(2)}, u32[]{:S(2)}) collective-permute-start(bf16[448,128]{1,0:T(8,128)(2,1)S(1)} %get-tuple-element.314), channel_id=1, source_target_pairs={{0,20},{1,21},{2,22},{3,23},{4,16},{5,17},{6,18},{7,19},{8,28},{9,... | collective-permute-start | bytes 344072 | tf_op jit(solution)/shard_map/ppermute | solution.py:323
  233.0 9.6 %collective-permute-start.58 = (bf16[448,128]{1,0:T(8,128)(2,1)S(1)}, bf16[448,128]{1,0:T(8,128)(2,1)S(1)}, u32[]{:S(2)}, u32[]{:S(2)}) collective-permute-start(bf16[448,128]{1,0:T(8,128)(2,1)S(1)} %get-tuple-element.315), channel_id=1, source_target_pairs={{0,4},{1,5},{2,6},{3,7},{4,0},{5,1},{6,2},{7,3},{8,12},{9,13},{10,... | collective-permute-start | bytes 344072 | tf_op jit(solution)/shard_map/ppermute | solution.py:323
  238.6 7.6 %collective-permute-start.62 = (bf16[1152,128]{1,0:T(8,128)(2,1)S(1)}, bf16[1152,128]{1,0:T(8,128)(2,1)S(1)}, u32[]{:S(2)}, u32[]{:S(2)}) collective-permute-start(bf16[1152,128]{1,0:T(8,128)(2,1)S(1)} %get-tuple-element.295), channel_id=1, source_target_pairs={{0,4},{1,5},{2,6},{3,7},{4,0},{5,1},{6,2},{7,3},{8,12},{9,13},{10,... | collective-permute-start | bytes 884744 | tf_op jit(solution)/shard_map/ppermute | solution.py:323
  240.0 6.7 %collective-permute-start.61 = (bf16[1152,128]{1,0:T(8,128)(2,1)S(1)}, bf16[1152,128]{1,0:T(8,128)(2,1)S(1)}, u32[]{:S(2)}, u32[]{:S(2)}) collective-permute-start(bf16[1152,128]{1,0:T(8,128)(2,1)S(1)} %get-tuple-element.296), channel_id=1, source_target_pairs={{0,16},{1,17},{2,18},{3,19},{4,20},{5,21},{6,22},{7,23},{8,24},{9,... | collective-permute-start | bytes 884744 | tf_op jit(solution)/shard_map/ppermute | solution.py:323
  243.1 6.7 %collective-permute-start.60 = (f32[32,128]{1,0:T(8,128)S(1)}, f32[32,128]{1,0:T(8,128)S(1)}, u32[]{:S(2)}, u32[]{:S(2)}) collective-permute-start(f32[32,128]{1,0:T(8,128)S(1)} %sum_lines.1), channel_id=1, source_target_pairs={{0,1},{1,0},{2,3},{3,2},{4,5},{5,4},{6,7},{7,6},{8,9},{9,8},{10,11... | collective-permute-start | bytes 49160 | tf_op jit(solution)/shard_map/ppermute | solution.py:323
  244.7 7.8 %collective-permute-start.54 = (bf16[3,64,1024]{2,1,0:T(8,128)(2,1)S(1)}, bf16[3,64,1024]{2,1,0:T(8,128)(2,1)S(1)}, u32[]{:S(2)}, u32[]{:S(2)}) collective-permute-start(bf16[3,64,1024]{2,1,0:T(8,128)(2,1)S(1)} %pad_maximum_fusion), channel_id=1, source_target_pairs={{0,1},{1,0},{2,3},{3,2},{4,5},{5,4},{6,7},{7,6},{8,9},{9,8},{10,11... | collective-permute-start | bytes 1179656 | tf_op jit(solution)/shard_map/ppermute | solution.py:323
  (29 other events, 175.8 us)

commit v2 on v1

--- a/solution.py
+++ b/solution.py
@@ -1211,6 +1211,8 @@
         after(sent_down, got_up, *x_parts[4:], first["qkv"], first["rows"]), SECTION
     )
 
+    g_near = swapped(after(g_mine, *x_parts[4:]), NEAR)
+
     def bring_up(*earlier):
         up = up_weights(at, up_weight, got_up, swapped(after(got_up, *earlier), CORE))
         for i, layer in enumerate(layers):
@@ -1233,7 +1235,7 @@
         active, slope = units_forward(at, mlp_in, w)
         mixed, lse = attention_forward(at, q, kv, kv_other)
         if is_start:
-            bring_rows(active, mixed)
+            bring_rows(active, mixed, g_near)
         pieces = outputs_forward(at, mixed, active, w)
         saved = dict(
             attn_in=attn_in, mlp_in=mlp_in, normed=normed, q=q, kv=kv, kv_other=kv_other,
@@ -1241,17 +1243,24 @@
         )
         return pieces, saved, got[5:]
 
-    def backward(loader, sources, saved, w, with_piece):
+    def backward(loader, sources, saved, w, with_piece, grads_first):
         made = units_backward(at, loader, sources, saved["slope"], w, with_piece)
         g, up_grad, mixed_grad = made[:3]
+        if grads_first:
+            early = early_grads(
+                at, saved["active"], saved["mixed"], saved["mlp_in"], up_grad, g
+            )
+            mixed_grad = after(mixed_grad, early[0])
         dq, dkv, dkv_other = attention_backward(
             at, saved["q"], saved["kv"], saved["kv_other"], saved["lse"], mixed_grad
         )
         dkv_got = swapped(dkv_other, CORE)
-        early = early_grads(
-            at, saved["active"], saved["mixed"], saved["mlp_in"], up_grad, after(g, dkv_other)
-        )
-        given = (after(dq, early[0]), dkv, dkv_got, up_grad, saved["normed"], g)
+        if not grads_first:
+            early = early_grads(
+                at, saved["active"], saved["mixed"], saved["mlp_in"], up_grad, after(g, dkv_other)
+            )
+            dq = after(dq, early[0])
+        given = (dq, dkv, dkv_got, up_grad, saved["normed"], g)
         return early, given, made[3:]
 
     def backward_end(given, saved, w):
@@ -1267,14 +1276,14 @@
     piece = join_forward(at, x_piece, [keep, swapped(give, NEAR)], first)
     near = after(swapped(piece, NEAR), *sides)
     middle = gathered(piece, near)
-    g_near = swapped(after(g_mine, near), NEAR)
-    middle[0] = after(middle[0], g_near)
     g_parts = (g_mine, g_near, *strips, *sides)
 
     parts_last, saved_second, blocks = forward(piece_loader, middle, second, False)
     acts_mine, acts_give = blocks
 
-    early, given, (g_piece,) = backward(start_loader, g_parts, saved_second, second, True)
+    early, given, (g_piece,) = backward(
+        start_loader, g_parts, saved_second, second, True, False
+    )
     early_keep, early_give = summed_cores(*early, given[2])
     qkv_grad, table_second, pieces = backward_end(given, saved_second, second)
     late = late_grads(at, saved_second["attn_in"], qkv_grad, ())
@@ -1292,14 +1301,17 @@
     g_middle[0] = after(g_middle[0], close_second)
     keep_last, give_last = fold(at, parts_last)
 
-    early, given, blocks = backward(piece_loader, g_middle, saved_first, first, False)
+    early, given, blocks = backward(
+        piece_loader, g_middle, saved_first, first, False, True
+    )
     in_mine, in_give = blocks
     early_second = [plus(a, b) for a, b in zip(early_keep, (close_second, far_second))]
     late_second = [plus(a, b) for a, b in zip(late_keep, late_got)]
-    early_keep, early_give = summed_cores(*early, given[2])
+    early_keep, early_give = summed_cores(*early)
     given = (after(given[0], *early_give),) + given[1:]
     qkv_grad, table_first, pieces = backward_end(given, saved_first, first)
-    parts = exchanged(pieces)
+    last_near = swapped(give_last, NEAR)
+    parts = exchanged([after(p, last_near) for p in pieces])
     far_first = swapped(early_give[1], HALF)
     late = late_grads(at, saved_first["attn_in"], qkv_grad, (table_first, table_second))
     parts[0] = after(parts[0], far_first)
@@ -1310,7 +1322,7 @@
     back_last = join_backward(
         at, back, x_piece, [keep, after(swapped(give, NEAR), close_first)]
     )
-    last = join_forward(at, piece, [keep_last, swapped(after(give_last, give), NEAR)], second)
+    last = join_forward(at, piece, [keep_last, last_near], second)
     early_first = [plus(a, b) for a, b in zip(early_keep, (close_first, far_first))]
     late_first = [plus(a, b) for a, b in zip(late_keep, late_got)]
     tall = 3 * ONE + LINES
@@ -1325,10 +1337,9 @@
         cross = swapped(jnp.where(is_first, far[1], far[0]), SECTION | NEAR)
         return own, got, near, cross
 
-    early, late = [
-        brought((one[0], two[0]), (one[1], two[1]))
-        for one, two in ((early_first, early_second), (late_first, late_second))
-    ]
+    early = brought((early_first[0], early_second[0]), (early_first[1], early_second[1]))
+    late_first[1] = after(late_first[1], *early)
+    late = brought((late_first[0], late_second[0]), (late_first[1], late_second[1]))
     lines = sum_lines(at, late)
     lines = lines + swapped(lines, SIDE)
     sizes = dict(units=up_weight.shape[2] // 4)

time: 254 us -> 246 us (0.969)
  waiting for transfers between devices: 113 us -> 96.5 us
  starting transfers between devices: 64.8 us -> 72.5 us
    ppermute x64, waiting for transfers between devices: 113 us -> 96.5 us  [swapped(): return lax.ppermute(array, ALL, pairs)]
    ppermute x64, starting transfers between devices: 64.8 us -> 72.5 us  [swapped(): return lax.ppermute(array, ALL, pairs)]
  transfers between devices with their start and end apart: 64 -> 64, of which waited for: 35 -> 31; matrix products, arithmetic and copies ran while one was open for 2% -> 2% of each run, Pallas kernels for 17% -> 18%
where the time goes in v2:
time: 246 us; the launch traced here: 245 us
  waiting for transfers between devices  96.5 us (39%)
  starting transfers between devices  72.5 us (29%)
  Pallas kernels  65.9 us (27%)
  other arithmetic  4.76 us (2%)
  local copies, waits for them, and re-layouts  4.34 us (2%)
    ppermute x64, waiting for transfers between devices, swapped(): return lax.ppermute(array, ALL, pairs)  96.5 us
    ppermute x64, starting transfers between devices, swapped(): return lax.ppermute(array, ALL, pairs)  72.5 us
    pallas_call x32, Pallas kernels, kernel_call(): pl.pallas_call(body, name=name, out_shape=[(pltpu.VMEM if keep else jax.S...  62.1 us
  transfers between devices with their start and end apart: 64, of which 31 were waited for; matrix products, arithmetic and copies ran while one was open for 2% of the time, Pallas kernels for 18%

profile of v2, /device:TPU:0, one launch (start us, length us, event | category | flops | bytes accessed | tf_op | source)
XLA Modules:
  0.0 245.3 jit_solution(14104310781041799504)
XLA Ops:
  0.8 1.8 pack_first.1
  2.6 3.0 %collective-permute-start.5 = (bf16[1584,128]{1,0:T(8,128)(2,1)S(1)}, bf16[1584,128]{1,0:T(8,128)(2,1)S(1)}, u32[]{:S(2)}, u32[]{:S(2)}) collective-permute-start(bf16[1584,128]{1,0:T(8,128)(2,1)S(1)} %get-tuple-element.154), channel_id=1, source_target_pairs={{0,16},{1,17},{2,18},{3,19},{4,20},{5,21},{6,22},{7,23},{8,24},{9,... | collective-permute-start | bytes 1216520 | tf_op jit(solution)/shard_map/ppermute | solution.py:323
  5.6 3.6 %collective-permute-start.2 = (bf16[128,512]{1,0:T(8,128)(2,1)S(1)}, bf16[128,512]{1,0:T(8,128)(2,1)S(1)}, u32[]{:S(2)}, u32[]{:S(2)}) collective-permute-start(bf16[128,512]{1,0:T(8,128)(2,1)S(1)} %get-tuple-element.151), channel_id=1, source_target_pairs={{0,12},{1,13},{2,14},{3,15},{4,8},{5,9},{6,10},{7,11},{8,4},{9,5},... | collective-permute-start | bytes 393224 | tf_op jit(solution)/shard_map/ppermute | solution.py:323
  10.1 2.0 pack_second.1
  12.1 2.9 %collective-permute-done.5.refs_7_.refs_1_ = bf16[1584,128]{1,0:T(8,128)(2,1)S(1)} collective-permute-done((bf16[1584,128]{1,0:T(8,128)(2,1)S(1)}, bf16[1584,128]{1,0:T(8,128)(2,1)S(1)}, u32[]{:S(2)}, u32[]{:S(2)}) %collective-permute-start.5) | collective-permute-done | bytes 405536 | tf_op jit(solution)/shard_map/ppermute | solution.py:323
  17.3 1.8 negate_select_fusion.1
  23.1 2.0 choose_qkv.1
  25.5 2.4 collective-permute-done.3.refs_4_
  29.5 3.0 %front.2 = (bf16[512,1024]{1,0:T(8,128)(2,1)S(1)}, bf16[512,1024]{1,0:T(8,128)(2,1)S(1)}, bf16[512,1024]{1,0:T(8,128)(2,1)S(1)}, bf16[512,128]{1,0:T(8,128)(2,1)...) custom-call(s32[8]{0:T(128)S(1)} %stack.91.at, bf16[128,1024]{1,0:T(8,128)(2,1)S(1)} %get-tuple-element.150.refs_0_, ...), custom_call_target="tpu_custom_call" | custom-call | tf_op jit(solution)/shard_map/front/pallas_call | solution.py:347
  35.0 2.8 %attention_forward.2 = (bf16[512,128]{1,0:T(8,128)(2,1)S(1)}, f32[512,128]{1,0:T(8,128)S(1)}) custom-call(s32[8]{0:T(128)S(1)} %stack.91.at, bf16[512,128]{1,0:T(8,128)(2,1)S(1)} %get-tuple-element.158.q, bf16[2,512,128]{2,1,0:T(8,128)(2,1)S(1)} %get-tuple-element.159.kv, bf16[2,512,128]{2,1,0:T(8,128)(2,1)S(1)} %collective-permute-done.7.kv_other), custom_call_target="tpu_custom_call" | custom-call | tf_op jit(solution)/shard_map/attention_forward/pallas_call | solution.py:347
  38.5 2.1 choose_up.1
  40.7 2.2 units_forward.2
  44.3 2.1 collective-permute-done.12.refs_3_
  47.2 2.3 choose_rows.1
  49.5 1.8 outputs_forward.2
  54.8 3.6 %collective-permute-start.14 = (bf16[128,512]{1,0:T(8,128)(2,1)S(1)}, bf16[128,512]{1,0:T(8,128)(2,1)S(1)}, u32[]{:S(2)}, u32[]{:S(2)}) collective-permute-start(bf16[128,512]{1,0:T(8,128)(2,1)S(1)} %get-tuple-element.176), channel_id=1, source_target_pairs={{0,12},{1,13},{2,14},{3,15},{4,8},{5,9},{6,10},{7,11},{8,4},{9,5},... | collective-permute-start | bytes 393224 | tf_op jit(solution)/shard_map/ppermute | solution.py:323
  58.5 4.5 %collective-permute-done.14.refs_3_ = bf16[128,512]{1,0:T(8,128)(2,1)S(1)} collective-permute-done((bf16[128,512]{1,0:T(8,128)(2,1)S(1)}, bf16[128,512]{1,0:T(8,128)(2,1)S(1)}, u32[]{:S(2)}, u32[]{:S(2)}) %collective-permute-start.14) | collective-permute-done | bytes 131104 | tf_op jit(solution)/shard_map/ppermute | solution.py:323
  62.9 6.1 %collective-permute-done.13.refs_2_ = bf16[128,512]{1,0:T(8,128)(2,1)S(1)} collective-permute-done((bf16[128,512]{1,0:T(8,128)(2,1)S(1)}, bf16[128,512]{1,0:T(8,128)(2,1)S(1)}, u32[]{:S(2)}, u32[]{:S(2)}) %collective-permute-start.13) | collective-permute-done | bytes 131104 | tf_op jit(solution)/shard_map/ppermute | solution.py:323
  71.8 2.9 %collective-permute-done.18.rest_0_ = bf16[64,1024]{1,0:T(8,128)(2,1)S(1)} collective-permute-done((bf16[64,1024]{1,0:T(8,128)(2,1)S(1)}, bf16[64,1024]{1,0:T(8,128)(2,1)S(1)}, u32[]{:S(2)}, u32[]{:S(2)}) %collective-permute-start.18) | collective-permute-done | bytes 131104 | tf_op jit(solution)/shard_map/ppermute | solution.py:323
  77.1 3.2 %collective-permute-done.19 = bf16[64,1024]{1,0:T(8,128)(2,1)S(1)} collective-permute-done((bf16[64,1024]{1,0:T(8,128)(2,1)S(1)}, bf16[64,1024]{1,0:T(8,128)(2,1)S(1)}, u32[]{:S(2)}, u32[]{:S(2)}) %collective-permute-start.19) | collective-permute-done | bytes 131104 | tf_op jit(solution)/shard_map/ppermute | solution.py:323
  83.9 5.4 %collective-permute-done.24.refs_3_ = bf16[2,64,1024]{2,1,0:T(8,128)(2,1)S(1)} collective-permute-done((bf16[2,64,1024]{2,1,0:T(8,128)(2,1)S(1)}, bf16[2,64,1024]{2,1,0:T(8,128)(2,1)S(1)}, u32[]{:S(2)}, u32[]{:S(2)}) %collective-permute-start.24) | collective-permute-done | bytes 262176 | tf_op jit(solution)/shard_map/ppermute | solution.py:323
  89.4 2.9 %collective-permute-done.23.refs_2_ = bf16[2,64,1024]{2,1,0:T(8,128)(2,1)S(1)} collective-permute-done((bf16[2,64,1024]{2,1,0:T(8,128)(2,1)S(1)}, bf16[2,64,1024]{2,1,0:T(8,128)(2,1)S(1)}, u32[]{:S(2)}, u32[]{:S(2)}) %collective-permute-start.23) | collective-permute-done | bytes 262176 | tf_op jit(solution)/shard_map/ppermute | solution.py:323
  92.2 3.1 %front.3 = (bf16[512,1024]{1,0:T(8,128)(2,1)S(1)}, bf16[512,1024]{1,0:T(8,128)(2,1)S(1)}, bf16[512,1024]{1,0:T(8,128)(2,1)S(1)}, bf16[512,128]{1,0:T(8,128)(2,1)...) custom-call(s32[8]{0:T(128)S(1)} %stack.91.at, ...), custom_call_target="tpu_custom_call" | custom-call | tf_op jit(solution)/shard_map/front/pallas_call | solution.py:347
  95.4 2.2 units_forward.3
  97.5 2.0 units_backward.2
  99.6 2.8 %attention_forward.3 = (bf16[512,128]{1,0:T(8,128)(2,1)S(1)}, f32[512,128]{1,0:T(8,128)S(1)}) custom-call(s32[8]{0:T(128)S(1)} %stack.91.at, bf16[512,128]{1,0:T(8,128)(2,1)S(1)} %get-tuple-element.193.q, bf16[2,512,128]{2,1,0:T(8,128)(2,1)S(1)} %get-tuple-element.194.kv, bf16[2,512,128]{2,1,0:T(8,128)(2,1)S(1)} %collective-permute-done.25.kv_other), custom_call_target="tpu_custom_call" | custom-call | tf_op jit(solution)/shard_map/attention_forward/pallas_call | solution.py:347
  102.4 4.0 %attention_backward.2 = (f32[512,128]{1,0:T(8,128)S(1)}, f32[2,512,128]{2,1,0:T(8,128)S(1)}, f32[2,512,128]{2,1,0:T(8,128)S(1)}) custom-call(s32[8]{0:T(128)S(1)} %stack.91.at, bf16[512,128]{1,0:T(8,128)(2,1)S(1)} %get-tuple-element.193.q, bf16[2,512,128]{2,1,0:T(8,128)(2,1)S(1)} %get-tuple-element.194.kv, ...), custom_call_target="tpu_custom_call" | custom-call | tf_op jit(solution)/shard_map/attention_backward/pallas_call | solution.py:347
  106.9 2.1 early_grads.2
  109.2 4.0 %inputs_backward.2 = (bf16[512,384]{1,0:T(8,128)(2,1)S(1)}, bf16[64,128]{1,0:T(8,128)(2,1)S(1)}, f32[2,64,1024]{2,1,0:T(8,128)S(1)}, bf16[2,64,1024]{2,1,0:T(8,1...) custom-call(s32[8]{0:T(128)S(1)} %stack.91.at, ...), custom_call_target="tpu_custom_call" | custom-call | tf_op jit(solution)/shard_map/inputs_backward/pallas_call | solution.py:347
  119.5 1.8 outputs_forward.3
  121.4 9.9 %collective-permute-done.28 = bf16[1152,128]{1,0:T(8,128)(2,1)S(1)} collective-permute-done((bf16[1152,128]{1,0:T(8,128)(2,1)S(1)}, bf16[1152,128]{1,0:T(8,128)(2,1)S(1)}, u32[]{:S(2)}, u32[]{:S(2)}) %collective-permute-start.28) | collective-permute-done | bytes 294944 | tf_op jit(solution)/shard_map/ppermute | solution.py:323
  140.2 6.6 %collective-permute-done.35 = bf16[2,384,128]{2,1,0:T(8,128)(2,1)S(1)} collective-permute-done((bf16[2,384,128]{2,1,0:T(8,128)(2,1)S(1)}, bf16[2,384,128]{2,1,0:T(8,128)(2,1)S(1)}, u32[]{:S(2)}, u32[]{:S(2)}) %collective-permute-start.35) | collective-permute-done | bytes 196640 | tf_op jit(solution)/shard_map/ppermute | solution.py:323
  147.2 2.0 collective-permute-start.39
  152.7 9.1 %collective-permute-done.39 = bf16[1152,128]{1,0:T(8,128)(2,1)S(1)} collective-permute-done((bf16[1152,128]{1,0:T(8,128)(2,1)S(1)}, bf16[1152,128]{1,0:T(8,128)(2,1)S(1)}, u32[]{:S(2)}, u32[]{:S(2)}) %collective-permute-start.39) | collective-permute-done | bytes 294944 | tf_op jit(solution)/shard_map/ppermute | solution.py:323
  162.2 2.1 units_backward.3
  164.3 2.1 early_grads.3
  166.6 4.0 %attention_backward.3 = (f32[512,128]{1,0:T(8,128)S(1)}, f32[2,512,128]{2,1,0:T(8,128)S(1)}, f32[2,512,128]{2,1,0:T(8,128)S(1)}) custom-call(s32[8]{0:T(128)S(1)} %stack.91.at, bf16[512,128]{1,0:T(8,128)(2,1)S(1)} %get-tuple-element.158.q, bf16[2,512,128]{2,1,0:T(8,128)(2,1)S(1)} %get-tuple-element.159.kv, ...), custom_call_target="tpu_custom_call" | custom-call | tf_op jit(solution)/shard_map/attention_backward/pallas_call | solution.py:347
  172.4 2.3 collective-permute-start.46
  174.7 4.0 %inputs_backward.3 = (bf16[512,384]{1,0:T(8,128)(2,1)S(1)}, bf16[64,128]{1,0:T(8,128)(2,1)S(1)}, f32[2,64,1024]{2,1,0:T(8,128)S(1)}, bf16[2,64,1024]{2,1,0:T(8,1...) custom-call(s32[8]{0:T(128)S(1)} %stack.91.at, ...), custom_call_target="tpu_custom_call" | custom-call | tf_op jit(solution)/shard_map/inputs_backward/pallas_call | solution.py:347
  184.8 3.6 %collective-permute-done.46 = bf16[1152,128]{1,0:T(8,128)(2,1)S(1)} collective-permute-done((bf16[1152,128]{1,0:T(8,128)(2,1)S(1)}, bf16[1152,128]{1,0:T(8,128)(2,1)S(1)}, u32[]{:S(2)}, u32[]{:S(2)}) %collective-permute-start.46) | collective-permute-done | bytes 294944 | tf_op jit(solution)/shard_map/ppermute | solution.py:323
  189.4 3.5 %collective-permute-done.48.refs_2_ = bf16[2,64,1024]{2,1,0:T(8,128)(2,1)S(1)} collective-permute-done((bf16[2,64,1024]{2,1,0:T(8,128)(2,1)S(1)}, bf16[2,64,1024]{2,1,0:T(8,128)(2,1)S(1)}, u32[]{:S(2)}, u32[]{:S(2)}) %collective-permute-start.48) | collective-permute-done | bytes 262176 | tf_op jit(solution)/shard_map/ppermute | solution.py:323
  196.4 2.1 collective-permute-start.51
  199.5 12.5 %collective-permute-done.50.rest_0_ = bf16[64,1024]{1,0:T(8,128)(2,1)S(1)} collective-permute-done((bf16[64,1024]{1,0:T(8,128)(2,1)S(1)}, bf16[64,1024]{1,0:T(8,128)(2,1)S(1)}, u32[]{:S(2)}, u32[]{:S(2)}) %collective-permute-start.50) | collective-permute-done | bytes 131104 | tf_op jit(solution)/shard_map/ppermute | solution.py:323
  211.9 4.9 %collective-permute-done.51 = bf16[1152,128]{1,0:T(8,128)(2,1)S(1)} collective-permute-done((bf16[1152,128]{1,0:T(8,128)(2,1)S(1)}, bf16[1152,128]{1,0:T(8,128)(2,1)S(1)}, u32[]{:S(2)}, u32[]{:S(2)}) %collective-permute-start.51) | collective-permute-done | bytes 294944 | tf_op jit(solution)/shard_map/ppermute | solution.py:323
  220.2 4.1 %collective-permute-done.52 = bf16[64,1024]{1,0:T(8,128)(2,1)S(1)} collective-permute-done((bf16[64,1024]{1,0:T(8,128)(2,1)S(1)}, bf16[64,1024]{1,0:T(8,128)(2,1)S(1)}, u32[]{:S(2)}, u32[]{:S(2)}) %collective-permute-start.52) | collective-permute-done | bytes 131104 | tf_op jit(solution)/shard_map/ppermute | solution.py:323
  224.3 3.4 %collective-permute-start.53 = (bf16[2,64,1024]{2,1,0:T(8,128)(2,1)S(1)}, bf16[2,64,1024]{2,1,0:T(8,128)(2,1)S(1)}, u32[]{:S(2)}, u32[]{:S(2)}) collective-permute-start(bf16[2,64,1024]{2,1,0:T(8,128)(2,1)S(1)} %pad_maximum_fusion.3), channel_id=1, source_target_pairs={{0,8},{1,9},{2,10},{3,11},{4,12},{5,13},{6,14},{7,15},{8,0},{9,1},... | collective-permute-start | bytes 786440 | tf_op jit(solution)/shard_map/ppermute | solution.py:323
  229.1 4.2 %collective-permute-start.62 = (bf16[448,128]{1,0:T(8,128)(2,1)S(1)}, bf16[448,128]{1,0:T(8,128)(2,1)S(1)}, u32[]{:S(2)}, u32[]{:S(2)}) collective-permute-start(bf16[448,128]{1,0:T(8,128)(2,1)S(1)} %get-tuple-element.318), channel_id=1, source_target_pairs={{0,20},{1,21},{2,22},{3,23},{4,16},{5,17},{6,18},{7,19},{8,28},{9,... | collective-permute-start | bytes 344072 | tf_op jit(solution)/shard_map/ppermute | solution.py:323
  240.0 2.5 %unpack_grads.1 = (f32[3,128,512]{2,1,0:T(8,128)}, f32[512,128]{1,0:T(8,128)}, f32[128,2048]{1,0:T(8,128)}, f32[2048,128]{1,0:T(8,128)}, f32[3,512]{1,0:T(4,128)...) custom-call(s32[8]{0:T(128)S(1)} %stack.91.at, bf16[1152,128]{1,0:T(8,128)(2,1)S(1)} %get-tuple-element.299.refs_0_, ...), custom_call_target="tpu_custom_call" | custom-call | tf_op jit(solution)/shard_map/unpack_grads/pallas_call | solution.py:347
  (179 shorter events, 74.9 us)
Async XLA Ops:
  2.6 12.4 %collective-permute-start.5 = (bf16[1584,128]{1,0:T(8,128)(2,1)S(1)}, bf16[1584,128]{1,0:T(8,128)(2,1)S(1)}, u32[]{:S(2)}, u32[]{:S(2)}) collective-permute-start(bf16[1584,128]{1,0:T(8,128)(2,1)S(1)} %get-tuple-element.154), channel_id=1, source_target_pairs={{0,16},{1,17},{2,18},{3,19},{4,20},{5,21},{6,22},{7,23},{8,24},{9,... | collective-permute-start | bytes 1216520 | tf_op jit(solution)/shard_map/ppermute | solution.py:323
  5.6 13.5 %collective-permute-start.2 = (bf16[128,512]{1,0:T(8,128)(2,1)S(1)}, bf16[128,512]{1,0:T(8,128)(2,1)S(1)}, u32[]{:S(2)}, u32[]{:S(2)}) collective-permute-start(bf16[128,512]{1,0:T(8,128)(2,1)S(1)} %get-tuple-element.151), channel_id=1, source_target_pairs={{0,12},{1,13},{2,14},{3,15},{4,8},{5,9},{6,10},{7,11},{8,4},{9,5},... | collective-permute-start | bytes 393224 | tf_op jit(solution)/shard_map/ppermute | solution.py:323
  9.2 11.5 %collective-permute-start.1 = (bf16[128,512]{1,0:T(8,128)(2,1)S(1)}, bf16[128,512]{1,0:T(8,128)(2,1)S(1)}, u32[]{:S(2)}, u32[]{:S(2)}) collective-permute-start(bf16[128,512]{1,0:T(8,128)(2,1)S(1)} %get-tuple-element.151), channel_id=1, source_target_pairs={{0,8},{1,9},{2,10},{3,11},{4,12},{5,13},{6,14},{7,15},{8,0},{9,1},... | collective-permute-start | bytes 393224 | tf_op jit(solution)/shard_map/ppermute | solution.py:323
  9.3 20.3 %collective-permute-start = (bf16[128,1024]{1,0:T(8,128)(2,1)S(1)}, bf16[128,1024]{1,0:T(8,128)(2,1)S(1)}, u32[]{:S(2)}, u32[]{:S(2)}) collective-permute-start(bf16[128,1024]{1,0:T(8,128)(2,1)S(1)} %get-tuple-element.150.refs_0_), channel_id=1, source_target_pairs={{0,4},{1,5},{2,6},{3,7},{4,0},{5,1},{6,2},{7,3},{8,12},{9,13},{10,... | collective-permute-start | bytes 786440 | tf_op jit(solution)/shard_map/ppermute | solution.py:323
  15.0 13.1 %collective-permute-start.8 = (bf16[512,512]{1,0:T(8,128)(2,1)S(1)}, bf16[512,512]{1,0:T(8,128)(2,1)S(1)}, u32[]{:S(2)}, u32[]{:S(2)}) collective-permute-start(bf16[512,512]{1,0:T(8,128)(2,1)S(1)} %get-tuple-element.163), channel_id=1, source_target_pairs={{0,16},{1,17},{2,18},{3,19},{4,20},{5,21},{6,22},{7,23},{8,24},{9,... | collective-permute-start | bytes 1572872 | tf_op jit(solution)/shard_map/ppermute | solution.py:323
  19.1 6.4 %collective-permute-start.4 = (bf16[128,512]{1,0:T(8,128)(2,1)S(1)}, bf16[128,512]{1,0:T(8,128)(2,1)S(1)}, u32[]{:S(2)}, u32[]{:S(2)}) collective-permute-start(bf16[128,512]{1,0:T(8,128)(2,1)S(1)} %collective-permute-done.2.refs_3_), channel_id=1, source_target_pairs={{0,1},{1,0},{2,3},{3,2},{4,5},{5,4},{6,7},{7,6},{8,9},{9,8},{10,11... | collective-permute-start | bytes 393224 | tf_op jit(solution)/shard_map/ppermute | solution.py:323
  20.7 7.2 %collective-permute-start.3 = (bf16[128,512]{1,0:T(8,128)(2,1)S(1)}, bf16[128,512]{1,0:T(8,128)(2,1)S(1)}, u32[]{:S(2)}, u32[]{:S(2)}) collective-permute-start(bf16[128,512]{1,0:T(8,128)(2,1)S(1)} %collective-permute-done.1.refs_2_), channel_id=1, source_target_pairs={{0,1},{1,0},{2,3},{3,2},{4,5},{5,4},{6,7},{7,6},{8,9},{9,8},{10,11... | collective-permute-start | bytes 393224 | tf_op jit(solution)/shard_map/ppermute | solution.py:323
  28.1 16.2 %collective-permute-start.10 = (bf16[320,1024]{1,0:T(8,128)(2,1)S(1)}, bf16[320,1024]{1,0:T(8,128)(2,1)S(1)}, u32[]{:S(2)}, u32[]{:S(2)}) collective-permute-start(bf16[320,1024]{1,0:T(8,128)(2,1)S(1)} %get-tuple-element.168), channel_id=1, source_target_pairs={{0,16},{1,17},{2,18},{3,19},{4,20},{5,21},{6,22},{7,23},{8,24},{9,... | collective-permute-start | bytes 1966088 | tf_op jit(solution)/shard_map/ppermute | solution.py:323
  33.2 9.7 %collective-permute-start.11 = (bf16[128,1024]{1,0:T(8,128)(2,1)S(1)}, bf16[128,1024]{1,0:T(8,128)(2,1)S(1)}, u32[]{:S(2)}, u32[]{:S(2)}) collective-permute-start(bf16[128,1024]{1,0:T(8,128)(2,1)S(1)} %get-tuple-element.170.refs_0_), channel_id=1, source_target_pairs={{0,4},{1,5},{2,6},{3,7},{4,0},{5,1},{6,2},{7,3},{8,12},{9,13},{10,... | collective-permute-start | bytes 786440 | tf_op jit(solution)/shard_map/ppermute | solution.py:323
  51.3 17.7 %collective-permute-start.15 = (bf16[2,64,1024]{2,1,0:T(8,128)(2,1)S(1)}, bf16[2,64,1024]{2,1,0:T(8,128)(2,1)S(1)}, u32[]{:S(2)}, u32[]{:S(2)}) collective-permute-start(bf16[2,64,1024]{2,1,0:T(8,128)(2,1)S(1)} %get-tuple-element.178), channel_id=1, source_target_pairs={{0,1},{1,0},{2,3},{3,2},{4,5},{5,4},{6,7},{7,6},{8,9},{9,8},{10,11... | collective-permute-start | bytes 786440 | tf_op jit(solution)/shard_map/ppermute | solution.py:323
  52.9 16.1 %collective-permute-start.16 = (bf16[2,64,1024]{2,1,0:T(8,128)(2,1)S(1)}, bf16[2,64,1024]{2,1,0:T(8,128)(2,1)S(1)}, u32[]{:S(2)}, u32[]{:S(2)}) collective-permute-start(bf16[2,64,1024]{2,1,0:T(8,128)(2,1)S(1)} %get-tuple-element.179), channel_id=1, source_target_pairs={{0,16},{1,17},{2,18},{3,19},{4,20},{5,21},{6,22},{7,23},{8,24},{9,... | collective-permute-start | bytes 786440 | tf_op jit(solution)/shard_map/ppermute | solution.py:323
  53.4 15.6 %collective-permute-start.17 = (bf16[2,64,1024]{2,1,0:T(8,128)(2,1)S(1)}, bf16[2,64,1024]{2,1,0:T(8,128)(2,1)S(1)}, u32[]{:S(2)}, u32[]{:S(2)}) collective-permute-start(bf16[2,64,1024]{2,1,0:T(8,128)(2,1)S(1)} %get-tuple-element.180), channel_id=1, source_target_pairs={{0,17},{1,16},{2,19},{3,18},{4,21},{5,20},{6,23},{7,22},{8,25},{9,... | collective-permute-start | bytes 786440 | tf_op jit(solution)/shard_map/ppermute | solution.py:323
  54.8 8.1 %collective-permute-start.14 = (bf16[128,512]{1,0:T(8,128)(2,1)S(1)}, bf16[128,512]{1,0:T(8,128)(2,1)S(1)}, u32[]{:S(2)}, u32[]{:S(2)}) collective-permute-start(bf16[128,512]{1,0:T(8,128)(2,1)S(1)} %get-tuple-element.176), channel_id=1, source_target_pairs={{0,12},{1,13},{2,14},{3,15},{4,8},{5,9},{6,10},{7,11},{8,4},{9,5},... | collective-permute-start | bytes 393224 | tf_op jit(solution)/shard_map/ppermute | solution.py:323
  58.5 10.5 %collective-permute-start.13 = (bf16[128,512]{1,0:T(8,128)(2,1)S(1)}, bf16[128,512]{1,0:T(8,128)(2,1)S(1)}, u32[]{:S(2)}, u32[]{:S(2)}) collective-permute-start(bf16[128,512]{1,0:T(8,128)(2,1)S(1)} %get-tuple-element.176), channel_id=1, source_target_pairs={{0,8},{1,9},{2,10},{3,11},{4,12},{5,13},{6,14},{7,15},{8,0},{9,1},... | collective-permute-start | bytes 393224 | tf_op jit(solution)/shard_map/ppermute | solution.py:323
  80.4 9.0 %collective-permute-start.24 = (bf16[2,64,1024]{2,1,0:T(8,128)(2,1)S(1)}, bf16[2,64,1024]{2,1,0:T(8,128)(2,1)S(1)}, u32[]{:S(2)}, u32[]{:S(2)}) collective-permute-start(bf16[2,64,1024]{2,1,0:T(8,128)(2,1)S(1)} %pad_maximum_fusion.1.refs_0_), channel_id=1, source_target_pairs={{0,17},{1,16},{2,19},{3,18},{4,21},{5,20},{6,23},{7,22},{8,25},{9,... | collective-permute-start | bytes 786440 | tf_op jit(solution)/shard_map/ppermute | solution.py:323
  81.9 10.3 %collective-permute-start.23 = (bf16[2,64,1024]{2,1,0:T(8,128)(2,1)S(1)}, bf16[2,64,1024]{2,1,0:T(8,128)(2,1)S(1)}, u32[]{:S(2)}, u32[]{:S(2)}) collective-permute-start(bf16[2,64,1024]{2,1,0:T(8,128)(2,1)S(1)} %pad_maximum_fusion.1.refs_0_), channel_id=1, source_target_pairs={{0,16},{1,17},{2,18},{3,19},{4,20},{5,21},{6,22},{7,23},{8,24},{9,... | collective-permute-start | bytes 786440 | tf_op jit(solution)/shard_map/ppermute | solution.py:323
  83.4 8.8 %collective-permute-start.22 = (bf16[2,64,1024]{2,1,0:T(8,128)(2,1)S(1)}, bf16[2,64,1024]{2,1,0:T(8,128)(2,1)S(1)}, u32[]{:S(2)}, u32[]{:S(2)}) collective-permute-start(bf16[2,64,1024]{2,1,0:T(8,128)(2,1)S(1)} %pad_maximum_fusion.1.refs_0_), channel_id=1, source_target_pairs={{0,1},{1,0},{2,3},{3,2},{4,5},{5,4},{6,7},{7,6},{8,9},{9,8},{10,11... | collective-permute-start | bytes 786440 | tf_op jit(solution)/shard_map/ppermute | solution.py:323
  114.5 6.8 %collective-permute-start.34 = (bf16[2,2,384,128]{3,2,1,0:T(8,128)(2,1)S(1)}, bf16[2,2,384,128]{3,2,1,0:T(8,128)(2,1)S(1)}, u32[]{:S(2)}, u32[]{:S(2)}) collective-permute-start(bf16[2,2,384,128]{3,2,1,0:T(8,128)(2,1)S(1)} %get-tuple-element.214), channel_id=1, source_target_pairs={{0,2},{1,3},{2,0},{3,1},{4,6},{5,7},{6,4},{7,5},{8,10},{9,11},{10,... | collective-permute-start | bytes 1179656 | tf_op jit(solution)/shard_map/ppermute | solution.py:323
  115.2 16.1 %collective-permute-start.28 = (bf16[1152,128]{1,0:T(8,128)(2,1)S(1)}, bf16[1152,128]{1,0:T(8,128)(2,1)S(1)}, u32[]{:S(2)}, u32[]{:S(2)}) collective-permute-start(bf16[1152,128]{1,0:T(8,128)(2,1)S(1)} %get-tuple-element.303), channel_id=1, source_target_pairs={{0,8},{1,9},{2,10},{3,11},{4,12},{5,13},{6,14},{7,15},{8,0},{9,1},... | collective-permute-start | bytes 884744 | tf_op jit(solution)/shard_map/ppermute | solution.py:323
  116.0 15.3 %collective-permute-start.29 = (bf16[2,64,1024]{2,1,0:T(8,128)(2,1)S(1)}, bf16[2,64,1024]{2,1,0:T(8,128)(2,1)S(1)}, u32[]{:S(2)}, u32[]{:S(2)}) collective-permute-start(bf16[2,64,1024]{2,1,0:T(8,128)(2,1)S(1)} %get-tuple-element.216), channel_id=1, source_target_pairs={{0,1},{1,0},{2,3},{3,2},{4,5},{5,4},{6,7},{7,6},{8,9},{9,8},{10,11... | collective-permute-start | bytes 786440 | tf_op jit(solution)/shard_map/ppermute | solution.py:323
  117.4 13.9 %collective-permute-start.30 = (bf16[2,64,1024]{2,1,0:T(8,128)(2,1)S(1)}, bf16[2,64,1024]{2,1,0:T(8,128)(2,1)S(1)}, u32[]{:S(2)}, u32[]{:S(2)}) collective-permute-start(bf16[2,64,1024]{2,1,0:T(8,128)(2,1)S(1)} %get-tuple-element.217), channel_id=1, source_target_pairs={{0,16},{1,17},{2,18},{3,19},{4,20},{5,21},{6,22},{7,23},{8,24},{9,... | collective-permute-start | bytes 786440 | tf_op jit(solution)/shard_map/ppermute | solution.py:323
  118.0 13.4 %collective-permute-start.31 = (bf16[2,64,1024]{2,1,0:T(8,128)(2,1)S(1)}, bf16[2,64,1024]{2,1,0:T(8,128)(2,1)S(1)}, u32[]{:S(2)}, u32[]{:S(2)}) collective-permute-start(bf16[2,64,1024]{2,1,0:T(8,128)(2,1)S(1)} %get-tuple-element.218), channel_id=1, source_target_pairs={{0,17},{1,16},{2,19},{3,18},{4,21},{5,20},{6,23},{7,22},{8,25},{9,... | collective-permute-start | bytes 786440 | tf_op jit(solution)/shard_map/ppermute | solution.py:323
  133.1 13.7 %collective-permute-start.36 = (bf16[2,64,1024]{2,1,0:T(8,128)(2,1)S(1)}, bf16[2,64,1024]{2,1,0:T(8,128)(2,1)S(1)}, u32[]{:S(2)}, u32[]{:S(2)}) collective-permute-start(bf16[2,64,1024]{2,1,0:T(8,128)(2,1)S(1)} %get-tuple-element.225), channel_id=1, source_target_pairs={{0,1},{1,0},{2,3},{3,2},{4,5},{5,4},{6,7},{7,6},{8,9},{9,8},{10,11... | collective-permute-start | bytes 786440 | tf_op jit(solution)/shard_map/ppermute | solution.py:323
  134.4 12.4 %collective-permute-start.37 = (bf16[2,64,1024]{2,1,0:T(8,128)(2,1)S(1)}, bf16[2,64,1024]{2,1,0:T(8,128)(2,1)S(1)}, u32[]{:S(2)}, u32[]{:S(2)}) collective-permute-start(bf16[2,64,1024]{2,1,0:T(8,128)(2,1)S(1)} %get-tuple-element.227), channel_id=1, source_target_pairs={{0,16},{1,17},{2,18},{3,19},{4,20},{5,21},{6,22},{7,23},{8,24},{9,... | collective-permute-start | bytes 786440 | tf_op jit(solution)/shard_map/ppermute | solution.py:323
  135.0 12.2 %collective-permute-start.38 = (bf16[2,64,1024]{2,1,0:T(8,128)(2,1)S(1)}, bf16[2,64,1024]{2,1,0:T(8,128)(2,1)S(1)}, u32[]{:S(2)}, u32[]{:S(2)}) collective-permute-start(bf16[2,64,1024]{2,1,0:T(8,128)(2,1)S(1)} %get-tuple-element.229), channel_id=1, source_target_pairs={{0,17},{1,16},{2,19},{3,18},{4,21},{5,20},{6,23},{7,22},{8,25},{9,... | collective-permute-start | bytes 786440 | tf_op jit(solution)/shard_map/ppermute | solution.py:323
  136.6 10.2 %collective-permute-start.35 = (bf16[2,384,128]{2,1,0:T(8,128)(2,1)S(1)}, bf16[2,384,128]{2,1,0:T(8,128)(2,1)S(1)}, u32[]{:S(2)}, u32[]{:S(2)}) collective-permute-start(bf16[2,384,128]{2,1,0:T(8,128)(2,1)S(1)} %pad_maximum_fusion.5), channel_id=1, source_target_pairs={{0,8},{1,9},{2,10},{3,11},{4,12},{5,13},{6,14},{7,15},{8,0},{9,1},... | collective-permute-start | bytes 589832 | tf_op jit(solution)/shard_map/ppermute | solution.py:323
  138.8 8.0 %collective-permute-start.33 = (bf16[64,1024]{1,0:T(8,128)(2,1)S(1)}, bf16[64,1024]{1,0:T(8,128)(2,1)S(1)}, u32[]{:S(2)}, u32[]{:S(2)}) collective-permute-start(bf16[64,1024]{1,0:T(8,128)(2,1)S(1)} %join_backward.2.g), channel_id=1, source_target_pairs={{0,4},{1,5},{2,6},{3,7},{4,0},{5,1},{6,2},{7,3},{8,12},{9,13},{10,... | collective-permute-start | bytes 393224 | tf_op jit(solution)/shard_map/ppermute | solution.py:323
  147.2 14.7 %collective-permute-start.39 = (bf16[1152,128]{1,0:T(8,128)(2,1)S(1)}, bf16[1152,128]{1,0:T(8,128)(2,1)S(1)}, u32[]{:S(2)}, u32[]{:S(2)}) collective-permute-start(bf16[1152,128]{1,0:T(8,128)(2,1)S(1)} %get-tuple-element.231), channel_id=1, source_target_pairs={{0,8},{1,9},{2,10},{3,11},{4,12},{5,13},{6,14},{7,15},{8,0},{9,1},... | collective-permute-start | bytes 884744 | tf_op jit(solution)/shard_map/ppermute | solution.py:323
  149.2 12.7 %collective-permute-start.42 = (bf16[2,64,1024]{2,1,0:T(8,128)(2,1)S(1)}, bf16[2,64,1024]{2,1,0:T(8,128)(2,1)S(1)}, u32[]{:S(2)}, u32[]{:S(2)}) collective-permute-start(bf16[2,64,1024]{2,1,0:T(8,128)(2,1)S(1)} %pad_maximum_fusion.2.refs_0_), channel_id=1, source_target_pairs={{0,17},{1,16},{2,19},{3,18},{4,21},{5,20},{6,23},{7,22},{8,25},{9,... | collective-permute-start | bytes 786440 | tf_op jit(solution)/shard_map/ppermute | solution.py:323
  150.6 11.6 %collective-permute-start.41 = (bf16[2,64,1024]{2,1,0:T(8,128)(2,1)S(1)}, bf16[2,64,1024]{2,1,0:T(8,128)(2,1)S(1)}, u32[]{:S(2)}, u32[]{:S(2)}) collective-permute-start(bf16[2,64,1024]{2,1,0:T(8,128)(2,1)S(1)} %pad_maximum_fusion.2.refs_0_), channel_id=1, source_target_pairs={{0,16},{1,17},{2,18},{3,19},{4,20},{5,21},{6,22},{7,23},{8,24},{9,... | collective-permute-start | bytes 786440 | tf_op jit(solution)/shard_map/ppermute | solution.py:323
  152.1 10.2 %collective-permute-start.40 = (bf16[2,64,1024]{2,1,0:T(8,128)(2,1)S(1)}, bf16[2,64,1024]{2,1,0:T(8,128)(2,1)S(1)}, u32[]{:S(2)}, u32[]{:S(2)}) collective-permute-start(bf16[2,64,1024]{2,1,0:T(8,128)(2,1)S(1)} %pad_maximum_fusion.2.refs_0_), channel_id=1, source_target_pairs={{0,1},{1,0},{2,3},{3,2},{4,5},{5,4},{6,7},{7,6},{8,9},{9,8},{10,11... | collective-permute-start | bytes 786440 | tf_op jit(solution)/shard_map/ppermute | solution.py:323
  171.8 7.4 %collective-permute-start.45 = (bf16[64,1024]{1,0:T(8,128)(2,1)S(1)}, bf16[64,1024]{1,0:T(8,128)(2,1)S(1)}, u32[]{:S(2)}, u32[]{:S(2)}) collective-permute-start(bf16[64,1024]{1,0:T(8,128)(2,1)S(1)} %get-tuple-element.250), channel_id=1, source_target_pairs={{0,4},{1,5},{2,6},{3,7},{4,0},{5,1},{6,2},{7,3},{8,12},{9,13},{10,... | collective-permute-start | bytes 393224 | tf_op jit(solution)/shard_map/ppermute | solution.py:323
  172.4 16.0 %collective-permute-start.46 = (bf16[1152,128]{1,0:T(8,128)(2,1)S(1)}, bf16[1152,128]{1,0:T(8,128)(2,1)S(1)}, u32[]{:S(2)}, u32[]{:S(2)}) collective-permute-start(bf16[1152,128]{1,0:T(8,128)(2,1)S(1)} %get-tuple-element.300), channel_id=1, source_target_pairs={{0,8},{1,9},{2,10},{3,11},{4,12},{5,13},{6,14},{7,15},{8,0},{9,1},... | collective-permute-start | bytes 884744 | tf_op jit(solution)/shard_map/ppermute | solution.py:323
  179.2 10.2 %collective-permute-start.49 = (bf16[2,64,1024]{2,1,0:T(8,128)(2,1)S(1)}, bf16[2,64,1024]{2,1,0:T(8,128)(2,1)S(1)}, u32[]{:S(2)}, u32[]{:S(2)}) collective-permute-start(bf16[2,64,1024]{2,1,0:T(8,128)(2,1)S(1)} %get-tuple-element.258), channel_id=1, source_target_pairs={{0,17},{1,16},{2,19},{3,18},{4,21},{5,20},{6,23},{7,22},{8,25},{9,... | collective-permute-start | bytes 786440 | tf_op jit(solution)/shard_map/ppermute | solution.py:323
  180.6 12.3 %collective-permute-start.48 = (bf16[2,64,1024]{2,1,0:T(8,128)(2,1)S(1)}, bf16[2,64,1024]{2,1,0:T(8,128)(2,1)S(1)}, u32[]{:S(2)}, u32[]{:S(2)}) collective-permute-start(bf16[2,64,1024]{2,1,0:T(8,128)(2,1)S(1)} %get-tuple-element.256), channel_id=1, source_target_pairs={{0,16},{1,17},{2,18},{3,19},{4,20},{5,21},{6,22},{7,23},{8,24},{9,... | collective-permute-start | bytes 786440 | tf_op jit(solution)/shard_map/ppermute | solution.py:323
  182.2 10.8 %collective-permute-start.47 = (bf16[2,64,1024]{2,1,0:T(8,128)(2,1)S(1)}, bf16[2,64,1024]{2,1,0:T(8,128)(2,1)S(1)}, u32[]{:S(2)}, u32[]{:S(2)}) collective-permute-start(bf16[2,64,1024]{2,1,0:T(8,128)(2,1)S(1)} %get-tuple-element.254), channel_id=1, source_target_pairs={{0,1},{1,0},{2,3},{3,2},{4,5},{5,4},{6,7},{7,6},{8,9},{9,8},{10,11... | collective-permute-start | bytes 786440 | tf_op jit(solution)/shard_map/ppermute | solution.py:323
  184.7 13.8 %collective-permute-start.55 = (bf16[2,2,512,128]{3,2,1,0:T(8,128)(2,1)S(1)}, bf16[2,2,512,128]{3,2,1,0:T(8,128)(2,1)S(1)}, u32[]{:S(2)}, u32[]{:S(2)}) collective-permute-start(bf16[2,2,512,128]{3,2,1,0:T(8,128)(2,1)S(1)} %get-tuple-element.271), channel_id=1, source_target_pairs={{0,2},{1,3},{2,0},{3,1},{4,6},{5,7},{6,4},{7,5},{8,10},{9,11},{10,... | collective-permute-start | bytes 1572872 | tf_op jit(solution)/shard_map/ppermute | solution.py:323
  193.6 18.4 %collective-permute-start.50 = (bf16[64,1024]{1,0:T(8,128)(2,1)S(1)}, bf16[64,1024]{1,0:T(8,128)(2,1)S(1)}, u32[]{:S(2)}, u32[]{:S(2)}) collective-permute-start(bf16[64,1024]{1,0:T(8,128)(2,1)S(1)} %get-tuple-element.260), channel_id=1, source_target_pairs={{0,4},{1,5},{2,6},{3,7},{4,0},{5,1},{6,2},{7,3},{8,12},{9,13},{10,... | collective-permute-start | bytes 393224 | tf_op jit(solution)/shard_map/ppermute | solution.py:323
  194.3 34.4 %collective-permute-start.60 = (bf16[1152,128]{1,0:T(8,128)(2,1)S(1)}, bf16[1152,128]{1,0:T(8,128)(2,1)S(1)}, u32[]{:S(2)}, u32[]{:S(2)}) collective-permute-start(bf16[1152,128]{1,0:T(8,128)(2,1)S(1)} %get-tuple-element.296), channel_id=1, source_target_pairs={{0,20},{1,21},{2,22},{3,23},{4,16},{5,17},{6,18},{7,19},{8,28},{9,... | collective-permute-start | bytes 884744 | tf_op jit(solution)/shard_map/ppermute | solution.py:323
  196.0 32.7 %collective-permute-start.59 = (bf16[1152,128]{1,0:T(8,128)(2,1)S(1)}, bf16[1152,128]{1,0:T(8,128)(2,1)S(1)}, u32[]{:S(2)}, u32[]{:S(2)}) collective-permute-start(bf16[1152,128]{1,0:T(8,128)(2,1)S(1)} %get-tuple-element.297), channel_id=1, source_target_pairs={{0,4},{1,5},{2,6},{3,7},{4,0},{5,1},{6,2},{7,3},{8,12},{9,13},{10,... | collective-permute-start | bytes 884744 | tf_op jit(solution)/shard_map/ppermute | solution.py:323
  196.4 20.5 %collective-permute-start.51 = (bf16[1152,128]{1,0:T(8,128)(2,1)S(1)}, bf16[1152,128]{1,0:T(8,128)(2,1)S(1)}, u32[]{:S(2)}, u32[]{:S(2)}) collective-permute-start(bf16[1152,128]{1,0:T(8,128)(2,1)S(1)} %get-tuple-element.261), channel_id=1, source_target_pairs={{0,8},{1,9},{2,10},{3,11},{4,12},{5,13},{6,14},{7,15},{8,0},{9,1},... | collective-permute-start | bytes 884744 | tf_op jit(solution)/shard_map/ppermute | solution.py:323
  198.6 29.2 %collective-permute-start.56 = (bf16[2,512,128]{2,1,0:T(8,128)(2,1)S(1)}, bf16[2,512,128]{2,1,0:T(8,128)(2,1)S(1)}, u32[]{:S(2)}, u32[]{:S(2)}) collective-permute-start(bf16[2,512,128]{2,1,0:T(8,128)(2,1)S(1)} %pad_maximum_fusion.4), channel_id=1, source_target_pairs={{0,8},{1,9},{2,10},{3,11},{4,12},{5,13},{6,14},{7,15},{8,0},{9,1},... | collective-permute-start | bytes 786440 | tf_op jit(solution)/shard_map/ppermute | solution.py:323
  217.7 6.5 %collective-permute-start.52 = (bf16[64,1024]{1,0:T(8,128)(2,1)S(1)}, bf16[64,1024]{1,0:T(8,128)(2,1)S(1)}, u32[]{:S(2)}, u32[]{:S(2)}) collective-permute-start(bf16[64,1024]{1,0:T(8,128)(2,1)S(1)} %broadcast_select_fusion.4), channel_id=1, source_target_pairs={{0,16},{1,17},{2,18},{3,19},{4,20},{5,21},{6,22},{7,23},{8,24},{9,... | collective-permute-start | bytes 393224 | tf_op jit(solution)/shard_map/ppermute | solution.py:323
  218.8 10.2 %collective-permute-start.58 = (bf16[1152,128]{1,0:T(8,128)(2,1)S(1)}, bf16[1152,128]{1,0:T(8,128)(2,1)S(1)}, u32[]{:S(2)}, u32[]{:S(2)}) collective-permute-start(bf16[1152,128]{1,0:T(8,128)(2,1)S(1)} %get-tuple-element.298), channel_id=1, source_target_pairs={{0,16},{1,17},{2,18},{3,19},{4,20},{5,21},{6,22},{7,23},{8,24},{9,... | collective-permute-start | bytes 884744 | tf_op jit(solution)/shard_map/ppermute | solution.py:323
  224.3 10.7 %collective-permute-start.53 = (bf16[2,64,1024]{2,1,0:T(8,128)(2,1)S(1)}, bf16[2,64,1024]{2,1,0:T(8,128)(2,1)S(1)}, u32[]{:S(2)}, u32[]{:S(2)}) collective-permute-start(bf16[2,64,1024]{2,1,0:T(8,128)(2,1)S(1)} %pad_maximum_fusion.3), channel_id=1, source_target_pairs={{0,8},{1,9},{2,10},{3,11},{4,12},{5,13},{6,14},{7,15},{8,0},{9,1},... | collective-permute-start | bytes 786440 | tf_op jit(solution)/shard_map/ppermute | solution.py:323
  228.0 8.6 %collective-permute-start.57 = (bf16[448,128]{1,0:T(8,128)(2,1)S(1)}, bf16[448,128]{1,0:T(8,128)(2,1)S(1)}, u32[]{:S(2)}, u32[]{:S(2)}) collective-permute-start(bf16[448,128]{1,0:T(8,128)(2,1)S(1)} %get-tuple-element.316), channel_id=1, source_target_pairs={{0,16},{1,17},{2,18},{3,19},{4,20},{5,21},{6,22},{7,23},{8,24},{9,... | collective-permute-start | bytes 344072 | tf_op jit(solution)/shard_map/ppermute | solution.py:323
  229.1 7.5 %collective-permute-start.62 = (bf16[448,128]{1,0:T(8,128)(2,1)S(1)}, bf16[448,128]{1,0:T(8,128)(2,1)S(1)}, u32[]{:S(2)}, u32[]{:S(2)}) collective-permute-start(bf16[448,128]{1,0:T(8,128)(2,1)S(1)} %get-tuple-element.318), channel_id=1, source_target_pairs={{0,20},{1,21},{2,22},{3,23},{4,16},{5,17},{6,18},{7,19},{8,28},{9,... | collective-permute-start | bytes 344072 | tf_op jit(solution)/shard_map/ppermute | solution.py:323
  235.1 8.8 %collective-permute-start.54 = (bf16[3,64,1024]{2,1,0:T(8,128)(2,1)S(1)}, bf16[3,64,1024]{2,1,0:T(8,128)(2,1)S(1)}, u32[]{:S(2)}, u32[]{:S(2)}) collective-permute-start(bf16[3,64,1024]{2,1,0:T(8,128)(2,1)S(1)} %pad_maximum_fusion), channel_id=1, source_target_pairs={{0,1},{1,0},{2,3},{3,2},{4,5},{5,4},{6,7},{7,6},{8,9},{9,8},{10,11... | collective-permute-start | bytes 1179656 | tf_op jit(solution)/shard_map/ppermute | solution.py:323
  (29 other events, 178.3 us)

commit v3 on v2

--- a/solution.py
+++ b/solution.py
@@ -341,7 +341,7 @@
     return [pltpu.with_memory_space_constraint(a, pltpu.HBM) for a in arrays]
 
 
-def kernel_call(body, outs, at, *arrays, hbm=(), scratch=(), flops=0, exps=0, name=None, keep=True):
+def kernel_call(body, outs, at, *arrays, hbm=(), free=(), scratch=(), flops=0, exps=0, name=None, keep=True):
     moved = sum(a.size * a.dtype.itemsize for a in arrays)
     moved += sum(math.prod(s) * jnp.dtype(d).itemsize for s, d in outs)
     return pl.pallas_call(
@@ -350,12 +350,13 @@
         out_shape=[(pltpu.VMEM if keep else jax.ShapeDtypeStruct)(s, d) for s, d in outs],
         in_specs=[pl.BlockSpec(memory_space=pltpu.SMEM)]
         + [pl.BlockSpec(memory_space=pltpu.VMEM)] * len(arrays)
-        + [pl.BlockSpec(memory_space=pltpu.HBM)] * len(hbm),
+        + [pl.BlockSpec(memory_space=pltpu.HBM)] * len(hbm)
+        + [pl.BlockSpec(memory_space=pl.ANY)] * len(free),
         out_specs=[pl.BlockSpec(memory_space=pltpu.VMEM)] * len(outs),
         scratch_shapes=list(scratch),
         compiler_params=pltpu.CompilerParams(vmem_limit_bytes=VMEM_BYTES),
         cost_estimate=pl.CostEstimate(flops=0, bytes_accessed=0, transcendentals=0),
-    )(at, *arrays, *in_hbm(hbm))
+    )(at, *arrays, *in_hbm(hbm), *free)
 
 
 VMEM_BYTES = 12 * 1024 * 1024
@@ -620,7 +621,7 @@
 
     outs = [(shape, B16) for shape in shapes for _ in range(2)]
     return kernel_call(
-        body, outs, at, hbm=[*owns, got, rest],
+        body, outs, at, hbm=owns, free=[got, rest],
         scratch=[pltpu.SemaphoreType.DMA((9,))], name=name,
     )
 
@@ -737,8 +738,8 @@
                 target[span] = flat.astype(B16)
             kv[1, span] = projected[:, 2 * ONE :].astype(B16)
 
-        by_rows(rows, 128, norm)
-        by_rows(rows, 256, project)
+        by_rows(rows, 256, norm)
+        by_rows(rows, rows, project)
 
     outs = [((rows, dim), B16)] * 3 + [((rows, ONE), B16), ((2, rows, ONE), B16)]
     outs += [((rows // 8, dim), B16)] if with_piece else [((n, dim), B16) for n in (ONE, ONE // 2)]
@@ -763,7 +764,7 @@
             active[span] = (value * cdf).astype(B16)
             slope[span] = (cdf + value * pdf).astype(B16)
 
-        by_rows(rows, 128, gelu)
+        by_rows(rows, rows, gelu)
 
     return weights_call(
         "units_forward", body, [((rows, units), B16)] * 2, at, [mlp_in, w["rows"]], [w["up"]],
@@ -775,9 +776,22 @@
     return lax.broadcasted_iota(jnp.int32, (1, ONE), 1) < HD
 
 
+def by_head(array):
+    first_head = head_lanes()
+    zero = jnp.zeros_like(array)
+    return jnp.concatenate(
+        [jnp.where(first_head, array, zero), jnp.where(first_head, zero, array)], axis=0
+    )
+
+
+def joined_heads(array):
+    half = array.shape[0] // 2
+    return jnp.where(head_lanes(), array[:half], array[half:])
+
+
 def allowed_keys(at, first, step, count):
-    row = lax.broadcasted_iota(jnp.int32, (step, count), 0) + first
-    column = lax.broadcasted_iota(jnp.int32, (step, count), 1)
+    row = lax.broadcasted_iota(jnp.int32, (2 * step, count), 0) % step + first
+    column = lax.broadcasted_iota(jnp.int32, (2 * step, count), 1)
     return column <= row, column < (row // ONE + at[S_CORE]) * ONE
 
 
@@ -825,37 +839,31 @@
     scale = 1.0 / math.sqrt(HD)
 
     def body(at, q, kv, kv_other, mixed, lse):
-        first_head = head_lanes()
         step = 256
         for first in range(0, rows, step):
             span = slice(first, first + step)
             count = first + step
-            queries = q[span]
-            masks = allowed_keys(at, first, step, count)
-            results, totals = [], []
-            for head in range(2):
-                lanes = first_head if head == 0 else jnp.logical_not(first_head)
-                one = jnp.where(lanes, queries, jnp.zeros_like(queries))
-                scores = [
-                    jnp.where(mask, nt(one, keys[0, :count]) * scale, -1e9)
-                    for mask, keys in zip(masks, (kv, kv_other))
-                ]
-                most = jnp.maximum(
-                    jnp.max(scores[0], axis=1, keepdims=True),
-                    jnp.max(scores[1], axis=1, keepdims=True),
-                )
-                exponents = [jnp.exp(s - most) for s in scores]
-                summed = jnp.sum(exponents[0], axis=1, keepdims=True) + jnp.sum(
-                    exponents[1], axis=1, keepdims=True
-                )
-                inverse = 1.0 / summed
-                results.append(
-                    nn((exponents[0] * inverse).astype(B16), kv[1, :count])
-                    + nn((exponents[1] * inverse).astype(B16), kv_other[1, :count])
-                )
-                totals.append(most + jnp.log(summed))
-            mixed[span] = jnp.where(first_head, results[0], results[1]).astype(B16)
-            lse[span] = jnp.where(first_head, totals[0], totals[1])
+            one = by_head(q[span] * scale)
+            scores = [
+                jnp.where(mask, nt(one, keys[0, :count]), -1e9)
+                for mask, keys in zip(allowed_keys(at, first, step, count), (kv, kv_other))
+            ]
+            most = jnp.maximum(
+                jnp.max(scores[0], axis=1, keepdims=True),
+                jnp.max(scores[1], axis=1, keepdims=True),
+            )
+            exponents = [jnp.exp(s - most) for s in scores]
+            summed = jnp.sum(exponents[0], axis=1, keepdims=True) + jnp.sum(
+                exponents[1], axis=1, keepdims=True
+            )
+            inverse = 1.0 / summed
+            result = nn(exponents[0].astype(B16), kv[1, :count]) + nn(
+                exponents[1].astype(B16), kv_other[1, :count]
+            )
+            mixed[span] = joined_heads(result * inverse).astype(B16)
+            lse[span] = joined_heads(
+                jnp.broadcast_to(most + jnp.log(summed), (2 * step, ONE))
+            )
 
     return kernel_call_named(
         "attention_forward", body, [((rows, ONE), B16), ((rows, ONE), F32)], at, q, kv, kv_other,
@@ -873,7 +881,7 @@
         def one(span):
             total[span] = nn(mixed[span], out[...]) + nn(active[span], down[...])
 
-        by_rows(rows, 256, one)
+        by_rows(rows, rows, one)
         pieces_out(at, total, pieces)
 
     return weights_call(
@@ -904,7 +912,7 @@
             up_grad[span] = (nt(g[span], down[...]) * slope[span].astype(F32)).astype(B16)
             mixed_grad[span] = nt(g[span], out[...]).astype(B16)
 
-        by_rows(rows, 256, back)
+        by_rows(rows, rows, back)
 
     outs = [((rows, dim), B16), ((rows, units), B16), ((rows, ONE), B16)]
     outs += [((rows // 8, dim), B16)] if with_piece else [((n, dim), B16) for n in (ONE, ONE // 2)]
@@ -919,38 +927,31 @@
     scale = 1.0 / math.sqrt(HD)
 
     def body(at, q, kv, kv_other, lse, mixed_grad, dq, dkv, dkv_other):
-        first_head = head_lanes()
         step = 256
         dkv[...] = jnp.zeros_like(dkv)
         dkv_other[...] = jnp.zeros_like(dkv_other)
         for first in range(0, rows, step):
             span = slice(first, first + step)
             count = first + step
-            queries, back = q[span], mixed_grad[span]
+            one, one_back = by_head(q[span] * scale), by_head(mixed_grad[span])
             masks = allowed_keys(at, first, step, count)
             sides = ((masks[0], kv, dkv), (masks[1], kv_other, dkv_other))
-            results = []
-            for head in range(2):
-                lanes = first_head if head == 0 else jnp.logical_not(first_head)
-                one = jnp.where(lanes, queries, jnp.zeros_like(queries))
-                one_back = jnp.where(lanes, back, jnp.zeros_like(back))
-                level = lse[span, head * HD : head * HD + 1]
-                probs, grads = [], []
-                for mask, keys, _ in sides:
-                    scores = nt(one, keys[0, :count]) * scale
-                    probs.append(jnp.exp(jnp.where(mask, scores, -1e9) - level))
-                    grads.append(nt(one_back, keys[1, :count]))
-                delta = jnp.sum(probs[0] * grads[0], axis=1, keepdims=True) + jnp.sum(
-                    probs[1] * grads[1], axis=1, keepdims=True
-                )
-                result = 0.0
-                for (_, keys, target), prob, grad in zip(sides, probs, grads):
-                    score_grad = (prob * (grad - delta) * scale).astype(B16)
-                    result = result + nn(score_grad, keys[0, :count])
-                    target[0, :count] += tn(score_grad, one)
-                    target[1, :count] += tn(prob.astype(B16), one_back)
-                results.append(result)
-            dq[span] = jnp.where(first_head, results[0], results[1])
+            level = jnp.concatenate([lse[span, :1], lse[span, HD : HD + 1]], axis=0)
+            probs, grads = [], []
+            for mask, keys, _ in sides:
+                scores = nt(one, keys[0, :count])
+                probs.append(jnp.exp(jnp.where(mask, scores, -1e9) - level))
+                grads.append(nt(one_back, keys[1, :count]))
+            delta = jnp.sum(probs[0] * grads[0], axis=1, keepdims=True) + jnp.sum(
+                probs[1] * grads[1], axis=1, keepdims=True
+            )
+            result = 0.0
+            for (_, keys, target), prob, grad in zip(sides, probs, grads):
+                score_grad = (prob * (grad - delta)).astype(B16)
+                result = result + nn(score_grad, keys[0, :count])
+                target[0, :count] += tn(score_grad, one)
+                target[1, :count] += tn(prob.astype(B16), one_back)
+            dq[span] = joined_heads(result) * scale
 
     return kernel_call_named(
         "attention_backward",
@@ -969,7 +970,7 @@
         qkv_grad, table = rest[:2]
         pieces, (qkv, up, total, lines) = rest[2:6], rest[6:]
         gain_one, gain_two = vectors[0:1], vectors[2:3]
-        step = 128
+        step = rows
 
         def one(i, sums):
             span = pl.ds(pl.multiple_of(i * step, step), step)
@@ -1072,20 +1073,20 @@
 
     def body(at, active, mixed, mlp_in, up_grad, g, keep, give):
         for core, target in ((0, keep), (1, give)):
+            strip = jnp.concatenate([columns(at, g, core, high) for high in range(2)], axis=1)
+            down = tn(active[...], strip).astype(B16)
+            out = tn(mixed[...], strip).astype(B16)
             for high in range(2):
-                strip = columns(at, g, core, high)
-                down = tn(active[...], strip).astype(B16)
-                out = tn(mixed[...], strip).astype(B16)
                 up = tn(columns(at, mlp_in, core, high), up_grad[...]).astype(B16)
                 for low in range(2):
-                    lanes = slice(low * ONE, (low + 1) * ONE)
+                    lanes = slice((2 * high + low) * ONE, (2 * high + low + 1) * ONE)
                     where = (at[S_HALF] ^ high, at[S_NEAR] ^ low)
                     target[where[0], where[1], :units] = down[:, lanes]
                     target[where[0], where[1], units : units + ONE] = out[:, lanes]
                     for i in range(tiles):
                         base = units + (1 + i) * ONE
                         target[where[0], where[1], base : base + ONE] = up[
-                            lanes, i * ONE : (i + 1) * ONE
+                            low * ONE : (low + 1) * ONE, i * ONE : (i + 1) * ONE
                         ]
 
     shape = (2, 2, 2 * units + ONE, ONE)

time: 246 us -> 240 us (0.976)
  Pallas kernels: 65.9 us -> 57.4 us
  waiting for transfers between devices: 96.5 us -> 101 us
    pallas_call x32, Pallas kernels: 62.1 us -> 53.6 us  [kernel_call(): pl.pallas_call(body, name=name, out_shape=[(pltpu.VMEM if keep else jax.S...]
    ppermute x64, waiting for transfers between devices: 96.5 us -> 101 us  [swapped(): return lax.ppermute(array, ALL, pairs)]
  transfers between devices with their start and end apart: 64 -> 64, of which waited for: 31 -> 31; matrix products, arithmetic and copies ran while one was open for 2% -> 2% of each run, Pallas kernels for 18% -> 16%
where the time goes in v3:
time: 240 us
  waiting for transfers between devices  101 us (42%)
  starting transfers between devices  73.3 us (31%)
  Pallas kernels  57.4 us (24%)
  other arithmetic  4.78 us (2%)
    ppermute x64, waiting for transfers between devices, swapped(): return lax.ppermute(array, ALL, pairs)  101 us
    ppermute x64, starting transfers between devices, swapped(): return lax.ppermute(array, ALL, pairs)  73.3 us
    pallas_call x32, Pallas kernels, kernel_call(): pl.pallas_call(body, name=name, out_shape=[(pltpu.VMEM if keep else jax.S...  53.6 us
  transfers between devices with their start and end apart: 64, of which 31 were waited for; matrix products, arithmetic and copies ran while one was open for 2% of the time, Pallas kernels for 16%

profile of v3, /device:TPU:0, one launch (start us, length us, event | category | flops | bytes accessed | tf_op | source)
XLA Modules:
  0.0 239.5 jit_solution(15679879333039511723)
XLA Ops:
  0.8 1.8 pack_first.1
  2.6 3.0 %collective-permute-start.5 = (bf16[1584,128]{1,0:T(8,128)(2,1)S(1)}, bf16[1584,128]{1,0:T(8,128)(2,1)S(1)}, u32[]{:S(2)}, u32[]{:S(2)}) collective-permute-start(bf16[1584,128]{1,0:T(8,128)(2,1)S(1)} %get-tuple-element.154), channel_id=1, source_target_pairs={{0,16},{1,17},{2,18},{3,19},{4,20},{5,21},{6,22},{7,23},{8,24},{9,... | collective-permute-start | bytes 1216520 | tf_op jit(solution)/shard_map/ppermute | solution.py:323
  5.6 3.6 %collective-permute-start.2 = (bf16[128,512]{1,0:T(8,128)(2,1)S(1)}, bf16[128,512]{1,0:T(8,128)(2,1)S(1)}, u32[]{:S(2)}, u32[]{:S(2)}) collective-permute-start(bf16[128,512]{1,0:T(8,128)(2,1)S(1)} %get-tuple-element.151), channel_id=1, source_target_pairs={{0,12},{1,13},{2,14},{3,15},{4,8},{5,9},{6,10},{7,11},{8,4},{9,5},... | collective-permute-start | bytes 393224 | tf_op jit(solution)/shard_map/ppermute | solution.py:323
  10.1 2.0 pack_second.1
  12.1 2.9 %collective-permute-done.5.refs_7_.refs_1_ = bf16[1584,128]{1,0:T(8,128)(2,1)S(1)} collective-permute-done((bf16[1584,128]{1,0:T(8,128)(2,1)S(1)}, bf16[1584,128]{1,0:T(8,128)(2,1)S(1)}, u32[]{:S(2)}, u32[]{:S(2)}) %collective-permute-start.5) | collective-permute-done | bytes 405536 | tf_op jit(solution)/shard_map/ppermute | solution.py:323
  17.3 1.8 negate_select_fusion.1
  22.3 1.8 choose_qkv.1
  25.5 2.4 %collective-permute-done.3.refs_4_ = bf16[128,512]{1,0:T(8,128)(2,1)S(1)} collective-permute-done((bf16[128,512]{1,0:T(8,128)(2,1)S(1)}, bf16[128,512]{1,0:T(8,128)(2,1)S(1)}, u32[]{:S(2)}, u32[]{:S(2)}) %collective-permute-start.3) | collective-permute-done | bytes 131104 | tf_op jit(solution)/shard_map/ppermute | solution.py:323
  29.5 2.5 %front.2 = (bf16[512,1024]{1,0:T(8,128)(2,1)S(1)}, bf16[512,1024]{1,0:T(8,128)(2,1)S(1)}, bf16[512,1024]{1,0:T(8,128)(2,1)S(1)}, bf16[512,128]{1,0:T(8,128)(2,1)...) custom-call(s32[8]{0:T(128)S(1)} %stack.91.at, bf16[128,1024]{1,0:T(8,128)(2,1)S(1)} %get-tuple-element.150.refs_0_, ...), custom_call_target="tpu_custom_call" | custom-call | tf_op jit(solution)/shard_map/front/pallas_call | solution.py:347
  34.4 2.4 %attention_forward.2 = (bf16[512,128]{1,0:T(8,128)(2,1)S(1)}, f32[512,128]{1,0:T(8,128)S(1)}) custom-call(s32[8]{0:T(128)S(1)} %stack.91.at, bf16[512,128]{1,0:T(8,128)(2,1)S(1)} %get-tuple-element.158.q, bf16[2,512,128]{2,1,0:T(8,128)(2,1)S(1)} %get-tuple-element.159.kv, bf16[2,512,128]{2,1,0:T(8,128)(2,1)S(1)} %collective-permute-done.7.kv_other), custom_call_target="tpu_custom_call" | custom-call | tf_op jit(solution)/shard_map/attention_forward/pallas_call | solution.py:347
  36.8 1.9 choose_up.1
  40.9 3.3 %collective-permute-done.10.refs_2_ = bf16[320,1024]{1,0:T(8,128)(2,1)S(1)} collective-permute-done((bf16[320,1024]{1,0:T(8,128)(2,1)S(1)}, bf16[320,1024]{1,0:T(8,128)(2,1)S(1)}, u32[]{:S(2)}, u32[]{:S(2)}) %collective-permute-start.10) | collective-permute-done | bytes 655392 | tf_op jit(solution)/shard_map/ppermute | solution.py:323
  44.3 2.1 collective-permute-done.12.refs_3_
  46.4 1.9 choose_rows.1
  53.5 3.6 %collective-permute-start.14 = (bf16[128,512]{1,0:T(8,128)(2,1)S(1)}, bf16[128,512]{1,0:T(8,128)(2,1)S(1)}, u32[]{:S(2)}, u32[]{:S(2)}) collective-permute-start(bf16[128,512]{1,0:T(8,128)(2,1)S(1)} %get-tuple-element.176), channel_id=1, source_target_pairs={{0,12},{1,13},{2,14},{3,15},{4,8},{5,9},{6,10},{7,11},{8,4},{9,5},... | collective-permute-start | bytes 393224 | tf_op jit(solution)/shard_map/ppermute | solution.py:323
  57.1 4.5 %collective-permute-done.14.refs_3_ = bf16[128,512]{1,0:T(8,128)(2,1)S(1)} collective-permute-done((bf16[128,512]{1,0:T(8,128)(2,1)S(1)}, bf16[128,512]{1,0:T(8,128)(2,1)S(1)}, u32[]{:S(2)}, u32[]{:S(2)}) %collective-permute-start.14) | collective-permute-done | bytes 131104 | tf_op jit(solution)/shard_map/ppermute | solution.py:323
  61.5 6.1 %collective-permute-done.13.refs_2_ = bf16[128,512]{1,0:T(8,128)(2,1)S(1)} collective-permute-done((bf16[128,512]{1,0:T(8,128)(2,1)S(1)}, bf16[128,512]{1,0:T(8,128)(2,1)S(1)}, u32[]{:S(2)}, u32[]{:S(2)}) %collective-permute-start.13) | collective-permute-done | bytes 131104 | tf_op jit(solution)/shard_map/ppermute | solution.py:323
  70.5 2.9 %collective-permute-done.18.rest_0_ = bf16[64,1024]{1,0:T(8,128)(2,1)S(1)} collective-permute-done((bf16[64,1024]{1,0:T(8,128)(2,1)S(1)}, bf16[64,1024]{1,0:T(8,128)(2,1)S(1)}, u32[]{:S(2)}, u32[]{:S(2)}) %collective-permute-start.18) | collective-permute-done | bytes 131104 | tf_op jit(solution)/shard_map/ppermute | solution.py:323
  75.7 3.2 %collective-permute-done.19 = bf16[64,1024]{1,0:T(8,128)(2,1)S(1)} collective-permute-done((bf16[64,1024]{1,0:T(8,128)(2,1)S(1)}, bf16[64,1024]{1,0:T(8,128)(2,1)S(1)}, u32[]{:S(2)}, u32[]{:S(2)}) %collective-permute-start.19) | collective-permute-done | bytes 131104 | tf_op jit(solution)/shard_map/ppermute | solution.py:323
  82.5 5.4 %collective-permute-done.24.refs_3_ = bf16[2,64,1024]{2,1,0:T(8,128)(2,1)S(1)} collective-permute-done((bf16[2,64,1024]{2,1,0:T(8,128)(2,1)S(1)}, bf16[2,64,1024]{2,1,0:T(8,128)(2,1)S(1)}, u32[]{:S(2)}, u32[]{:S(2)}) %collective-permute-start.24) | collective-permute-done | bytes 262176 | tf_op jit(solution)/shard_map/ppermute | solution.py:323
  88.0 2.8 %collective-permute-done.23.refs_2_ = bf16[2,64,1024]{2,1,0:T(8,128)(2,1)S(1)} collective-permute-done((bf16[2,64,1024]{2,1,0:T(8,128)(2,1)S(1)}, bf16[2,64,1024]{2,1,0:T(8,128)(2,1)S(1)}, u32[]{:S(2)}, u32[]{:S(2)}) %collective-permute-start.23) | collective-permute-done | bytes 262176 | tf_op jit(solution)/shard_map/ppermute | solution.py:323
  90.8 2.7 %front.3 = (bf16[512,1024]{1,0:T(8,128)(2,1)S(1)}, bf16[512,1024]{1,0:T(8,128)(2,1)S(1)}, bf16[512,1024]{1,0:T(8,128)(2,1)S(1)}, bf16[512,128]{1,0:T(8,128)(2,1)...) custom-call(s32[8]{0:T(128)S(1)} %stack.91.at, ...), custom_call_target="tpu_custom_call" | custom-call | tf_op jit(solution)/shard_map/front/pallas_call | solution.py:347
  96.8 2.4 %attention_forward.3 = (bf16[512,128]{1,0:T(8,128)(2,1)S(1)}, f32[512,128]{1,0:T(8,128)S(1)}) custom-call(s32[8]{0:T(128)S(1)} %stack.91.at, bf16[512,128]{1,0:T(8,128)(2,1)S(1)} %get-tuple-element.193.q, bf16[2,512,128]{2,1,0:T(8,128)(2,1)S(1)} %get-tuple-element.194.kv, bf16[2,512,128]{2,1,0:T(8,128)(2,1)S(1)} %collective-permute-done.25.kv_other), custom_call_target="tpu_custom_call" | custom-call | tf_op jit(solution)/shard_map/attention_forward/pallas_call | solution.py:347
  99.3 3.6 %attention_backward.2 = (f32[512,128]{1,0:T(8,128)S(1)}, f32[2,512,128]{2,1,0:T(8,128)S(1)}, f32[2,512,128]{2,1,0:T(8,128)S(1)}) custom-call(s32[8]{0:T(128)S(1)} %stack.91.at, bf16[512,128]{1,0:T(8,128)(2,1)S(1)} %get-tuple-element.193.q, bf16[2,512,128]{2,1,0:T(8,128)(2,1)S(1)} %get-tuple-element.194.kv, ...), custom_call_target="tpu_custom_call" | custom-call | tf_op jit(solution)/shard_map/attention_backward/pallas_call | solution.py:347
  103.4 2.1 early_grads.2
  105.6 2.5 %inputs_backward.2 = (bf16[512,384]{1,0:T(8,128)(2,1)S(1)}, bf16[64,128]{1,0:T(8,128)(2,1)S(1)}, f32[2,64,1024]{2,1,0:T(8,128)S(1)}, bf16[2,64,1024]{2,1,0:T(8,1...) custom-call(s32[8]{0:T(128)S(1)} %stack.91.at, ...), custom_call_target="tpu_custom_call" | custom-call | tf_op jit(solution)/shard_map/inputs_backward/pallas_call | solution.py:347
  114.5 1.8 outputs_forward.3
  116.4 9.9 %collective-permute-done.28 = bf16[1152,128]{1,0:T(8,128)(2,1)S(1)} collective-permute-done((bf16[1152,128]{1,0:T(8,128)(2,1)S(1)}, bf16[1152,128]{1,0:T(8,128)(2,1)S(1)}, u32[]{:S(2)}, u32[]{:S(2)}) %collective-permute-start.28) | collective-permute-done | bytes 294944 | tf_op jit(solution)/shard_map/ppermute | solution.py:323
  135.2 6.6 %collective-permute-done.35 = bf16[2,384,128]{2,1,0:T(8,128)(2,1)S(1)} collective-permute-done((bf16[2,384,128]{2,1,0:T(8,128)(2,1)S(1)}, bf16[2,384,128]{2,1,0:T(8,128)(2,1)S(1)}, u32[]{:S(2)}, u32[]{:S(2)}) %collective-permute-start.35) | collective-permute-done | bytes 196640 | tf_op jit(solution)/shard_map/ppermute | solution.py:323
  142.1 2.0 collective-permute-start.39
  147.7 9.1 %collective-permute-done.39 = bf16[1152,128]{1,0:T(8,128)(2,1)S(1)} collective-permute-done((bf16[1152,128]{1,0:T(8,128)(2,1)S(1)}, bf16[1152,128]{1,0:T(8,128)(2,1)S(1)}, u32[]{:S(2)}, u32[]{:S(2)}) %collective-permute-start.39) | collective-permute-done | bytes 294944 | tf_op jit(solution)/shard_map/ppermute | solution.py:323
  158.8 2.1 early_grads.3
  161.0 3.6 %attention_backward.3 = (f32[512,128]{1,0:T(8,128)S(1)}, f32[2,512,128]{2,1,0:T(8,128)S(1)}, f32[2,512,128]{2,1,0:T(8,128)S(1)}) custom-call(s32[8]{0:T(128)S(1)} %stack.91.at, bf16[512,128]{1,0:T(8,128)(2,1)S(1)} %get-tuple-element.158.q, bf16[2,512,128]{2,1,0:T(8,128)(2,1)S(1)} %get-tuple-element.159.kv, ...), custom_call_target="tpu_custom_call" | custom-call | tf_op jit(solution)/shard_map/attention_backward/pallas_call | solution.py:347
  166.4 2.3 collective-permute-start.46
  168.7 2.5 %inputs_backward.3 = (bf16[512,384]{1,0:T(8,128)(2,1)S(1)}, bf16[64,128]{1,0:T(8,128)(2,1)S(1)}, f32[2,64,1024]{2,1,0:T(8,128)S(1)}, bf16[2,64,1024]{2,1,0:T(8,1...) custom-call(s32[8]{0:T(128)S(1)} %stack.91.at, ...), custom_call_target="tpu_custom_call" | custom-call | tf_op jit(solution)/shard_map/inputs_backward/pallas_call | solution.py:347
  171.3 2.0 collective-permute-done.45.rest_0_
  178.8 3.6 %collective-permute-done.46 = bf16[1152,128]{1,0:T(8,128)(2,1)S(1)} collective-permute-done((bf16[1152,128]{1,0:T(8,128)(2,1)S(1)}, bf16[1152,128]{1,0:T(8,128)(2,1)S(1)}, u32[]{:S(2)}, u32[]{:S(2)}) %collective-permute-start.46) | collective-permute-done | bytes 294944 | tf_op jit(solution)/shard_map/ppermute | solution.py:323
  183.4 3.3 %collective-permute-done.48.refs_2_ = bf16[2,64,1024]{2,1,0:T(8,128)(2,1)S(1)} collective-permute-done((bf16[2,64,1024]{2,1,0:T(8,128)(2,1)S(1)}, bf16[2,64,1024]{2,1,0:T(8,128)(2,1)S(1)}, u32[]{:S(2)}, u32[]{:S(2)}) %collective-permute-start.48) | collective-permute-done | bytes 262176 | tf_op jit(solution)/shard_map/ppermute | solution.py:323
  187.8 2.1 collective-permute-start.60
  189.9 2.5 %collective-permute-start.51 = (bf16[1152,128]{1,0:T(8,128)(2,1)S(1)}, bf16[1152,128]{1,0:T(8,128)(2,1)S(1)}, u32[]{:S(2)}, u32[]{:S(2)}) collective-permute-start(bf16[1152,128]{1,0:T(8,128)(2,1)S(1)} %get-tuple-element.261), channel_id=1, source_target_pairs={{0,8},{1,9},{2,10},{3,11},{4,12},{5,13},{6,14},{7,15},{8,0},{9,1},... | collective-permute-start | bytes 884744 | tf_op jit(solution)/shard_map/ppermute | solution.py:323
  193.0 12.8 %collective-permute-done.50.rest_0_ = bf16[64,1024]{1,0:T(8,128)(2,1)S(1)} collective-permute-done((bf16[64,1024]{1,0:T(8,128)(2,1)S(1)}, bf16[64,1024]{1,0:T(8,128)(2,1)S(1)}, u32[]{:S(2)}, u32[]{:S(2)}) %collective-permute-start.50) | collective-permute-done | bytes 131104 | tf_op jit(solution)/shard_map/ppermute | solution.py:323
  205.8 4.4 %collective-permute-done.51 = bf16[1152,128]{1,0:T(8,128)(2,1)S(1)} collective-permute-done((bf16[1152,128]{1,0:T(8,128)(2,1)S(1)}, bf16[1152,128]{1,0:T(8,128)(2,1)S(1)}, u32[]{:S(2)}, u32[]{:S(2)}) %collective-permute-start.51) | collective-permute-done | bytes 294944 | tf_op jit(solution)/shard_map/ppermute | solution.py:323
  213.5 4.1 %collective-permute-done.52 = bf16[64,1024]{1,0:T(8,128)(2,1)S(1)} collective-permute-done((bf16[64,1024]{1,0:T(8,128)(2,1)S(1)}, bf16[64,1024]{1,0:T(8,128)(2,1)S(1)}, u32[]{:S(2)}, u32[]{:S(2)}) %collective-permute-start.52) | collective-permute-done | bytes 131104 | tf_op jit(solution)/shard_map/ppermute | solution.py:323
  217.7 3.4 %collective-permute-start.53 = (bf16[2,64,1024]{2,1,0:T(8,128)(2,1)S(1)}, bf16[2,64,1024]{2,1,0:T(8,128)(2,1)S(1)}, u32[]{:S(2)}, u32[]{:S(2)}) collective-permute-start(bf16[2,64,1024]{2,1,0:T(8,128)(2,1)S(1)} %pad_maximum_fusion.3), channel_id=1, source_target_pairs={{0,8},{1,9},{2,10},{3,11},{4,12},{5,13},{6,14},{7,15},{8,0},{9,1},... | collective-permute-start | bytes 786440 | tf_op jit(solution)/shard_map/ppermute | solution.py:323
  222.8 3.8 %collective-permute-start.62 = (bf16[448,128]{1,0:T(8,128)(2,1)S(1)}, bf16[448,128]{1,0:T(8,128)(2,1)S(1)}, u32[]{:S(2)}, u32[]{:S(2)}) collective-permute-start(bf16[448,128]{1,0:T(8,128)(2,1)S(1)} %get-tuple-element.318), channel_id=1, source_target_pairs={{0,20},{1,21},{2,22},{3,23},{4,16},{5,17},{6,18},{7,19},{8,28},{9,... | collective-permute-start | bytes 344072 | tf_op jit(solution)/shard_map/ppermute | solution.py:323
  226.5 2.6 %collective-permute-done.53 = bf16[2,64,1024]{2,1,0:T(8,128)(2,1)S(1)} collective-permute-done((bf16[2,64,1024]{2,1,0:T(8,128)(2,1)S(1)}, bf16[2,64,1024]{2,1,0:T(8,128)(2,1)S(1)}, u32[]{:S(2)}, u32[]{:S(2)}) %collective-permute-start.53) | collective-permute-done | bytes 262176 | tf_op jit(solution)/shard_map/ppermute | solution.py:323
  231.9 2.1 collective-permute-start.63
  234.0 2.5 %unpack_grads.1 = (f32[3,128,512]{2,1,0:T(8,128)}, f32[512,128]{1,0:T(8,128)}, f32[128,2048]{1,0:T(8,128)}, f32[2048,128]{1,0:T(8,128)}, f32[3,512]{1,0:T(4,128)...) custom-call(s32[8]{0:T(128)S(1)} %stack.91.at, bf16[1152,128]{1,0:T(8,128)(2,1)S(1)} %get-tuple-element.299.refs_0_, ...), custom_call_target="tpu_custom_call" | custom-call | tf_op jit(solution)/shard_map/unpack_grads/pallas_call | solution.py:347
  (167 shorter events, 73.9 us)
Async XLA Ops:
  2.6 12.4 %collective-permute-start.5 = (bf16[1584,128]{1,0:T(8,128)(2,1)S(1)}, bf16[1584,128]{1,0:T(8,128)(2,1)S(1)}, u32[]{:S(2)}, u32[]{:S(2)}) collective-permute-start(bf16[1584,128]{1,0:T(8,128)(2,1)S(1)} %get-tuple-element.154), channel_id=1, source_target_pairs={{0,16},{1,17},{2,18},{3,19},{4,20},{5,21},{6,22},{7,23},{8,24},{9,... | collective-permute-start | bytes 1216520 | tf_op jit(solution)/shard_map/ppermute | solution.py:323
  5.6 13.5 %collective-permute-start.2 = (bf16[128,512]{1,0:T(8,128)(2,1)S(1)}, bf16[128,512]{1,0:T(8,128)(2,1)S(1)}, u32[]{:S(2)}, u32[]{:S(2)}) collective-permute-start(bf16[128,512]{1,0:T(8,128)(2,1)S(1)} %get-tuple-element.151), channel_id=1, source_target_pairs={{0,12},{1,13},{2,14},{3,15},{4,8},{5,9},{6,10},{7,11},{8,4},{9,5},... | collective-permute-start | bytes 393224 | tf_op jit(solution)/shard_map/ppermute | solution.py:323
  9.2 11.5 %collective-permute-start.1 = (bf16[128,512]{1,0:T(8,128)(2,1)S(1)}, bf16[128,512]{1,0:T(8,128)(2,1)S(1)}, u32[]{:S(2)}, u32[]{:S(2)}) collective-permute-start(bf16[128,512]{1,0:T(8,128)(2,1)S(1)} %get-tuple-element.151), channel_id=1, source_target_pairs={{0,8},{1,9},{2,10},{3,11},{4,12},{5,13},{6,14},{7,15},{8,0},{9,1},... | collective-permute-start | bytes 393224 | tf_op jit(solution)/shard_map/ppermute | solution.py:323
  9.3 20.2 %collective-permute-start = (bf16[128,1024]{1,0:T(8,128)(2,1)S(1)}, bf16[128,1024]{1,0:T(8,128)(2,1)S(1)}, u32[]{:S(2)}, u32[]{:S(2)}) collective-permute-start(bf16[128,1024]{1,0:T(8,128)(2,1)S(1)} %get-tuple-element.150.refs_0_), channel_id=1, source_target_pairs={{0,4},{1,5},{2,6},{3,7},{4,0},{5,1},{6,2},{7,3},{8,12},{9,13},{10,... | collective-permute-start | bytes 786440 | tf_op jit(solution)/shard_map/ppermute | solution.py:323
  15.0 13.1 %collective-permute-start.8 = (bf16[512,512]{1,0:T(8,128)(2,1)S(1)}, bf16[512,512]{1,0:T(8,128)(2,1)S(1)}, u32[]{:S(2)}, u32[]{:S(2)}) collective-permute-start(bf16[512,512]{1,0:T(8,128)(2,1)S(1)} %get-tuple-element.163), channel_id=1, source_target_pairs={{0,16},{1,17},{2,18},{3,19},{4,20},{5,21},{6,22},{7,23},{8,24},{9,... | collective-permute-start | bytes 1572872 | tf_op jit(solution)/shard_map/ppermute | solution.py:323
  19.1 6.4 %collective-permute-start.4 = (bf16[128,512]{1,0:T(8,128)(2,1)S(1)}, bf16[128,512]{1,0:T(8,128)(2,1)S(1)}, u32[]{:S(2)}, u32[]{:S(2)}) collective-permute-start(bf16[128,512]{1,0:T(8,128)(2,1)S(1)} %collective-permute-done.2.refs_3_), channel_id=1, source_target_pairs={{0,1},{1,0},{2,3},{3,2},{4,5},{5,4},{6,7},{7,6},{8,9},{9,8},{10,11... | collective-permute-start | bytes 393224 | tf_op jit(solution)/shard_map/ppermute | solution.py:323
  20.7 7.2 %collective-permute-start.3 = (bf16[128,512]{1,0:T(8,128)(2,1)S(1)}, bf16[128,512]{1,0:T(8,128)(2,1)S(1)}, u32[]{:S(2)}, u32[]{:S(2)}) collective-permute-start(bf16[128,512]{1,0:T(8,128)(2,1)S(1)} %collective-permute-done.1.refs_2_), channel_id=1, source_target_pairs={{0,1},{1,0},{2,3},{3,2},{4,5},{5,4},{6,7},{7,6},{8,9},{9,8},{10,11... | collective-permute-start | bytes 393224 | tf_op jit(solution)/shard_map/ppermute | solution.py:323
  28.1 16.2 %collective-permute-start.10 = (bf16[320,1024]{1,0:T(8,128)(2,1)S(1)}, bf16[320,1024]{1,0:T(8,128)(2,1)S(1)}, u32[]{:S(2)}, u32[]{:S(2)}) collective-permute-start(bf16[320,1024]{1,0:T(8,128)(2,1)S(1)} %get-tuple-element.168), channel_id=1, source_target_pairs={{0,16},{1,17},{2,18},{3,19},{4,20},{5,21},{6,22},{7,23},{8,24},{9,... | collective-permute-start | bytes 1966088 | tf_op jit(solution)/shard_map/ppermute | solution.py:323
  32.6 8.3 %collective-permute-start.11 = (bf16[128,1024]{1,0:T(8,128)(2,1)S(1)}, bf16[128,1024]{1,0:T(8,128)(2,1)S(1)}, u32[]{:S(2)}, u32[]{:S(2)}) collective-permute-start(bf16[128,1024]{1,0:T(8,128)(2,1)S(1)} %get-tuple-element.170.refs_0_), channel_id=1, source_target_pairs={{0,4},{1,5},{2,6},{3,7},{4,0},{5,1},{6,2},{7,3},{8,12},{9,13},{10,... | collective-permute-start | bytes 786440 | tf_op jit(solution)/shard_map/ppermute | solution.py:323
  49.9 17.7 %collective-permute-start.15 = (bf16[2,64,1024]{2,1,0:T(8,128)(2,1)S(1)}, bf16[2,64,1024]{2,1,0:T(8,128)(2,1)S(1)}, u32[]{:S(2)}, u32[]{:S(2)}) collective-permute-start(bf16[2,64,1024]{2,1,0:T(8,128)(2,1)S(1)} %get-tuple-element.178), channel_id=1, source_target_pairs={{0,1},{1,0},{2,3},{3,2},{4,5},{5,4},{6,7},{7,6},{8,9},{9,8},{10,11... | collective-permute-start | bytes 786440 | tf_op jit(solution)/shard_map/ppermute | solution.py:323
  51.5 16.1 %collective-permute-start.16 = (bf16[2,64,1024]{2,1,0:T(8,128)(2,1)S(1)}, bf16[2,64,1024]{2,1,0:T(8,128)(2,1)S(1)}, u32[]{:S(2)}, u32[]{:S(2)}) collective-permute-start(bf16[2,64,1024]{2,1,0:T(8,128)(2,1)S(1)} %get-tuple-element.179), channel_id=1, source_target_pairs={{0,16},{1,17},{2,18},{3,19},{4,20},{5,21},{6,22},{7,23},{8,24},{9,... | collective-permute-start | bytes 786440 | tf_op jit(solution)/shard_map/ppermute | solution.py:323
  52.0 15.6 %collective-permute-start.17 = (bf16[2,64,1024]{2,1,0:T(8,128)(2,1)S(1)}, bf16[2,64,1024]{2,1,0:T(8,128)(2,1)S(1)}, u32[]{:S(2)}, u32[]{:S(2)}) collective-permute-start(bf16[2,64,1024]{2,1,0:T(8,128)(2,1)S(1)} %get-tuple-element.180), channel_id=1, source_target_pairs={{0,17},{1,16},{2,19},{3,18},{4,21},{5,20},{6,23},{7,22},{8,25},{9,... | collective-permute-start | bytes 786440 | tf_op jit(solution)/shard_map/ppermute | solution.py:323
  53.5 8.1 %collective-permute-start.14 = (bf16[128,512]{1,0:T(8,128)(2,1)S(1)}, bf16[128,512]{1,0:T(8,128)(2,1)S(1)}, u32[]{:S(2)}, u32[]{:S(2)}) collective-permute-start(bf16[128,512]{1,0:T(8,128)(2,1)S(1)} %get-tuple-element.176), channel_id=1, source_target_pairs={{0,12},{1,13},{2,14},{3,15},{4,8},{5,9},{6,10},{7,11},{8,4},{9,5},... | collective-permute-start | bytes 393224 | tf_op jit(solution)/shard_map/ppermute | solution.py:323
  57.1 10.5 %collective-permute-start.13 = (bf16[128,512]{1,0:T(8,128)(2,1)S(1)}, bf16[128,512]{1,0:T(8,128)(2,1)S(1)}, u32[]{:S(2)}, u32[]{:S(2)}) collective-permute-start(bf16[128,512]{1,0:T(8,128)(2,1)S(1)} %get-tuple-element.176), channel_id=1, source_target_pairs={{0,8},{1,9},{2,10},{3,11},{4,12},{5,13},{6,14},{7,15},{8,0},{9,1},... | collective-permute-start | bytes 393224 | tf_op jit(solution)/shard_map/ppermute | solution.py:323
  79.0 9.0 %collective-permute-start.24 = (bf16[2,64,1024]{2,1,0:T(8,128)(2,1)S(1)}, bf16[2,64,1024]{2,1,0:T(8,128)(2,1)S(1)}, u32[]{:S(2)}, u32[]{:S(2)}) collective-permute-start(bf16[2,64,1024]{2,1,0:T(8,128)(2,1)S(1)} %pad_maximum_fusion.1.refs_0_), channel_id=1, source_target_pairs={{0,17},{1,16},{2,19},{3,18},{4,21},{5,20},{6,23},{7,22},{8,25},{9,... | collective-permute-start | bytes 786440 | tf_op jit(solution)/shard_map/ppermute | solution.py:323
  80.6 10.3 %collective-permute-start.23 = (bf16[2,64,1024]{2,1,0:T(8,128)(2,1)S(1)}, bf16[2,64,1024]{2,1,0:T(8,128)(2,1)S(1)}, u32[]{:S(2)}, u32[]{:S(2)}) collective-permute-start(bf16[2,64,1024]{2,1,0:T(8,128)(2,1)S(1)} %pad_maximum_fusion.1.refs_0_), channel_id=1, source_target_pairs={{0,16},{1,17},{2,18},{3,19},{4,20},{5,21},{6,22},{7,23},{8,24},{9,... | collective-permute-start | bytes 786440 | tf_op jit(solution)/shard_map/ppermute | solution.py:323
  82.0 8.8 %collective-permute-start.22 = (bf16[2,64,1024]{2,1,0:T(8,128)(2,1)S(1)}, bf16[2,64,1024]{2,1,0:T(8,128)(2,1)S(1)}, u32[]{:S(2)}, u32[]{:S(2)}) collective-permute-start(bf16[2,64,1024]{2,1,0:T(8,128)(2,1)S(1)} %pad_maximum_fusion.1.refs_0_), channel_id=1, source_target_pairs={{0,1},{1,0},{2,3},{3,2},{4,5},{5,4},{6,7},{7,6},{8,9},{9,8},{10,11... | collective-permute-start | bytes 786440 | tf_op jit(solution)/shard_map/ppermute | solution.py:323
  109.5 6.9 %collective-permute-start.34 = (bf16[2,2,384,128]{3,2,1,0:T(8,128)(2,1)S(1)}, bf16[2,2,384,128]{3,2,1,0:T(8,128)(2,1)S(1)}, u32[]{:S(2)}, u32[]{:S(2)}) collective-permute-start(bf16[2,2,384,128]{3,2,1,0:T(8,128)(2,1)S(1)} %get-tuple-element.214), channel_id=1, source_target_pairs={{0,2},{1,3},{2,0},{3,1},{4,6},{5,7},{6,4},{7,5},{8,10},{9,11},{10,... | collective-permute-start | bytes 1179656 | tf_op jit(solution)/shard_map/ppermute | solution.py:323
  110.2 16.1 %collective-permute-start.28 = (bf16[1152,128]{1,0:T(8,128)(2,1)S(1)}, bf16[1152,128]{1,0:T(8,128)(2,1)S(1)}, u32[]{:S(2)}, u32[]{:S(2)}) collective-permute-start(bf16[1152,128]{1,0:T(8,128)(2,1)S(1)} %get-tuple-element.303), channel_id=1, source_target_pairs={{0,8},{1,9},{2,10},{3,11},{4,12},{5,13},{6,14},{7,15},{8,0},{9,1},... | collective-permute-start | bytes 884744 | tf_op jit(solution)/shard_map/ppermute | solution.py:323
  111.0 15.3 %collective-permute-start.29 = (bf16[2,64,1024]{2,1,0:T(8,128)(2,1)S(1)}, bf16[2,64,1024]{2,1,0:T(8,128)(2,1)S(1)}, u32[]{:S(2)}, u32[]{:S(2)}) collective-permute-start(bf16[2,64,1024]{2,1,0:T(8,128)(2,1)S(1)} %get-tuple-element.216), channel_id=1, source_target_pairs={{0,1},{1,0},{2,3},{3,2},{4,5},{5,4},{6,7},{7,6},{8,9},{9,8},{10,11... | collective-permute-start | bytes 786440 | tf_op jit(solution)/shard_map/ppermute | solution.py:323
  112.4 13.9 %collective-permute-start.30 = (bf16[2,64,1024]{2,1,0:T(8,128)(2,1)S(1)}, bf16[2,64,1024]{2,1,0:T(8,128)(2,1)S(1)}, u32[]{:S(2)}, u32[]{:S(2)}) collective-permute-start(bf16[2,64,1024]{2,1,0:T(8,128)(2,1)S(1)} %get-tuple-element.217), channel_id=1, source_target_pairs={{0,16},{1,17},{2,18},{3,19},{4,20},{5,21},{6,22},{7,23},{8,24},{9,... | collective-permute-start | bytes 786440 | tf_op jit(solution)/shard_map/ppermute | solution.py:323
  112.9 13.4 %collective-permute-start.31 = (bf16[2,64,1024]{2,1,0:T(8,128)(2,1)S(1)}, bf16[2,64,1024]{2,1,0:T(8,128)(2,1)S(1)}, u32[]{:S(2)}, u32[]{:S(2)}) collective-permute-start(bf16[2,64,1024]{2,1,0:T(8,128)(2,1)S(1)} %get-tuple-element.218), channel_id=1, source_target_pairs={{0,17},{1,16},{2,19},{3,18},{4,21},{5,20},{6,23},{7,22},{8,25},{9,... | collective-permute-start | bytes 786440 | tf_op jit(solution)/shard_map/ppermute | solution.py:323
  128.0 13.8 %collective-permute-start.36 = (bf16[2,64,1024]{2,1,0:T(8,128)(2,1)S(1)}, bf16[2,64,1024]{2,1,0:T(8,128)(2,1)S(1)}, u32[]{:S(2)}, u32[]{:S(2)}) collective-permute-start(bf16[2,64,1024]{2,1,0:T(8,128)(2,1)S(1)} %get-tuple-element.225), channel_id=1, source_target_pairs={{0,1},{1,0},{2,3},{3,2},{4,5},{5,4},{6,7},{7,6},{8,9},{9,8},{10,11... | collective-permute-start | bytes 786440 | tf_op jit(solution)/shard_map/ppermute | solution.py:323
  129.4 12.4 %collective-permute-start.37 = (bf16[2,64,1024]{2,1,0:T(8,128)(2,1)S(1)}, bf16[2,64,1024]{2,1,0:T(8,128)(2,1)S(1)}, u32[]{:S(2)}, u32[]{:S(2)}) collective-permute-start(bf16[2,64,1024]{2,1,0:T(8,128)(2,1)S(1)} %get-tuple-element.227), channel_id=1, source_target_pairs={{0,16},{1,17},{2,18},{3,19},{4,20},{5,21},{6,22},{7,23},{8,24},{9,... | collective-permute-start | bytes 786440 | tf_op jit(solution)/shard_map/ppermute | solution.py:323
  130.0 12.2 %collective-permute-start.38 = (bf16[2,64,1024]{2,1,0:T(8,128)(2,1)S(1)}, bf16[2,64,1024]{2,1,0:T(8,128)(2,1)S(1)}, u32[]{:S(2)}, u32[]{:S(2)}) collective-permute-start(bf16[2,64,1024]{2,1,0:T(8,128)(2,1)S(1)} %get-tuple-element.229), channel_id=1, source_target_pairs={{0,17},{1,16},{2,19},{3,18},{4,21},{5,20},{6,23},{7,22},{8,25},{9,... | collective-permute-start | bytes 786440 | tf_op jit(solution)/shard_map/ppermute | solution.py:323
  131.6 10.2 %collective-permute-start.35 = (bf16[2,384,128]{2,1,0:T(8,128)(2,1)S(1)}, bf16[2,384,128]{2,1,0:T(8,128)(2,1)S(1)}, u32[]{:S(2)}, u32[]{:S(2)}) collective-permute-start(bf16[2,384,128]{2,1,0:T(8,128)(2,1)S(1)} %pad_maximum_fusion.5), channel_id=1, source_target_pairs={{0,8},{1,9},{2,10},{3,11},{4,12},{5,13},{6,14},{7,15},{8,0},{9,1},... | collective-permute-start | bytes 589832 | tf_op jit(solution)/shard_map/ppermute | solution.py:323
  133.8 8.0 %collective-permute-start.33 = (bf16[64,1024]{1,0:T(8,128)(2,1)S(1)}, bf16[64,1024]{1,0:T(8,128)(2,1)S(1)}, u32[]{:S(2)}, u32[]{:S(2)}) collective-permute-start(bf16[64,1024]{1,0:T(8,128)(2,1)S(1)} %join_backward.2.g), channel_id=1, source_target_pairs={{0,4},{1,5},{2,6},{3,7},{4,0},{5,1},{6,2},{7,3},{8,12},{9,13},{10,... | collective-permute-start | bytes 393224 | tf_op jit(solution)/shard_map/ppermute | solution.py:323
  142.1 14.7 %collective-permute-start.39 = (bf16[1152,128]{1,0:T(8,128)(2,1)S(1)}, bf16[1152,128]{1,0:T(8,128)(2,1)S(1)}, u32[]{:S(2)}, u32[]{:S(2)}) collective-permute-start(bf16[1152,128]{1,0:T(8,128)(2,1)S(1)} %get-tuple-element.231), channel_id=1, source_target_pairs={{0,8},{1,9},{2,10},{3,11},{4,12},{5,13},{6,14},{7,15},{8,0},{9,1},... | collective-permute-start | bytes 884744 | tf_op jit(solution)/shard_map/ppermute | solution.py:323
  144.1 12.7 %collective-permute-start.42 = (bf16[2,64,1024]{2,1,0:T(8,128)(2,1)S(1)}, bf16[2,64,1024]{2,1,0:T(8,128)(2,1)S(1)}, u32[]{:S(2)}, u32[]{:S(2)}) collective-permute-start(bf16[2,64,1024]{2,1,0:T(8,128)(2,1)S(1)} %pad_maximum_fusion.2.refs_0_), channel_id=1, source_target_pairs={{0,17},{1,16},{2,19},{3,18},{4,21},{5,20},{6,23},{7,22},{8,25},{9,... | collective-permute-start | bytes 786440 | tf_op jit(solution)/shard_map/ppermute | solution.py:323
  145.6 11.6 %collective-permute-start.41 = (bf16[2,64,1024]{2,1,0:T(8,128)(2,1)S(1)}, bf16[2,64,1024]{2,1,0:T(8,128)(2,1)S(1)}, u32[]{:S(2)}, u32[]{:S(2)}) collective-permute-start(bf16[2,64,1024]{2,1,0:T(8,128)(2,1)S(1)} %pad_maximum_fusion.2.refs_0_), channel_id=1, source_target_pairs={{0,16},{1,17},{2,18},{3,19},{4,20},{5,21},{6,22},{7,23},{8,24},{9,... | collective-permute-start | bytes 786440 | tf_op jit(solution)/shard_map/ppermute | solution.py:323
  147.1 10.1 %collective-permute-start.40 = (bf16[2,64,1024]{2,1,0:T(8,128)(2,1)S(1)}, bf16[2,64,1024]{2,1,0:T(8,128)(2,1)S(1)}, u32[]{:S(2)}, u32[]{:S(2)}) collective-permute-start(bf16[2,64,1024]{2,1,0:T(8,128)(2,1)S(1)} %pad_maximum_fusion.2.refs_0_), channel_id=1, source_target_pairs={{0,1},{1,0},{2,3},{3,2},{4,5},{5,4},{6,7},{7,6},{8,9},{9,8},{10,11... | collective-permute-start | bytes 786440 | tf_op jit(solution)/shard_map/ppermute | solution.py:323
  165.8 7.4 %collective-permute-start.45 = (bf16[64,1024]{1,0:T(8,128)(2,1)S(1)}, bf16[64,1024]{1,0:T(8,128)(2,1)S(1)}, u32[]{:S(2)}, u32[]{:S(2)}) collective-permute-start(bf16[64,1024]{1,0:T(8,128)(2,1)S(1)} %get-tuple-element.250), channel_id=1, source_target_pairs={{0,4},{1,5},{2,6},{3,7},{4,0},{5,1},{6,2},{7,3},{8,12},{9,13},{10,... | collective-permute-start | bytes 393224 | tf_op jit(solution)/shard_map/ppermute | solution.py:323
  166.4 16.0 %collective-permute-start.46 = (bf16[1152,128]{1,0:T(8,128)(2,1)S(1)}, bf16[1152,128]{1,0:T(8,128)(2,1)S(1)}, u32[]{:S(2)}, u32[]{:S(2)}) collective-permute-start(bf16[1152,128]{1,0:T(8,128)(2,1)S(1)} %get-tuple-element.300), channel_id=1, source_target_pairs={{0,8},{1,9},{2,10},{3,11},{4,12},{5,13},{6,14},{7,15},{8,0},{9,1},... | collective-permute-start | bytes 884744 | tf_op jit(solution)/shard_map/ppermute | solution.py:323
  173.2 10.2 %collective-permute-start.49 = (bf16[2,64,1024]{2,1,0:T(8,128)(2,1)S(1)}, bf16[2,64,1024]{2,1,0:T(8,128)(2,1)S(1)}, u32[]{:S(2)}, u32[]{:S(2)}) collective-permute-start(bf16[2,64,1024]{2,1,0:T(8,128)(2,1)S(1)} %get-tuple-element.258), channel_id=1, source_target_pairs={{0,17},{1,16},{2,19},{3,18},{4,21},{5,20},{6,23},{7,22},{8,25},{9,... | collective-permute-start | bytes 786440 | tf_op jit(solution)/shard_map/ppermute | solution.py:323
  174.6 12.1 %collective-permute-start.48 = (bf16[2,64,1024]{2,1,0:T(8,128)(2,1)S(1)}, bf16[2,64,1024]{2,1,0:T(8,128)(2,1)S(1)}, u32[]{:S(2)}, u32[]{:S(2)}) collective-permute-start(bf16[2,64,1024]{2,1,0:T(8,128)(2,1)S(1)} %get-tuple-element.256), channel_id=1, source_target_pairs={{0,16},{1,17},{2,18},{3,19},{4,20},{5,21},{6,22},{7,23},{8,24},{9,... | collective-permute-start | bytes 786440 | tf_op jit(solution)/shard_map/ppermute | solution.py:323
  176.2 10.6 %collective-permute-start.47 = (bf16[2,64,1024]{2,1,0:T(8,128)(2,1)S(1)}, bf16[2,64,1024]{2,1,0:T(8,128)(2,1)S(1)}, u32[]{:S(2)}, u32[]{:S(2)}) collective-permute-start(bf16[2,64,1024]{2,1,0:T(8,128)(2,1)S(1)} %get-tuple-element.254), channel_id=1, source_target_pairs={{0,1},{1,0},{2,3},{3,2},{4,5},{5,4},{6,7},{7,6},{8,9},{9,8},{10,11... | collective-permute-start | bytes 786440 | tf_op jit(solution)/shard_map/ppermute | solution.py:323
  178.7 13.7 %collective-permute-start.55 = (bf16[2,2,512,128]{3,2,1,0:T(8,128)(2,1)S(1)}, bf16[2,2,512,128]{3,2,1,0:T(8,128)(2,1)S(1)}, u32[]{:S(2)}, u32[]{:S(2)}) collective-permute-start(bf16[2,2,512,128]{3,2,1,0:T(8,128)(2,1)S(1)} %get-tuple-element.271), channel_id=1, source_target_pairs={{0,2},{1,3},{2,0},{3,1},{4,6},{5,7},{6,4},{7,5},{8,10},{9,11},{10,... | collective-permute-start | bytes 1572872 | tf_op jit(solution)/shard_map/ppermute | solution.py:323
  187.4 18.4 %collective-permute-start.50 = (bf16[64,1024]{1,0:T(8,128)(2,1)S(1)}, bf16[64,1024]{1,0:T(8,128)(2,1)S(1)}, u32[]{:S(2)}, u32[]{:S(2)}) collective-permute-start(bf16[64,1024]{1,0:T(8,128)(2,1)S(1)} %get-tuple-element.260), channel_id=1, source_target_pairs={{0,4},{1,5},{2,6},{3,7},{4,0},{5,1},{6,2},{7,3},{8,12},{9,13},{10,... | collective-permute-start | bytes 393224 | tf_op jit(solution)/shard_map/ppermute | solution.py:323
  187.8 34.9 %collective-permute-start.60 = (bf16[1152,128]{1,0:T(8,128)(2,1)S(1)}, bf16[1152,128]{1,0:T(8,128)(2,1)S(1)}, u32[]{:S(2)}, u32[]{:S(2)}) collective-permute-start(bf16[1152,128]{1,0:T(8,128)(2,1)S(1)} %get-tuple-element.296), channel_id=1, source_target_pairs={{0,20},{1,21},{2,22},{3,23},{4,16},{5,17},{6,18},{7,19},{8,28},{9,... | collective-permute-start | bytes 884744 | tf_op jit(solution)/shard_map/ppermute | solution.py:323
  189.8 32.9 %collective-permute-start.59 = (bf16[1152,128]{1,0:T(8,128)(2,1)S(1)}, bf16[1152,128]{1,0:T(8,128)(2,1)S(1)}, u32[]{:S(2)}, u32[]{:S(2)}) collective-permute-start(bf16[1152,128]{1,0:T(8,128)(2,1)S(1)} %get-tuple-element.297), channel_id=1, source_target_pairs={{0,4},{1,5},{2,6},{3,7},{4,0},{5,1},{6,2},{7,3},{8,12},{9,13},{10,... | collective-permute-start | bytes 884744 | tf_op jit(solution)/shard_map/ppermute | solution.py:323
  189.9 20.3 %collective-permute-start.51 = (bf16[1152,128]{1,0:T(8,128)(2,1)S(1)}, bf16[1152,128]{1,0:T(8,128)(2,1)S(1)}, u32[]{:S(2)}, u32[]{:S(2)}) collective-permute-start(bf16[1152,128]{1,0:T(8,128)(2,1)S(1)} %get-tuple-element.261), channel_id=1, source_target_pairs={{0,8},{1,9},{2,10},{3,11},{4,12},{5,13},{6,14},{7,15},{8,0},{9,1},... | collective-permute-start | bytes 884744 | tf_op jit(solution)/shard_map/ppermute | solution.py:323
  192.6 28.5 %collective-permute-start.56 = (bf16[2,512,128]{2,1,0:T(8,128)(2,1)S(1)}, bf16[2,512,128]{2,1,0:T(8,128)(2,1)S(1)}, u32[]{:S(2)}, u32[]{:S(2)}) collective-permute-start(bf16[2,512,128]{2,1,0:T(8,128)(2,1)S(1)} %pad_maximum_fusion.4), channel_id=1, source_target_pairs={{0,8},{1,9},{2,10},{3,11},{4,12},{5,13},{6,14},{7,15},{8,0},{9,1},... | collective-permute-start | bytes 786440 | tf_op jit(solution)/shard_map/ppermute | solution.py:323
  211.1 6.5 %collective-permute-start.52 = (bf16[64,1024]{1,0:T(8,128)(2,1)S(1)}, bf16[64,1024]{1,0:T(8,128)(2,1)S(1)}, u32[]{:S(2)}, u32[]{:S(2)}) collective-permute-start(bf16[64,1024]{1,0:T(8,128)(2,1)S(1)} %broadcast_select_fusion.4), channel_id=1, source_target_pairs={{0,16},{1,17},{2,18},{3,19},{4,20},{5,21},{6,22},{7,23},{8,24},{9,... | collective-permute-start | bytes 393224 | tf_op jit(solution)/shard_map/ppermute | solution.py:323
  212.7 10.0 %collective-permute-start.58 = (bf16[1152,128]{1,0:T(8,128)(2,1)S(1)}, bf16[1152,128]{1,0:T(8,128)(2,1)S(1)}, u32[]{:S(2)}, u32[]{:S(2)}) collective-permute-start(bf16[1152,128]{1,0:T(8,128)(2,1)S(1)} %get-tuple-element.298), channel_id=1, source_target_pairs={{0,16},{1,17},{2,18},{3,19},{4,20},{5,21},{6,22},{7,23},{8,24},{9,... | collective-permute-start | bytes 884744 | tf_op jit(solution)/shard_map/ppermute | solution.py:323
  217.7 11.5 %collective-permute-start.53 = (bf16[2,64,1024]{2,1,0:T(8,128)(2,1)S(1)}, bf16[2,64,1024]{2,1,0:T(8,128)(2,1)S(1)}, u32[]{:S(2)}, u32[]{:S(2)}) collective-permute-start(bf16[2,64,1024]{2,1,0:T(8,128)(2,1)S(1)} %pad_maximum_fusion.3), channel_id=1, source_target_pairs={{0,8},{1,9},{2,10},{3,11},{4,12},{5,13},{6,14},{7,15},{8,0},{9,1},... | collective-permute-start | bytes 786440 | tf_op jit(solution)/shard_map/ppermute | solution.py:323
  221.3 9.6 %collective-permute-start.57 = (bf16[448,128]{1,0:T(8,128)(2,1)S(1)}, bf16[448,128]{1,0:T(8,128)(2,1)S(1)}, u32[]{:S(2)}, u32[]{:S(2)}) collective-permute-start(bf16[448,128]{1,0:T(8,128)(2,1)S(1)} %get-tuple-element.316), channel_id=1, source_target_pairs={{0,16},{1,17},{2,18},{3,19},{4,20},{5,21},{6,22},{7,23},{8,24},{9,... | collective-permute-start | bytes 344072 | tf_op jit(solution)/shard_map/ppermute | solution.py:323
  222.8 8.1 %collective-permute-start.62 = (bf16[448,128]{1,0:T(8,128)(2,1)S(1)}, bf16[448,128]{1,0:T(8,128)(2,1)S(1)}, u32[]{:S(2)}, u32[]{:S(2)}) collective-permute-start(bf16[448,128]{1,0:T(8,128)(2,1)S(1)} %get-tuple-element.318), channel_id=1, source_target_pairs={{0,20},{1,21},{2,22},{3,23},{4,16},{5,17},{6,18},{7,19},{8,28},{9,... | collective-permute-start | bytes 344072 | tf_op jit(solution)/shard_map/ppermute | solution.py:323
  229.2 8.8 %collective-permute-start.54 = (bf16[3,64,1024]{2,1,0:T(8,128)(2,1)S(1)}, bf16[3,64,1024]{2,1,0:T(8,128)(2,1)S(1)}, u32[]{:S(2)}, u32[]{:S(2)}) collective-permute-start(bf16[3,64,1024]{2,1,0:T(8,128)(2,1)S(1)} %pad_maximum_fusion), channel_id=1, source_target_pairs={{0,1},{1,0},{2,3},{3,2},{4,5},{5,4},{6,7},{7,6},{8,9},{9,8},{10,11... | collective-permute-start | bytes 1179656 | tf_op jit(solution)/shard_map/ppermute | solution.py:323
  (23 other events, 159.7 us)

commit v4 on v3

--- a/solution.py
+++ b/solution.py
@@ -359,7 +359,7 @@
     )(at, *arrays, *in_hbm(hbm), *free)
 
 
-VMEM_BYTES = 12 * 1024 * 1024
+VMEM_BYTES = 16 * 1024 * 1024
 
 
 def kernel_call_named(name, *args, **kwargs):
@@ -738,7 +738,7 @@
                 target[span] = flat.astype(B16)
             kv[1, span] = projected[:, 2 * ONE :].astype(B16)
 
-        by_rows(rows, 256, norm)
+        by_rows(rows, rows, norm)
         by_rows(rows, rows, project)
 
     outs = [((rows, dim), B16)] * 3 + [((rows, ONE), B16), ((2, rows, ONE), B16)]
@@ -839,7 +839,7 @@
     scale = 1.0 / math.sqrt(HD)
 
     def body(at, q, kv, kv_other, mixed, lse):
-        step = 256
+        step = 128
         for first in range(0, rows, step):
             span = slice(first, first + step)
             count = first + step

time: 240 us -> 239 us (level)
  transfers between devices with their start and end apart: 64 -> 64, of which waited for: 31 -> 32; matrix products, arithmetic and copies ran while one was open for 2% -> 2% of each run, Pallas kernels for 16% -> 16%
where the time goes in v4:
time: 239 us
  waiting for transfers between devices  101 us (42%)
  starting transfers between devices  73.2 us (31%)
  Pallas kernels  56.1 us (23%)
  other arithmetic  5.05 us (2%)
    ppermute x64, waiting for transfers between devices, swapped(): return lax.ppermute(array, ALL, pairs)  101 us
    ppermute x64, starting transfers between devices, swapped(): return lax.ppermute(array, ALL, pairs)  73.2 us
    pallas_call x32, Pallas kernels, kernel_call(): pl.pallas_call(body, name=name, out_shape=[(pltpu.VMEM if keep else jax.S...  52.3 us
  transfers between devices with their start and end apart: 64, of which 32 were waited for; matrix products, arithmetic and copies ran while one was open for 2% of the time, Pallas kernels for 16%

profile of v4, /device:TPU:0, one launch (start us, length us, event | category | flops | bytes accessed | tf_op | source)
XLA Modules:
  0.0 239.0 jit_solution(8126632555383952427)
XLA Ops:
  0.8 1.8 pack_first.1
  2.6 3.0 %collective-permute-start.5 = (bf16[1584,128]{1,0:T(8,128)(2,1)S(1)}, bf16[1584,128]{1,0:T(8,128)(2,1)S(1)}, u32[]{:S(2)}, u32[]{:S(2)}) collective-permute-start(bf16[1584,128]{1,0:T(8,128)(2,1)S(1)} %get-tuple-element.154), channel_id=1, source_target_pairs={{0,16},{1,17},{2,18},{3,19},{4,20},{5,21},{6,22},{7,23},{8,24},{9,... | collective-permute-start | bytes 1216520 | tf_op jit(solution)/shard_map/ppermute | solution.py:323
  5.6 3.6 %collective-permute-start.2 = (bf16[128,512]{1,0:T(8,128)(2,1)S(1)}, bf16[128,512]{1,0:T(8,128)(2,1)S(1)}, u32[]{:S(2)}, u32[]{:S(2)}) collective-permute-start(bf16[128,512]{1,0:T(8,128)(2,1)S(1)} %get-tuple-element.151), channel_id=1, source_target_pairs={{0,12},{1,13},{2,14},{3,15},{4,8},{5,9},{6,10},{7,11},{8,4},{9,5},... | collective-permute-start | bytes 393224 | tf_op jit(solution)/shard_map/ppermute | solution.py:323
  10.1 2.0 pack_second.1
  12.1 2.9 %collective-permute-done.5.refs_7_.refs_1_ = bf16[1584,128]{1,0:T(8,128)(2,1)S(1)} collective-permute-done((bf16[1584,128]{1,0:T(8,128)(2,1)S(1)}, bf16[1584,128]{1,0:T(8,128)(2,1)S(1)}, u32[]{:S(2)}, u32[]{:S(2)}) %collective-permute-start.5) | collective-permute-done | bytes 405536 | tf_op jit(solution)/shard_map/ppermute | solution.py:323
  15.0 1.7 collective-permute-start.8
  17.3 1.8 negate_select_fusion.1
  22.3 1.8 choose_qkv.1
  25.5 2.4 %collective-permute-done.3.refs_4_ = bf16[128,512]{1,0:T(8,128)(2,1)S(1)} collective-permute-done((bf16[128,512]{1,0:T(8,128)(2,1)S(1)}, bf16[128,512]{1,0:T(8,128)(2,1)S(1)}, u32[]{:S(2)}, u32[]{:S(2)}) %collective-permute-start.3) | collective-permute-done | bytes 131104 | tf_op jit(solution)/shard_map/ppermute | solution.py:323
  29.5 2.0 front.2
  33.9 2.3 attention_forward.2
  36.3 1.9 choose_up.1
  40.4 3.8 %collective-permute-done.10.refs_2_ = bf16[320,1024]{1,0:T(8,128)(2,1)S(1)} collective-permute-done((bf16[320,1024]{1,0:T(8,128)(2,1)S(1)}, bf16[320,1024]{1,0:T(8,128)(2,1)S(1)}, u32[]{:S(2)}, u32[]{:S(2)}) %collective-permute-start.10) | collective-permute-done | bytes 655392 | tf_op jit(solution)/shard_map/ppermute | solution.py:323
  44.3 2.1 collective-permute-done.12.refs_3_
  46.4 1.9 choose_rows.1
  53.5 3.6 %collective-permute-start.14 = (bf16[128,512]{1,0:T(8,128)(2,1)S(1)}, bf16[128,512]{1,0:T(8,128)(2,1)S(1)}, u32[]{:S(2)}, u32[]{:S(2)}) collective-permute-start(bf16[128,512]{1,0:T(8,128)(2,1)S(1)} %get-tuple-element.176), channel_id=1, source_target_pairs={{0,12},{1,13},{2,14},{3,15},{4,8},{5,9},{6,10},{7,11},{8,4},{9,5},... | collective-permute-start | bytes 393224 | tf_op jit(solution)/shard_map/ppermute | solution.py:323
  57.1 4.5 %collective-permute-done.14.refs_3_ = bf16[128,512]{1,0:T(8,128)(2,1)S(1)} collective-permute-done((bf16[128,512]{1,0:T(8,128)(2,1)S(1)}, bf16[128,512]{1,0:T(8,128)(2,1)S(1)}, u32[]{:S(2)}, u32[]{:S(2)}) %collective-permute-start.14) | collective-permute-done | bytes 131104 | tf_op jit(solution)/shard_map/ppermute | solution.py:323
  61.5 6.1 %collective-permute-done.13.refs_2_ = bf16[128,512]{1,0:T(8,128)(2,1)S(1)} collective-permute-done((bf16[128,512]{1,0:T(8,128)(2,1)S(1)}, bf16[128,512]{1,0:T(8,128)(2,1)S(1)}, u32[]{:S(2)}, u32[]{:S(2)}) %collective-permute-start.13) | collective-permute-done | bytes 131104 | tf_op jit(solution)/shard_map/ppermute | solution.py:323
  70.5 2.9 %collective-permute-done.18.rest_0_ = bf16[64,1024]{1,0:T(8,128)(2,1)S(1)} collective-permute-done((bf16[64,1024]{1,0:T(8,128)(2,1)S(1)}, bf16[64,1024]{1,0:T(8,128)(2,1)S(1)}, u32[]{:S(2)}, u32[]{:S(2)}) %collective-permute-start.18) | collective-permute-done | bytes 131104 | tf_op jit(solution)/shard_map/ppermute | solution.py:323
  75.7 3.2 %collective-permute-done.19 = bf16[64,1024]{1,0:T(8,128)(2,1)S(1)} collective-permute-done((bf16[64,1024]{1,0:T(8,128)(2,1)S(1)}, bf16[64,1024]{1,0:T(8,128)(2,1)S(1)}, u32[]{:S(2)}, u32[]{:S(2)}) %collective-permute-start.19) | collective-permute-done | bytes 131104 | tf_op jit(solution)/shard_map/ppermute | solution.py:323
  82.5 5.4 %collective-permute-done.24.refs_3_ = bf16[2,64,1024]{2,1,0:T(8,128)(2,1)S(1)} collective-permute-done((bf16[2,64,1024]{2,1,0:T(8,128)(2,1)S(1)}, bf16[2,64,1024]{2,1,0:T(8,128)(2,1)S(1)}, u32[]{:S(2)}, u32[]{:S(2)}) %collective-permute-start.24) | collective-permute-done | bytes 262176 | tf_op jit(solution)/shard_map/ppermute | solution.py:323
  88.0 2.8 %collective-permute-done.23.refs_2_ = bf16[2,64,1024]{2,1,0:T(8,128)(2,1)S(1)} collective-permute-done((bf16[2,64,1024]{2,1,0:T(8,128)(2,1)S(1)}, bf16[2,64,1024]{2,1,0:T(8,128)(2,1)S(1)}, u32[]{:S(2)}, u32[]{:S(2)}) %collective-permute-start.23) | collective-permute-done | bytes 262176 | tf_op jit(solution)/shard_map/ppermute | solution.py:323
  90.8 2.1 front.3
  96.2 2.3 attention_forward.3
  98.5 3.6 %attention_backward.2 = (f32[512,128]{1,0:T(8,128)S(1)}, f32[2,512,128]{2,1,0:T(8,128)S(1)}, f32[2,512,128]{2,1,0:T(8,128)S(1)}) custom-call(s32[8]{0:T(128)S(1)} %stack.91.at, bf16[512,128]{1,0:T(8,128)(2,1)S(1)} %get-tuple-element.193.q, bf16[2,512,128]{2,1,0:T(8,128)(2,1)S(1)} %get-tuple-element.194.kv, ...), custom_call_target="tpu_custom_call" | custom-call | tf_op jit(solution)/shard_map/attention_backward/pallas_call | solution.py:347
  102.7 2.1 early_grads.2
  104.9 2.8 %inputs_backward.2 = (bf16[512,384]{1,0:T(8,128)(2,1)S(1)}, bf16[64,128]{1,0:T(8,128)(2,1)S(1)}, f32[2,64,1024]{2,1,0:T(8,128)S(1)}, bf16[2,64,1024]{2,1,0:T(8,1...) custom-call(s32[8]{0:T(128)S(1)} %stack.91.at, ...), custom_call_target="tpu_custom_call" | custom-call | tf_op jit(solution)/shard_map/inputs_backward/pallas_call | solution.py:347
  115.7 10.1 %collective-permute-done.28 = bf16[1152,128]{1,0:T(8,128)(2,1)S(1)} collective-permute-done((bf16[1152,128]{1,0:T(8,128)(2,1)S(1)}, bf16[1152,128]{1,0:T(8,128)(2,1)S(1)}, u32[]{:S(2)}, u32[]{:S(2)}) %collective-permute-start.28) | collective-permute-done | bytes 294944 | tf_op jit(solution)/shard_map/ppermute | solution.py:323
  134.7 6.6 %collective-permute-done.35 = bf16[2,384,128]{2,1,0:T(8,128)(2,1)S(1)} collective-permute-done((bf16[2,384,128]{2,1,0:T(8,128)(2,1)S(1)}, bf16[2,384,128]{2,1,0:T(8,128)(2,1)S(1)}, u32[]{:S(2)}, u32[]{:S(2)}) %collective-permute-start.35) | collective-permute-done | bytes 196640 | tf_op jit(solution)/shard_map/ppermute | solution.py:323
  141.6 2.0 collective-permute-start.39
  147.2 9.1 %collective-permute-done.39 = bf16[1152,128]{1,0:T(8,128)(2,1)S(1)} collective-permute-done((bf16[1152,128]{1,0:T(8,128)(2,1)S(1)}, bf16[1152,128]{1,0:T(8,128)(2,1)S(1)}, u32[]{:S(2)}, u32[]{:S(2)}) %collective-permute-start.39) | collective-permute-done | bytes 294944 | tf_op jit(solution)/shard_map/ppermute | solution.py:323
  158.3 2.1 early_grads.3
  160.5 3.6 %attention_backward.3 = (f32[512,128]{1,0:T(8,128)S(1)}, f32[2,512,128]{2,1,0:T(8,128)S(1)}, f32[2,512,128]{2,1,0:T(8,128)S(1)}) custom-call(s32[8]{0:T(128)S(1)} %stack.91.at, bf16[512,128]{1,0:T(8,128)(2,1)S(1)} %get-tuple-element.158.q, bf16[2,512,128]{2,1,0:T(8,128)(2,1)S(1)} %get-tuple-element.159.kv, ...), custom_call_target="tpu_custom_call" | custom-call | tf_op jit(solution)/shard_map/attention_backward/pallas_call | solution.py:347
  165.9 2.3 collective-permute-start.46
  168.2 2.6 %inputs_backward.3 = (bf16[512,384]{1,0:T(8,128)(2,1)S(1)}, bf16[64,128]{1,0:T(8,128)(2,1)S(1)}, f32[2,64,1024]{2,1,0:T(8,128)S(1)}, bf16[2,64,1024]{2,1,0:T(8,1...) custom-call(s32[8]{0:T(128)S(1)} %stack.91.at, ...), custom_call_target="tpu_custom_call" | custom-call | tf_op jit(solution)/shard_map/inputs_backward/pallas_call | solution.py:347
  170.7 2.0 collective-permute-done.45.rest_0_
  178.5 3.4 %collective-permute-done.46 = bf16[1152,128]{1,0:T(8,128)(2,1)S(1)} collective-permute-done((bf16[1152,128]{1,0:T(8,128)(2,1)S(1)}, bf16[1152,128]{1,0:T(8,128)(2,1)S(1)}, u32[]{:S(2)}, u32[]{:S(2)}) %collective-permute-start.46) | collective-permute-done | bytes 294944 | tf_op jit(solution)/shard_map/ppermute | solution.py:323
  182.9 3.3 %collective-permute-done.48.refs_2_ = bf16[2,64,1024]{2,1,0:T(8,128)(2,1)S(1)} collective-permute-done((bf16[2,64,1024]{2,1,0:T(8,128)(2,1)S(1)}, bf16[2,64,1024]{2,1,0:T(8,128)(2,1)S(1)}, u32[]{:S(2)}, u32[]{:S(2)}) %collective-permute-start.48) | collective-permute-done | bytes 262176 | tf_op jit(solution)/shard_map/ppermute | solution.py:323
  187.3 2.1 collective-permute-start.60
  189.4 2.6 %collective-permute-start.51 = (bf16[1152,128]{1,0:T(8,128)(2,1)S(1)}, bf16[1152,128]{1,0:T(8,128)(2,1)S(1)}, u32[]{:S(2)}, u32[]{:S(2)}) collective-permute-start(bf16[1152,128]{1,0:T(8,128)(2,1)S(1)} %get-tuple-element.261), channel_id=1, source_target_pairs={{0,8},{1,9},{2,10},{3,11},{4,12},{5,13},{6,14},{7,15},{8,0},{9,1},... | collective-permute-start | bytes 884744 | tf_op jit(solution)/shard_map/ppermute | solution.py:323
  192.5 12.8 %collective-permute-done.50.rest_0_ = bf16[64,1024]{1,0:T(8,128)(2,1)S(1)} collective-permute-done((bf16[64,1024]{1,0:T(8,128)(2,1)S(1)}, bf16[64,1024]{1,0:T(8,128)(2,1)S(1)}, u32[]{:S(2)}, u32[]{:S(2)}) %collective-permute-start.50) | collective-permute-done | bytes 131104 | tf_op jit(solution)/shard_map/ppermute | solution.py:323
  205.3 4.4 %collective-permute-done.51 = bf16[1152,128]{1,0:T(8,128)(2,1)S(1)} collective-permute-done((bf16[1152,128]{1,0:T(8,128)(2,1)S(1)}, bf16[1152,128]{1,0:T(8,128)(2,1)S(1)}, u32[]{:S(2)}, u32[]{:S(2)}) %collective-permute-start.51) | collective-permute-done | bytes 294944 | tf_op jit(solution)/shard_map/ppermute | solution.py:323
  213.1 4.1 %collective-permute-done.52 = bf16[64,1024]{1,0:T(8,128)(2,1)S(1)} collective-permute-done((bf16[64,1024]{1,0:T(8,128)(2,1)S(1)}, bf16[64,1024]{1,0:T(8,128)(2,1)S(1)}, u32[]{:S(2)}, u32[]{:S(2)}) %collective-permute-start.52) | collective-permute-done | bytes 131104 | tf_op jit(solution)/shard_map/ppermute | solution.py:323
  217.2 3.4 %collective-permute-start.53 = (bf16[2,64,1024]{2,1,0:T(8,128)(2,1)S(1)}, bf16[2,64,1024]{2,1,0:T(8,128)(2,1)S(1)}, u32[]{:S(2)}, u32[]{:S(2)}) collective-permute-start(bf16[2,64,1024]{2,1,0:T(8,128)(2,1)S(1)} %pad_maximum_fusion.3), channel_id=1, source_target_pairs={{0,8},{1,9},{2,10},{3,11},{4,12},{5,13},{6,14},{7,15},{8,0},{9,1},... | collective-permute-start | bytes 786440 | tf_op jit(solution)/shard_map/ppermute | solution.py:323
  222.3 3.7 %collective-permute-start.62 = (bf16[448,128]{1,0:T(8,128)(2,1)S(1)}, bf16[448,128]{1,0:T(8,128)(2,1)S(1)}, u32[]{:S(2)}, u32[]{:S(2)}) collective-permute-start(bf16[448,128]{1,0:T(8,128)(2,1)S(1)} %get-tuple-element.318), channel_id=1, source_target_pairs={{0,20},{1,21},{2,22},{3,23},{4,16},{5,17},{6,18},{7,19},{8,28},{9,... | collective-permute-start | bytes 344072 | tf_op jit(solution)/shard_map/ppermute | solution.py:323
  225.9 2.7 %collective-permute-done.53 = bf16[2,64,1024]{2,1,0:T(8,128)(2,1)S(1)} collective-permute-done((bf16[2,64,1024]{2,1,0:T(8,128)(2,1)S(1)}, bf16[2,64,1024]{2,1,0:T(8,128)(2,1)S(1)}, u32[]{:S(2)}, u32[]{:S(2)}) %collective-permute-start.53) | collective-permute-done | bytes 262176 | tf_op jit(solution)/shard_map/ppermute | solution.py:323
  231.3 2.1 collective-permute-start.63
  233.5 2.5 %unpack_grads.1 = (f32[3,128,512]{2,1,0:T(8,128)}, f32[512,128]{1,0:T(8,128)}, f32[128,2048]{1,0:T(8,128)}, f32[2048,128]{1,0:T(8,128)}, f32[3,512]{1,0:T(4,128)...) custom-call(s32[8]{0:T(128)S(1)} %stack.91.at, bf16[1152,128]{1,0:T(8,128)(2,1)S(1)} %get-tuple-element.299.refs_0_, ...), custom_call_target="tpu_custom_call" | custom-call | tf_op jit(solution)/shard_map/unpack_grads/pallas_call | solution.py:347
  (167 shorter events, 74.1 us)
Async XLA Ops:
  2.6 12.4 %collective-permute-start.5 = (bf16[1584,128]{1,0:T(8,128)(2,1)S(1)}, bf16[1584,128]{1,0:T(8,128)(2,1)S(1)}, u32[]{:S(2)}, u32[]{:S(2)}) collective-permute-start(bf16[1584,128]{1,0:T(8,128)(2,1)S(1)} %get-tuple-element.154), channel_id=1, source_target_pairs={{0,16},{1,17},{2,18},{3,19},{4,20},{5,21},{6,22},{7,23},{8,24},{9,... | collective-permute-start | bytes 1216520 | tf_op jit(solution)/shard_map/ppermute | solution.py:323
  5.6 13.5 %collective-permute-start.2 = (bf16[128,512]{1,0:T(8,128)(2,1)S(1)}, bf16[128,512]{1,0:T(8,128)(2,1)S(1)}, u32[]{:S(2)}, u32[]{:S(2)}) collective-permute-start(bf16[128,512]{1,0:T(8,128)(2,1)S(1)} %get-tuple-element.151), channel_id=1, source_target_pairs={{0,12},{1,13},{2,14},{3,15},{4,8},{5,9},{6,10},{7,11},{8,4},{9,5},... | collective-permute-start | bytes 393224 | tf_op jit(solution)/shard_map/ppermute | solution.py:323
  9.2 11.5 %collective-permute-start.1 = (bf16[128,512]{1,0:T(8,128)(2,1)S(1)}, bf16[128,512]{1,0:T(8,128)(2,1)S(1)}, u32[]{:S(2)}, u32[]{:S(2)}) collective-permute-start(bf16[128,512]{1,0:T(8,128)(2,1)S(1)} %get-tuple-element.151), channel_id=1, source_target_pairs={{0,8},{1,9},{2,10},{3,11},{4,12},{5,13},{6,14},{7,15},{8,0},{9,1},... | collective-permute-start | bytes 393224 | tf_op jit(solution)/shard_map/ppermute | solution.py:323
  9.3 20.2 %collective-permute-start = (bf16[128,1024]{1,0:T(8,128)(2,1)S(1)}, bf16[128,1024]{1,0:T(8,128)(2,1)S(1)}, u32[]{:S(2)}, u32[]{:S(2)}) collective-permute-start(bf16[128,1024]{1,0:T(8,128)(2,1)S(1)} %get-tuple-element.150.refs_0_), channel_id=1, source_target_pairs={{0,4},{1,5},{2,6},{3,7},{4,0},{5,1},{6,2},{7,3},{8,12},{9,13},{10,... | collective-permute-start | bytes 786440 | tf_op jit(solution)/shard_map/ppermute | solution.py:323
  15.0 13.1 %collective-permute-start.8 = (bf16[512,512]{1,0:T(8,128)(2,1)S(1)}, bf16[512,512]{1,0:T(8,128)(2,1)S(1)}, u32[]{:S(2)}, u32[]{:S(2)}) collective-permute-start(bf16[512,512]{1,0:T(8,128)(2,1)S(1)} %get-tuple-element.163), channel_id=1, source_target_pairs={{0,16},{1,17},{2,18},{3,19},{4,20},{5,21},{6,22},{7,23},{8,24},{9,... | collective-permute-start | bytes 1572872 | tf_op jit(solution)/shard_map/ppermute | solution.py:323
  19.1 6.4 %collective-permute-start.4 = (bf16[128,512]{1,0:T(8,128)(2,1)S(1)}, bf16[128,512]{1,0:T(8,128)(2,1)S(1)}, u32[]{:S(2)}, u32[]{:S(2)}) collective-permute-start(bf16[128,512]{1,0:T(8,128)(2,1)S(1)} %collective-permute-done.2.refs_3_), channel_id=1, source_target_pairs={{0,1},{1,0},{2,3},{3,2},{4,5},{5,4},{6,7},{7,6},{8,9},{9,8},{10,11... | collective-permute-start | bytes 393224 | tf_op jit(solution)/shard_map/ppermute | solution.py:323
  20.7 7.2 %collective-permute-start.3 = (bf16[128,512]{1,0:T(8,128)(2,1)S(1)}, bf16[128,512]{1,0:T(8,128)(2,1)S(1)}, u32[]{:S(2)}, u32[]{:S(2)}) collective-permute-start(bf16[128,512]{1,0:T(8,128)(2,1)S(1)} %collective-permute-done.1.refs_2_), channel_id=1, source_target_pairs={{0,1},{1,0},{2,3},{3,2},{4,5},{5,4},{6,7},{7,6},{8,9},{9,8},{10,11... | collective-permute-start | bytes 393224 | tf_op jit(solution)/shard_map/ppermute | solution.py:323
  28.1 16.2 %collective-permute-start.10 = (bf16[320,1024]{1,0:T(8,128)(2,1)S(1)}, bf16[320,1024]{1,0:T(8,128)(2,1)S(1)}, u32[]{:S(2)}, u32[]{:S(2)}) collective-permute-start(bf16[320,1024]{1,0:T(8,128)(2,1)S(1)} %get-tuple-element.168), channel_id=1, source_target_pairs={{0,16},{1,17},{2,18},{3,19},{4,20},{5,21},{6,22},{7,23},{8,24},{9,... | collective-permute-start | bytes 1966088 | tf_op jit(solution)/shard_map/ppermute | solution.py:323
  32.2 8.3 %collective-permute-start.11 = (bf16[128,1024]{1,0:T(8,128)(2,1)S(1)}, bf16[128,1024]{1,0:T(8,128)(2,1)S(1)}, u32[]{:S(2)}, u32[]{:S(2)}) collective-permute-start(bf16[128,1024]{1,0:T(8,128)(2,1)S(1)} %get-tuple-element.170.refs_0_), channel_id=1, source_target_pairs={{0,4},{1,5},{2,6},{3,7},{4,0},{5,1},{6,2},{7,3},{8,12},{9,13},{10,... | collective-permute-start | bytes 786440 | tf_op jit(solution)/shard_map/ppermute | solution.py:323
  49.9 17.7 %collective-permute-start.15 = (bf16[2,64,1024]{2,1,0:T(8,128)(2,1)S(1)}, bf16[2,64,1024]{2,1,0:T(8,128)(2,1)S(1)}, u32[]{:S(2)}, u32[]{:S(2)}) collective-permute-start(bf16[2,64,1024]{2,1,0:T(8,128)(2,1)S(1)} %get-tuple-element.178), channel_id=1, source_target_pairs={{0,1},{1,0},{2,3},{3,2},{4,5},{5,4},{6,7},{7,6},{8,9},{9,8},{10,11... | collective-permute-start | bytes 786440 | tf_op jit(solution)/shard_map/ppermute | solution.py:323
  51.5 16.1 %collective-permute-start.16 = (bf16[2,64,1024]{2,1,0:T(8,128)(2,1)S(1)}, bf16[2,64,1024]{2,1,0:T(8,128)(2,1)S(1)}, u32[]{:S(2)}, u32[]{:S(2)}) collective-permute-start(bf16[2,64,1024]{2,1,0:T(8,128)(2,1)S(1)} %get-tuple-element.179), channel_id=1, source_target_pairs={{0,16},{1,17},{2,18},{3,19},{4,20},{5,21},{6,22},{7,23},{8,24},{9,... | collective-permute-start | bytes 786440 | tf_op jit(solution)/shard_map/ppermute | solution.py:323
  52.0 15.6 %collective-permute-start.17 = (bf16[2,64,1024]{2,1,0:T(8,128)(2,1)S(1)}, bf16[2,64,1024]{2,1,0:T(8,128)(2,1)S(1)}, u32[]{:S(2)}, u32[]{:S(2)}) collective-permute-start(bf16[2,64,1024]{2,1,0:T(8,128)(2,1)S(1)} %get-tuple-element.180), channel_id=1, source_target_pairs={{0,17},{1,16},{2,19},{3,18},{4,21},{5,20},{6,23},{7,22},{8,25},{9,... | collective-permute-start | bytes 786440 | tf_op jit(solution)/shard_map/ppermute | solution.py:323
  53.5 8.1 %collective-permute-start.14 = (bf16[128,512]{1,0:T(8,128)(2,1)S(1)}, bf16[128,512]{1,0:T(8,128)(2,1)S(1)}, u32[]{:S(2)}, u32[]{:S(2)}) collective-permute-start(bf16[128,512]{1,0:T(8,128)(2,1)S(1)} %get-tuple-element.176), channel_id=1, source_target_pairs={{0,12},{1,13},{2,14},{3,15},{4,8},{5,9},{6,10},{7,11},{8,4},{9,5},... | collective-permute-start | bytes 393224 | tf_op jit(solution)/shard_map/ppermute | solution.py:323
  57.1 10.5 %collective-permute-start.13 = (bf16[128,512]{1,0:T(8,128)(2,1)S(1)}, bf16[128,512]{1,0:T(8,128)(2,1)S(1)}, u32[]{:S(2)}, u32[]{:S(2)}) collective-permute-start(bf16[128,512]{1,0:T(8,128)(2,1)S(1)} %get-tuple-element.176), channel_id=1, source_target_pairs={{0,8},{1,9},{2,10},{3,11},{4,12},{5,13},{6,14},{7,15},{8,0},{9,1},... | collective-permute-start | bytes 393224 | tf_op jit(solution)/shard_map/ppermute | solution.py:323
  79.0 9.0 %collective-permute-start.24 = (bf16[2,64,1024]{2,1,0:T(8,128)(2,1)S(1)}, bf16[2,64,1024]{2,1,0:T(8,128)(2,1)S(1)}, u32[]{:S(2)}, u32[]{:S(2)}) collective-permute-start(bf16[2,64,1024]{2,1,0:T(8,128)(2,1)S(1)} %pad_maximum_fusion.1.refs_0_), channel_id=1, source_target_pairs={{0,17},{1,16},{2,19},{3,18},{4,21},{5,20},{6,23},{7,22},{8,25},{9,... | collective-permute-start | bytes 786440 | tf_op jit(solution)/shard_map/ppermute | solution.py:323
  80.6 10.3 %collective-permute-start.23 = (bf16[2,64,1024]{2,1,0:T(8,128)(2,1)S(1)}, bf16[2,64,1024]{2,1,0:T(8,128)(2,1)S(1)}, u32[]{:S(2)}, u32[]{:S(2)}) collective-permute-start(bf16[2,64,1024]{2,1,0:T(8,128)(2,1)S(1)} %pad_maximum_fusion.1.refs_0_), channel_id=1, source_target_pairs={{0,16},{1,17},{2,18},{3,19},{4,20},{5,21},{6,22},{7,23},{8,24},{9,... | collective-permute-start | bytes 786440 | tf_op jit(solution)/shard_map/ppermute | solution.py:323
  82.0 8.8 %collective-permute-start.22 = (bf16[2,64,1024]{2,1,0:T(8,128)(2,1)S(1)}, bf16[2,64,1024]{2,1,0:T(8,128)(2,1)S(1)}, u32[]{:S(2)}, u32[]{:S(2)}) collective-permute-start(bf16[2,64,1024]{2,1,0:T(8,128)(2,1)S(1)} %pad_maximum_fusion.1.refs_0_), channel_id=1, source_target_pairs={{0,1},{1,0},{2,3},{3,2},{4,5},{5,4},{6,7},{7,6},{8,9},{9,8},{10,11... | collective-permute-start | bytes 786440 | tf_op jit(solution)/shard_map/ppermute | solution.py:323
  108.9 6.7 %collective-permute-start.34 = (bf16[2,2,384,128]{3,2,1,0:T(8,128)(2,1)S(1)}, bf16[2,2,384,128]{3,2,1,0:T(8,128)(2,1)S(1)}, u32[]{:S(2)}, u32[]{:S(2)}) collective-permute-start(bf16[2,2,384,128]{3,2,1,0:T(8,128)(2,1)S(1)} %get-tuple-element.214), channel_id=1, source_target_pairs={{0,2},{1,3},{2,0},{3,1},{4,6},{5,7},{6,4},{7,5},{8,10},{9,11},{10,... | collective-permute-start | bytes 1179656 | tf_op jit(solution)/shard_map/ppermute | solution.py:323
  109.7 16.1 %collective-permute-start.28 = (bf16[1152,128]{1,0:T(8,128)(2,1)S(1)}, bf16[1152,128]{1,0:T(8,128)(2,1)S(1)}, u32[]{:S(2)}, u32[]{:S(2)}) collective-permute-start(bf16[1152,128]{1,0:T(8,128)(2,1)S(1)} %get-tuple-element.303), channel_id=1, source_target_pairs={{0,8},{1,9},{2,10},{3,11},{4,12},{5,13},{6,14},{7,15},{8,0},{9,1},... | collective-permute-start | bytes 884744 | tf_op jit(solution)/shard_map/ppermute | solution.py:323
  110.5 15.3 %collective-permute-start.29 = (bf16[2,64,1024]{2,1,0:T(8,128)(2,1)S(1)}, bf16[2,64,1024]{2,1,0:T(8,128)(2,1)S(1)}, u32[]{:S(2)}, u32[]{:S(2)}) collective-permute-start(bf16[2,64,1024]{2,1,0:T(8,128)(2,1)S(1)} %get-tuple-element.216), channel_id=1, source_target_pairs={{0,1},{1,0},{2,3},{3,2},{4,5},{5,4},{6,7},{7,6},{8,9},{9,8},{10,11... | collective-permute-start | bytes 786440 | tf_op jit(solution)/shard_map/ppermute | solution.py:323
  111.9 13.9 %collective-permute-start.30 = (bf16[2,64,1024]{2,1,0:T(8,128)(2,1)S(1)}, bf16[2,64,1024]{2,1,0:T(8,128)(2,1)S(1)}, u32[]{:S(2)}, u32[]{:S(2)}) collective-permute-start(bf16[2,64,1024]{2,1,0:T(8,128)(2,1)S(1)} %get-tuple-element.217), channel_id=1, source_target_pairs={{0,16},{1,17},{2,18},{3,19},{4,20},{5,21},{6,22},{7,23},{8,24},{9,... | collective-permute-start | bytes 786440 | tf_op jit(solution)/shard_map/ppermute | solution.py:323
  112.4 13.3 %collective-permute-start.31 = (bf16[2,64,1024]{2,1,0:T(8,128)(2,1)S(1)}, bf16[2,64,1024]{2,1,0:T(8,128)(2,1)S(1)}, u32[]{:S(2)}, u32[]{:S(2)}) collective-permute-start(bf16[2,64,1024]{2,1,0:T(8,128)(2,1)S(1)} %get-tuple-element.218), channel_id=1, source_target_pairs={{0,17},{1,16},{2,19},{3,18},{4,21},{5,20},{6,23},{7,22},{8,25},{9,... | collective-permute-start | bytes 786440 | tf_op jit(solution)/shard_map/ppermute | solution.py:323
  127.5 13.7 %collective-permute-start.36 = (bf16[2,64,1024]{2,1,0:T(8,128)(2,1)S(1)}, bf16[2,64,1024]{2,1,0:T(8,128)(2,1)S(1)}, u32[]{:S(2)}, u32[]{:S(2)}) collective-permute-start(bf16[2,64,1024]{2,1,0:T(8,128)(2,1)S(1)} %get-tuple-element.225), channel_id=1, source_target_pairs={{0,1},{1,0},{2,3},{3,2},{4,5},{5,4},{6,7},{7,6},{8,9},{9,8},{10,11... | collective-permute-start | bytes 786440 | tf_op jit(solution)/shard_map/ppermute | solution.py:323
  128.9 12.4 %collective-permute-start.37 = (bf16[2,64,1024]{2,1,0:T(8,128)(2,1)S(1)}, bf16[2,64,1024]{2,1,0:T(8,128)(2,1)S(1)}, u32[]{:S(2)}, u32[]{:S(2)}) collective-permute-start(bf16[2,64,1024]{2,1,0:T(8,128)(2,1)S(1)} %get-tuple-element.227), channel_id=1, source_target_pairs={{0,16},{1,17},{2,18},{3,19},{4,20},{5,21},{6,22},{7,23},{8,24},{9,... | collective-permute-start | bytes 786440 | tf_op jit(solution)/shard_map/ppermute | solution.py:323
  129.4 12.2 %collective-permute-start.38 = (bf16[2,64,1024]{2,1,0:T(8,128)(2,1)S(1)}, bf16[2,64,1024]{2,1,0:T(8,128)(2,1)S(1)}, u32[]{:S(2)}, u32[]{:S(2)}) collective-permute-start(bf16[2,64,1024]{2,1,0:T(8,128)(2,1)S(1)} %get-tuple-element.229), channel_id=1, source_target_pairs={{0,17},{1,16},{2,19},{3,18},{4,21},{5,20},{6,23},{7,22},{8,25},{9,... | collective-permute-start | bytes 786440 | tf_op jit(solution)/shard_map/ppermute | solution.py:323
  131.0 10.2 %collective-permute-start.35 = (bf16[2,384,128]{2,1,0:T(8,128)(2,1)S(1)}, bf16[2,384,128]{2,1,0:T(8,128)(2,1)S(1)}, u32[]{:S(2)}, u32[]{:S(2)}) collective-permute-start(bf16[2,384,128]{2,1,0:T(8,128)(2,1)S(1)} %pad_maximum_fusion.5), channel_id=1, source_target_pairs={{0,8},{1,9},{2,10},{3,11},{4,12},{5,13},{6,14},{7,15},{8,0},{9,1},... | collective-permute-start | bytes 589832 | tf_op jit(solution)/shard_map/ppermute | solution.py:323
  133.3 8.0 %collective-permute-start.33 = (bf16[64,1024]{1,0:T(8,128)(2,1)S(1)}, bf16[64,1024]{1,0:T(8,128)(2,1)S(1)}, u32[]{:S(2)}, u32[]{:S(2)}) collective-permute-start(bf16[64,1024]{1,0:T(8,128)(2,1)S(1)} %join_backward.2.g), channel_id=1, source_target_pairs={{0,4},{1,5},{2,6},{3,7},{4,0},{5,1},{6,2},{7,3},{8,12},{9,13},{10,... | collective-permute-start | bytes 393224 | tf_op jit(solution)/shard_map/ppermute | solution.py:323
  141.6 14.7 %collective-permute-start.39 = (bf16[1152,128]{1,0:T(8,128)(2,1)S(1)}, bf16[1152,128]{1,0:T(8,128)(2,1)S(1)}, u32[]{:S(2)}, u32[]{:S(2)}) collective-permute-start(bf16[1152,128]{1,0:T(8,128)(2,1)S(1)} %get-tuple-element.231), channel_id=1, source_target_pairs={{0,8},{1,9},{2,10},{3,11},{4,12},{5,13},{6,14},{7,15},{8,0},{9,1},... | collective-permute-start | bytes 884744 | tf_op jit(solution)/shard_map/ppermute | solution.py:323
  143.6 12.7 %collective-permute-start.42 = (bf16[2,64,1024]{2,1,0:T(8,128)(2,1)S(1)}, bf16[2,64,1024]{2,1,0:T(8,128)(2,1)S(1)}, u32[]{:S(2)}, u32[]{:S(2)}) collective-permute-start(bf16[2,64,1024]{2,1,0:T(8,128)(2,1)S(1)} %pad_maximum_fusion.2.refs_0_), channel_id=1, source_target_pairs={{0,17},{1,16},{2,19},{3,18},{4,21},{5,20},{6,23},{7,22},{8,25},{9,... | collective-permute-start | bytes 786440 | tf_op jit(solution)/shard_map/ppermute | solution.py:323
  145.1 11.6 %collective-permute-start.41 = (bf16[2,64,1024]{2,1,0:T(8,128)(2,1)S(1)}, bf16[2,64,1024]{2,1,0:T(8,128)(2,1)S(1)}, u32[]{:S(2)}, u32[]{:S(2)}) collective-permute-start(bf16[2,64,1024]{2,1,0:T(8,128)(2,1)S(1)} %pad_maximum_fusion.2.refs_0_), channel_id=1, source_target_pairs={{0,16},{1,17},{2,18},{3,19},{4,20},{5,21},{6,22},{7,23},{8,24},{9,... | collective-permute-start | bytes 786440 | tf_op jit(solution)/shard_map/ppermute | solution.py:323
  146.5 10.2 %collective-permute-start.40 = (bf16[2,64,1024]{2,1,0:T(8,128)(2,1)S(1)}, bf16[2,64,1024]{2,1,0:T(8,128)(2,1)S(1)}, u32[]{:S(2)}, u32[]{:S(2)}) collective-permute-start(bf16[2,64,1024]{2,1,0:T(8,128)(2,1)S(1)} %pad_maximum_fusion.2.refs_0_), channel_id=1, source_target_pairs={{0,1},{1,0},{2,3},{3,2},{4,5},{5,4},{6,7},{7,6},{8,9},{9,8},{10,11... | collective-permute-start | bytes 786440 | tf_op jit(solution)/shard_map/ppermute | solution.py:323
  165.3 7.4 %collective-permute-start.45 = (bf16[64,1024]{1,0:T(8,128)(2,1)S(1)}, bf16[64,1024]{1,0:T(8,128)(2,1)S(1)}, u32[]{:S(2)}, u32[]{:S(2)}) collective-permute-start(bf16[64,1024]{1,0:T(8,128)(2,1)S(1)} %get-tuple-element.250), channel_id=1, source_target_pairs={{0,4},{1,5},{2,6},{3,7},{4,0},{5,1},{6,2},{7,3},{8,12},{9,13},{10,... | collective-permute-start | bytes 393224 | tf_op jit(solution)/shard_map/ppermute | solution.py:323
  165.9 16.0 %collective-permute-start.46 = (bf16[1152,128]{1,0:T(8,128)(2,1)S(1)}, bf16[1152,128]{1,0:T(8,128)(2,1)S(1)}, u32[]{:S(2)}, u32[]{:S(2)}) collective-permute-start(bf16[1152,128]{1,0:T(8,128)(2,1)S(1)} %get-tuple-element.300), channel_id=1, source_target_pairs={{0,8},{1,9},{2,10},{3,11},{4,12},{5,13},{6,14},{7,15},{8,0},{9,1},... | collective-permute-start | bytes 884744 | tf_op jit(solution)/shard_map/ppermute | solution.py:323
  172.7 10.2 %collective-permute-start.49 = (bf16[2,64,1024]{2,1,0:T(8,128)(2,1)S(1)}, bf16[2,64,1024]{2,1,0:T(8,128)(2,1)S(1)}, u32[]{:S(2)}, u32[]{:S(2)}) collective-permute-start(bf16[2,64,1024]{2,1,0:T(8,128)(2,1)S(1)} %get-tuple-element.258), channel_id=1, source_target_pairs={{0,17},{1,16},{2,19},{3,18},{4,21},{5,20},{6,23},{7,22},{8,25},{9,... | collective-permute-start | bytes 786440 | tf_op jit(solution)/shard_map/ppermute | solution.py:323
  174.1 12.1 %collective-permute-start.48 = (bf16[2,64,1024]{2,1,0:T(8,128)(2,1)S(1)}, bf16[2,64,1024]{2,1,0:T(8,128)(2,1)S(1)}, u32[]{:S(2)}, u32[]{:S(2)}) collective-permute-start(bf16[2,64,1024]{2,1,0:T(8,128)(2,1)S(1)} %get-tuple-element.256), channel_id=1, source_target_pairs={{0,16},{1,17},{2,18},{3,19},{4,20},{5,21},{6,22},{7,23},{8,24},{9,... | collective-permute-start | bytes 786440 | tf_op jit(solution)/shard_map/ppermute | solution.py:323
  175.7 10.6 %collective-permute-start.47 = (bf16[2,64,1024]{2,1,0:T(8,128)(2,1)S(1)}, bf16[2,64,1024]{2,1,0:T(8,128)(2,1)S(1)}, u32[]{:S(2)}, u32[]{:S(2)}) collective-permute-start(bf16[2,64,1024]{2,1,0:T(8,128)(2,1)S(1)} %get-tuple-element.254), channel_id=1, source_target_pairs={{0,1},{1,0},{2,3},{3,2},{4,5},{5,4},{6,7},{7,6},{8,9},{9,8},{10,11... | collective-permute-start | bytes 786440 | tf_op jit(solution)/shard_map/ppermute | solution.py:323
  178.5 13.5 %collective-permute-start.55 = (bf16[2,2,512,128]{3,2,1,0:T(8,128)(2,1)S(1)}, bf16[2,2,512,128]{3,2,1,0:T(8,128)(2,1)S(1)}, u32[]{:S(2)}, u32[]{:S(2)}) collective-permute-start(bf16[2,2,512,128]{3,2,1,0:T(8,128)(2,1)S(1)} %get-tuple-element.271), channel_id=1, source_target_pairs={{0,2},{1,3},{2,0},{3,1},{4,6},{5,7},{6,4},{7,5},{8,10},{9,11},{10,... | collective-permute-start | bytes 1572872 | tf_op jit(solution)/shard_map/ppermute | solution.py:323
  186.9 18.4 %collective-permute-start.50 = (bf16[64,1024]{1,0:T(8,128)(2,1)S(1)}, bf16[64,1024]{1,0:T(8,128)(2,1)S(1)}, u32[]{:S(2)}, u32[]{:S(2)}) collective-permute-start(bf16[64,1024]{1,0:T(8,128)(2,1)S(1)} %get-tuple-element.260), channel_id=1, source_target_pairs={{0,4},{1,5},{2,6},{3,7},{4,0},{5,1},{6,2},{7,3},{8,12},{9,13},{10,... | collective-permute-start | bytes 393224 | tf_op jit(solution)/shard_map/ppermute | solution.py:323
  187.3 34.9 %collective-permute-start.60 = (bf16[1152,128]{1,0:T(8,128)(2,1)S(1)}, bf16[1152,128]{1,0:T(8,128)(2,1)S(1)}, u32[]{:S(2)}, u32[]{:S(2)}) collective-permute-start(bf16[1152,128]{1,0:T(8,128)(2,1)S(1)} %get-tuple-element.296), channel_id=1, source_target_pairs={{0,20},{1,21},{2,22},{3,23},{4,16},{5,17},{6,18},{7,19},{8,28},{9,... | collective-permute-start | bytes 884744 | tf_op jit(solution)/shard_map/ppermute | solution.py:323
  189.3 32.8 %collective-permute-start.59 = (bf16[1152,128]{1,0:T(8,128)(2,1)S(1)}, bf16[1152,128]{1,0:T(8,128)(2,1)S(1)}, u32[]{:S(2)}, u32[]{:S(2)}) collective-permute-start(bf16[1152,128]{1,0:T(8,128)(2,1)S(1)} %get-tuple-element.297), channel_id=1, source_target_pairs={{0,4},{1,5},{2,6},{3,7},{4,0},{5,1},{6,2},{7,3},{8,12},{9,13},{10,... | collective-permute-start | bytes 884744 | tf_op jit(solution)/shard_map/ppermute | solution.py:323
  189.4 20.3 %collective-permute-start.51 = (bf16[1152,128]{1,0:T(8,128)(2,1)S(1)}, bf16[1152,128]{1,0:T(8,128)(2,1)S(1)}, u32[]{:S(2)}, u32[]{:S(2)}) collective-permute-start(bf16[1152,128]{1,0:T(8,128)(2,1)S(1)} %get-tuple-element.261), channel_id=1, source_target_pairs={{0,8},{1,9},{2,10},{3,11},{4,12},{5,13},{6,14},{7,15},{8,0},{9,1},... | collective-permute-start | bytes 884744 | tf_op jit(solution)/shard_map/ppermute | solution.py:323
  192.1 28.6 %collective-permute-start.56 = (bf16[2,512,128]{2,1,0:T(8,128)(2,1)S(1)}, bf16[2,512,128]{2,1,0:T(8,128)(2,1)S(1)}, u32[]{:S(2)}, u32[]{:S(2)}) collective-permute-start(bf16[2,512,128]{2,1,0:T(8,128)(2,1)S(1)} %pad_maximum_fusion.4), channel_id=1, source_target_pairs={{0,8},{1,9},{2,10},{3,11},{4,12},{5,13},{6,14},{7,15},{8,0},{9,1},... | collective-permute-start | bytes 786440 | tf_op jit(solution)/shard_map/ppermute | solution.py:323
  210.6 6.5 %collective-permute-start.52 = (bf16[64,1024]{1,0:T(8,128)(2,1)S(1)}, bf16[64,1024]{1,0:T(8,128)(2,1)S(1)}, u32[]{:S(2)}, u32[]{:S(2)}) collective-permute-start(bf16[64,1024]{1,0:T(8,128)(2,1)S(1)} %broadcast_select_fusion.4), channel_id=1, source_target_pairs={{0,16},{1,17},{2,18},{3,19},{4,20},{5,21},{6,22},{7,23},{8,24},{9,... | collective-permute-start | bytes 393224 | tf_op jit(solution)/shard_map/ppermute | solution.py:323
  212.2 10.0 %collective-permute-start.58 = (bf16[1152,128]{1,0:T(8,128)(2,1)S(1)}, bf16[1152,128]{1,0:T(8,128)(2,1)S(1)}, u32[]{:S(2)}, u32[]{:S(2)}) collective-permute-start(bf16[1152,128]{1,0:T(8,128)(2,1)S(1)} %get-tuple-element.298), channel_id=1, source_target_pairs={{0,16},{1,17},{2,18},{3,19},{4,20},{5,21},{6,22},{7,23},{8,24},{9,... | collective-permute-start | bytes 884744 | tf_op jit(solution)/shard_map/ppermute | solution.py:323
  217.2 11.5 %collective-permute-start.53 = (bf16[2,64,1024]{2,1,0:T(8,128)(2,1)S(1)}, bf16[2,64,1024]{2,1,0:T(8,128)(2,1)S(1)}, u32[]{:S(2)}, u32[]{:S(2)}) collective-permute-start(bf16[2,64,1024]{2,1,0:T(8,128)(2,1)S(1)} %pad_maximum_fusion.3), channel_id=1, source_target_pairs={{0,8},{1,9},{2,10},{3,11},{4,12},{5,13},{6,14},{7,15},{8,0},{9,1},... | collective-permute-start | bytes 786440 | tf_op jit(solution)/shard_map/ppermute | solution.py:323
  220.8 9.5 %collective-permute-start.57 = (bf16[448,128]{1,0:T(8,128)(2,1)S(1)}, bf16[448,128]{1,0:T(8,128)(2,1)S(1)}, u32[]{:S(2)}, u32[]{:S(2)}) collective-permute-start(bf16[448,128]{1,0:T(8,128)(2,1)S(1)} %get-tuple-element.316), channel_id=1, source_target_pairs={{0,16},{1,17},{2,18},{3,19},{4,20},{5,21},{6,22},{7,23},{8,24},{9,... | collective-permute-start | bytes 344072 | tf_op jit(solution)/shard_map/ppermute | solution.py:323
  222.3 8.1 %collective-permute-start.62 = (bf16[448,128]{1,0:T(8,128)(2,1)S(1)}, bf16[448,128]{1,0:T(8,128)(2,1)S(1)}, u32[]{:S(2)}, u32[]{:S(2)}) collective-permute-start(bf16[448,128]{1,0:T(8,128)(2,1)S(1)} %get-tuple-element.318), channel_id=1, source_target_pairs={{0,20},{1,21},{2,22},{3,23},{4,16},{5,17},{6,18},{7,19},{8,28},{9,... | collective-permute-start | bytes 344072 | tf_op jit(solution)/shard_map/ppermute | solution.py:323
  228.8 8.8 %collective-permute-start.54 = (bf16[3,64,1024]{2,1,0:T(8,128)(2,1)S(1)}, bf16[3,64,1024]{2,1,0:T(8,128)(2,1)S(1)}, u32[]{:S(2)}, u32[]{:S(2)}) collective-permute-start(bf16[3,64,1024]{2,1,0:T(8,128)(2,1)S(1)} %pad_maximum_fusion), channel_id=1, source_target_pairs={{0,1},{1,0},{2,3},{3,2},{4,5},{5,4},{6,7},{7,6},{8,9},{9,8},{10,11... | collective-permute-start | bytes 1179656 | tf_op jit(solution)/shard_map/ppermute | solution.py:323
  (23 other events, 159.9 us)

commit v5 on v4

--- a/solution.py
+++ b/solution.py
@@ -1319,7 +1319,7 @@
     keep, give = fold(at, parts)
     close_first = swapped(after(early_give[0], give), HALF)
     late_keep, late_give = summed_cores(*late)
-    late_got = swapped(after(jnp.stack(late_give), give), HALF)
+    late_got = swapped(jnp.stack(late_give), HALF)
     back_last = join_backward(
         at, back, x_piece, [keep, after(swapped(give, NEAR), close_first)]
     )

time: 239 us -> 239 us (level)
  no operation moved by 1% of the time
where the time goes in v5:
time: 239 us
  waiting for transfers between devices  101 us (42%)
  starting transfers between devices  73.2 us (31%)
  Pallas kernels  56.1 us (23%)
  other arithmetic  5.05 us (2%)
    ppermute x64, waiting for transfers between devices, swapped(): return lax.ppermute(array, ALL, pairs)  101 us
    ppermute x64, starting transfers between devices, swapped(): return lax.ppermute(array, ALL, pairs)  73.2 us
    pallas_call x32, Pallas kernels, kernel_call(): pl.pallas_call(body, name=name, out_shape=[(pltpu.VMEM if keep else jax.S...  52.3 us
  transfers between devices with their start and end apart: 64, of which 32 were waited for; matrix products, arithmetic and copies ran while one was open for 2% of the time, Pallas kernels for 16%

profile of v5, /device:TPU:0, one launch (start us, length us, event | category | flops | bytes accessed | tf_op | source)
XLA Modules:
  0.0 239.0 jit_solution(8126632555383952427)
XLA Ops:
  0.8 1.8 pack_first.1
  2.6 3.0 %collective-permute-start.5 = (bf16[1584,128]{1,0:T(8,128)(2,1)S(1)}, bf16[1584,128]{1,0:T(8,128)(2,1)S(1)}, u32[]{:S(2)}, u32[]{:S(2)}) collective-permute-start(bf16[1584,128]{1,0:T(8,128)(2,1)S(1)} %get-tuple-element.153), channel_id=1, source_target_pairs={{0,16},{1,17},{2,18},{3,19},{4,20},{5,21},{6,22},{7,23},{8,24},{9,... | collective-permute-start | bytes 1216520 | tf_op jit(solution)/shard_map/ppermute | solution.py:323
  5.6 3.6 %collective-permute-start.2 = (bf16[128,512]{1,0:T(8,128)(2,1)S(1)}, bf16[128,512]{1,0:T(8,128)(2,1)S(1)}, u32[]{:S(2)}, u32[]{:S(2)}) collective-permute-start(bf16[128,512]{1,0:T(8,128)(2,1)S(1)} %get-tuple-element.150), channel_id=1, source_target_pairs={{0,12},{1,13},{2,14},{3,15},{4,8},{5,9},{6,10},{7,11},{8,4},{9,5},... | collective-permute-start | bytes 393224 | tf_op jit(solution)/shard_map/ppermute | solution.py:323
  10.1 2.0 pack_second.1
  12.1 2.9 %collective-permute-done.5.refs_7_.refs_1_ = bf16[1584,128]{1,0:T(8,128)(2,1)S(1)} collective-permute-done((bf16[1584,128]{1,0:T(8,128)(2,1)S(1)}, bf16[1584,128]{1,0:T(8,128)(2,1)S(1)}, u32[]{:S(2)}, u32[]{:S(2)}) %collective-permute-start.5) | collective-permute-done | bytes 405536 | tf_op jit(solution)/shard_map/ppermute | solution.py:323
  15.0 1.7 collective-permute-start.8
  17.3 1.8 negate_select_fusion.1
  22.3 1.8 choose_qkv.1
  25.5 2.4 %collective-permute-done.3.refs_4_ = bf16[128,512]{1,0:T(8,128)(2,1)S(1)} collective-permute-done((bf16[128,512]{1,0:T(8,128)(2,1)S(1)}, bf16[128,512]{1,0:T(8,128)(2,1)S(1)}, u32[]{:S(2)}, u32[]{:S(2)}) %collective-permute-start.3) | collective-permute-done | bytes 131104 | tf_op jit(solution)/shard_map/ppermute | solution.py:323
  29.5 2.0 front.2
  33.9 2.3 attention_forward.2
  36.3 1.9 choose_up.1
  40.4 3.8 %collective-permute-done.10.refs_2_ = bf16[320,1024]{1,0:T(8,128)(2,1)S(1)} collective-permute-done((bf16[320,1024]{1,0:T(8,128)(2,1)S(1)}, bf16[320,1024]{1,0:T(8,128)(2,1)S(1)}, u32[]{:S(2)}, u32[]{:S(2)}) %collective-permute-start.10) | collective-permute-done | bytes 655392 | tf_op jit(solution)/shard_map/ppermute | solution.py:323
  44.3 2.1 collective-permute-done.12.refs_3_
  46.4 1.9 choose_rows.1
  53.5 3.6 %collective-permute-start.14 = (bf16[128,512]{1,0:T(8,128)(2,1)S(1)}, bf16[128,512]{1,0:T(8,128)(2,1)S(1)}, u32[]{:S(2)}, u32[]{:S(2)}) collective-permute-start(bf16[128,512]{1,0:T(8,128)(2,1)S(1)} %get-tuple-element.175), channel_id=1, source_target_pairs={{0,12},{1,13},{2,14},{3,15},{4,8},{5,9},{6,10},{7,11},{8,4},{9,5},... | collective-permute-start | bytes 393224 | tf_op jit(solution)/shard_map/ppermute | solution.py:323
  57.1 4.5 %collective-permute-done.14.refs_3_ = bf16[128,512]{1,0:T(8,128)(2,1)S(1)} collective-permute-done((bf16[128,512]{1,0:T(8,128)(2,1)S(1)}, bf16[128,512]{1,0:T(8,128)(2,1)S(1)}, u32[]{:S(2)}, u32[]{:S(2)}) %collective-permute-start.14) | collective-permute-done | bytes 131104 | tf_op jit(solution)/shard_map/ppermute | solution.py:323
  61.5 6.1 %collective-permute-done.13.refs_2_ = bf16[128,512]{1,0:T(8,128)(2,1)S(1)} collective-permute-done((bf16[128,512]{1,0:T(8,128)(2,1)S(1)}, bf16[128,512]{1,0:T(8,128)(2,1)S(1)}, u32[]{:S(2)}, u32[]{:S(2)}) %collective-permute-start.13) | collective-permute-done | bytes 131104 | tf_op jit(solution)/shard_map/ppermute | solution.py:323
  70.5 2.9 %collective-permute-done.18.rest_0_ = bf16[64,1024]{1,0:T(8,128)(2,1)S(1)} collective-permute-done((bf16[64,1024]{1,0:T(8,128)(2,1)S(1)}, bf16[64,1024]{1,0:T(8,128)(2,1)S(1)}, u32[]{:S(2)}, u32[]{:S(2)}) %collective-permute-start.18) | collective-permute-done | bytes 131104 | tf_op jit(solution)/shard_map/ppermute | solution.py:323
  75.7 3.2 %collective-permute-done.19 = bf16[64,1024]{1,0:T(8,128)(2,1)S(1)} collective-permute-done((bf16[64,1024]{1,0:T(8,128)(2,1)S(1)}, bf16[64,1024]{1,0:T(8,128)(2,1)S(1)}, u32[]{:S(2)}, u32[]{:S(2)}) %collective-permute-start.19) | collective-permute-done | bytes 131104 | tf_op jit(solution)/shard_map/ppermute | solution.py:323
  82.5 5.4 %collective-permute-done.24.refs_3_ = bf16[2,64,1024]{2,1,0:T(8,128)(2,1)S(1)} collective-permute-done((bf16[2,64,1024]{2,1,0:T(8,128)(2,1)S(1)}, bf16[2,64,1024]{2,1,0:T(8,128)(2,1)S(1)}, u32[]{:S(2)}, u32[]{:S(2)}) %collective-permute-start.24) | collective-permute-done | bytes 262176 | tf_op jit(solution)/shard_map/ppermute | solution.py:323
  88.0 2.8 %collective-permute-done.23.refs_2_ = bf16[2,64,1024]{2,1,0:T(8,128)(2,1)S(1)} collective-permute-done((bf16[2,64,1024]{2,1,0:T(8,128)(2,1)S(1)}, bf16[2,64,1024]{2,1,0:T(8,128)(2,1)S(1)}, u32[]{:S(2)}, u32[]{:S(2)}) %collective-permute-start.23) | collective-permute-done | bytes 262176 | tf_op jit(solution)/shard_map/ppermute | solution.py:323
  90.8 2.1 front.3
  96.2 2.3 attention_forward.3
  98.5 3.6 %attention_backward.2 = (f32[512,128]{1,0:T(8,128)S(1)}, f32[2,512,128]{2,1,0:T(8,128)S(1)}, f32[2,512,128]{2,1,0:T(8,128)S(1)}) custom-call(s32[8]{0:T(128)S(1)} %stack.91.at, bf16[512,128]{1,0:T(8,128)(2,1)S(1)} %get-tuple-element.192.q, bf16[2,512,128]{2,1,0:T(8,128)(2,1)S(1)} %get-tuple-element.193.kv, ...), custom_call_target="tpu_custom_call" | custom-call | tf_op jit(solution)/shard_map/attention_backward/pallas_call | solution.py:347
  102.7 2.1 early_grads.2
  104.9 2.8 %inputs_backward.2 = (bf16[512,384]{1,0:T(8,128)(2,1)S(1)}, bf16[64,128]{1,0:T(8,128)(2,1)S(1)}, f32[2,64,1024]{2,1,0:T(8,128)S(1)}, bf16[2,64,1024]{2,1,0:T(8,1...) custom-call(s32[8]{0:T(128)S(1)} %stack.91.at, ...), custom_call_target="tpu_custom_call" | custom-call | tf_op jit(solution)/shard_map/inputs_backward/pallas_call | solution.py:347
  115.7 10.1 %collective-permute-done.28 = bf16[1152,128]{1,0:T(8,128)(2,1)S(1)} collective-permute-done((bf16[1152,128]{1,0:T(8,128)(2,1)S(1)}, bf16[1152,128]{1,0:T(8,128)(2,1)S(1)}, u32[]{:S(2)}, u32[]{:S(2)}) %collective-permute-start.28) | collective-permute-done | bytes 294944 | tf_op jit(solution)/shard_map/ppermute | solution.py:323
  134.7 6.6 %collective-permute-done.35 = bf16[2,384,128]{2,1,0:T(8,128)(2,1)S(1)} collective-permute-done((bf16[2,384,128]{2,1,0:T(8,128)(2,1)S(1)}, bf16[2,384,128]{2,1,0:T(8,128)(2,1)S(1)}, u32[]{:S(2)}, u32[]{:S(2)}) %collective-permute-start.35) | collective-permute-done | bytes 196640 | tf_op jit(solution)/shard_map/ppermute | solution.py:323
  141.6 2.0 collective-permute-start.39
  147.2 9.1 %collective-permute-done.39 = bf16[1152,128]{1,0:T(8,128)(2,1)S(1)} collective-permute-done((bf16[1152,128]{1,0:T(8,128)(2,1)S(1)}, bf16[1152,128]{1,0:T(8,128)(2,1)S(1)}, u32[]{:S(2)}, u32[]{:S(2)}) %collective-permute-start.39) | collective-permute-done | bytes 294944 | tf_op jit(solution)/shard_map/ppermute | solution.py:323
  158.3 2.1 early_grads.3
  160.5 3.6 %attention_backward.3 = (f32[512,128]{1,0:T(8,128)S(1)}, f32[2,512,128]{2,1,0:T(8,128)S(1)}, f32[2,512,128]{2,1,0:T(8,128)S(1)}) custom-call(s32[8]{0:T(128)S(1)} %stack.91.at, bf16[512,128]{1,0:T(8,128)(2,1)S(1)} %get-tuple-element.157.q, bf16[2,512,128]{2,1,0:T(8,128)(2,1)S(1)} %get-tuple-element.158.kv, ...), custom_call_target="tpu_custom_call" | custom-call | tf_op jit(solution)/shard_map/attention_backward/pallas_call | solution.py:347
  165.9 2.3 collective-permute-start.46
  168.2 2.6 %inputs_backward.3 = (bf16[512,384]{1,0:T(8,128)(2,1)S(1)}, bf16[64,128]{1,0:T(8,128)(2,1)S(1)}, f32[2,64,1024]{2,1,0:T(8,128)S(1)}, bf16[2,64,1024]{2,1,0:T(8,1...) custom-call(s32[8]{0:T(128)S(1)} %stack.91.at, ...), custom_call_target="tpu_custom_call" | custom-call | tf_op jit(solution)/shard_map/inputs_backward/pallas_call | solution.py:347
  170.7 2.0 collective-permute-done.45.rest_0_
  178.5 3.4 %collective-permute-done.46 = bf16[1152,128]{1,0:T(8,128)(2,1)S(1)} collective-permute-done((bf16[1152,128]{1,0:T(8,128)(2,1)S(1)}, bf16[1152,128]{1,0:T(8,128)(2,1)S(1)}, u32[]{:S(2)}, u32[]{:S(2)}) %collective-permute-start.46) | collective-permute-done | bytes 294944 | tf_op jit(solution)/shard_map/ppermute | solution.py:323
  182.9 3.3 %collective-permute-done.48.refs_2_ = bf16[2,64,1024]{2,1,0:T(8,128)(2,1)S(1)} collective-permute-done((bf16[2,64,1024]{2,1,0:T(8,128)(2,1)S(1)}, bf16[2,64,1024]{2,1,0:T(8,128)(2,1)S(1)}, u32[]{:S(2)}, u32[]{:S(2)}) %collective-permute-start.48) | collective-permute-done | bytes 262176 | tf_op jit(solution)/shard_map/ppermute | solution.py:323
  187.3 2.1 collective-permute-start.60
  189.4 2.6 %collective-permute-start.51 = (bf16[1152,128]{1,0:T(8,128)(2,1)S(1)}, bf16[1152,128]{1,0:T(8,128)(2,1)S(1)}, u32[]{:S(2)}, u32[]{:S(2)}) collective-permute-start(bf16[1152,128]{1,0:T(8,128)(2,1)S(1)} %get-tuple-element.260), channel_id=1, source_target_pairs={{0,8},{1,9},{2,10},{3,11},{4,12},{5,13},{6,14},{7,15},{8,0},{9,1},... | collective-permute-start | bytes 884744 | tf_op jit(solution)/shard_map/ppermute | solution.py:323
  192.5 12.8 %collective-permute-done.50.rest_0_ = bf16[64,1024]{1,0:T(8,128)(2,1)S(1)} collective-permute-done((bf16[64,1024]{1,0:T(8,128)(2,1)S(1)}, bf16[64,1024]{1,0:T(8,128)(2,1)S(1)}, u32[]{:S(2)}, u32[]{:S(2)}) %collective-permute-start.50) | collective-permute-done | bytes 131104 | tf_op jit(solution)/shard_map/ppermute | solution.py:323
  205.3 4.4 %collective-permute-done.51 = bf16[1152,128]{1,0:T(8,128)(2,1)S(1)} collective-permute-done((bf16[1152,128]{1,0:T(8,128)(2,1)S(1)}, bf16[1152,128]{1,0:T(8,128)(2,1)S(1)}, u32[]{:S(2)}, u32[]{:S(2)}) %collective-permute-start.51) | collective-permute-done | bytes 294944 | tf_op jit(solution)/shard_map/ppermute | solution.py:323
  213.1 4.1 %collective-permute-done.52 = bf16[64,1024]{1,0:T(8,128)(2,1)S(1)} collective-permute-done((bf16[64,1024]{1,0:T(8,128)(2,1)S(1)}, bf16[64,1024]{1,0:T(8,128)(2,1)S(1)}, u32[]{:S(2)}, u32[]{:S(2)}) %collective-permute-start.52) | collective-permute-done | bytes 131104 | tf_op jit(solution)/shard_map/ppermute | solution.py:323
  217.2 3.4 %collective-permute-start.53 = (bf16[2,64,1024]{2,1,0:T(8,128)(2,1)S(1)}, bf16[2,64,1024]{2,1,0:T(8,128)(2,1)S(1)}, u32[]{:S(2)}, u32[]{:S(2)}) collective-permute-start(bf16[2,64,1024]{2,1,0:T(8,128)(2,1)S(1)} %pad_maximum_fusion.3), channel_id=1, source_target_pairs={{0,8},{1,9},{2,10},{3,11},{4,12},{5,13},{6,14},{7,15},{8,0},{9,1},... | collective-permute-start | bytes 786440 | tf_op jit(solution)/shard_map/ppermute | solution.py:323
  222.3 3.7 %collective-permute-start.62 = (bf16[448,128]{1,0:T(8,128)(2,1)S(1)}, bf16[448,128]{1,0:T(8,128)(2,1)S(1)}, u32[]{:S(2)}, u32[]{:S(2)}) collective-permute-start(bf16[448,128]{1,0:T(8,128)(2,1)S(1)} %get-tuple-element.316), channel_id=1, source_target_pairs={{0,20},{1,21},{2,22},{3,23},{4,16},{5,17},{6,18},{7,19},{8,28},{9,... | collective-permute-start | bytes 344072 | tf_op jit(solution)/shard_map/ppermute | solution.py:323
  225.9 2.7 %collective-permute-done.53 = bf16[2,64,1024]{2,1,0:T(8,128)(2,1)S(1)} collective-permute-done((bf16[2,64,1024]{2,1,0:T(8,128)(2,1)S(1)}, bf16[2,64,1024]{2,1,0:T(8,128)(2,1)S(1)}, u32[]{:S(2)}, u32[]{:S(2)}) %collective-permute-start.53) | collective-permute-done | bytes 262176 | tf_op jit(solution)/shard_map/ppermute | solution.py:323
  231.3 2.1 collective-permute-start.63
  233.5 2.5 %unpack_grads.1 = (f32[3,128,512]{2,1,0:T(8,128)}, f32[512,128]{1,0:T(8,128)}, f32[128,2048]{1,0:T(8,128)}, f32[2048,128]{1,0:T(8,128)}, f32[3,512]{1,0:T(4,128)...) custom-call(s32[8]{0:T(128)S(1)} %stack.91.at, bf16[1152,128]{1,0:T(8,128)(2,1)S(1)} %get-tuple-element.297.refs_0_, ...), custom_call_target="tpu_custom_call" | custom-call | tf_op jit(solution)/shard_map/unpack_grads/pallas_call | solution.py:347
  (167 shorter events, 74.1 us)
Async XLA Ops:
  2.6 12.4 %collective-permute-start.5 = (bf16[1584,128]{1,0:T(8,128)(2,1)S(1)}, bf16[1584,128]{1,0:T(8,128)(2,1)S(1)}, u32[]{:S(2)}, u32[]{:S(2)}) collective-permute-start(bf16[1584,128]{1,0:T(8,128)(2,1)S(1)} %get-tuple-element.153), channel_id=1, source_target_pairs={{0,16},{1,17},{2,18},{3,19},{4,20},{5,21},{6,22},{7,23},{8,24},{9,... | collective-permute-start | bytes 1216520 | tf_op jit(solution)/shard_map/ppermute | solution.py:323
  5.6 13.5 %collective-permute-start.2 = (bf16[128,512]{1,0:T(8,128)(2,1)S(1)}, bf16[128,512]{1,0:T(8,128)(2,1)S(1)}, u32[]{:S(2)}, u32[]{:S(2)}) collective-permute-start(bf16[128,512]{1,0:T(8,128)(2,1)S(1)} %get-tuple-element.150), channel_id=1, source_target_pairs={{0,12},{1,13},{2,14},{3,15},{4,8},{5,9},{6,10},{7,11},{8,4},{9,5},... | collective-permute-start | bytes 393224 | tf_op jit(solution)/shard_map/ppermute | solution.py:323
  9.2 11.5 %collective-permute-start.1 = (bf16[128,512]{1,0:T(8,128)(2,1)S(1)}, bf16[128,512]{1,0:T(8,128)(2,1)S(1)}, u32[]{:S(2)}, u32[]{:S(2)}) collective-permute-start(bf16[128,512]{1,0:T(8,128)(2,1)S(1)} %get-tuple-element.150), channel_id=1, source_target_pairs={{0,8},{1,9},{2,10},{3,11},{4,12},{5,13},{6,14},{7,15},{8,0},{9,1},... | collective-permute-start | bytes 393224 | tf_op jit(solution)/shard_map/ppermute | solution.py:323
  9.3 20.2 %collective-permute-start = (bf16[128,1024]{1,0:T(8,128)(2,1)S(1)}, bf16[128,1024]{1,0:T(8,128)(2,1)S(1)}, u32[]{:S(2)}, u32[]{:S(2)}) collective-permute-start(bf16[128,1024]{1,0:T(8,128)(2,1)S(1)} %get-tuple-element.149.refs_0_), channel_id=1, source_target_pairs={{0,4},{1,5},{2,6},{3,7},{4,0},{5,1},{6,2},{7,3},{8,12},{9,13},{10,... | collective-permute-start | bytes 786440 | tf_op jit(solution)/shard_map/ppermute | solution.py:323
  15.0 13.1 %collective-permute-start.8 = (bf16[512,512]{1,0:T(8,128)(2,1)S(1)}, bf16[512,512]{1,0:T(8,128)(2,1)S(1)}, u32[]{:S(2)}, u32[]{:S(2)}) collective-permute-start(bf16[512,512]{1,0:T(8,128)(2,1)S(1)} %get-tuple-element.162), channel_id=1, source_target_pairs={{0,16},{1,17},{2,18},{3,19},{4,20},{5,21},{6,22},{7,23},{8,24},{9,... | collective-permute-start | bytes 1572872 | tf_op jit(solution)/shard_map/ppermute | solution.py:323
  19.1 6.4 %collective-permute-start.4 = (bf16[128,512]{1,0:T(8,128)(2,1)S(1)}, bf16[128,512]{1,0:T(8,128)(2,1)S(1)}, u32[]{:S(2)}, u32[]{:S(2)}) collective-permute-start(bf16[128,512]{1,0:T(8,128)(2,1)S(1)} %collective-permute-done.2.refs_3_), channel_id=1, source_target_pairs={{0,1},{1,0},{2,3},{3,2},{4,5},{5,4},{6,7},{7,6},{8,9},{9,8},{10,11... | collective-permute-start | bytes 393224 | tf_op jit(solution)/shard_map/ppermute | solution.py:323
  20.7 7.2 %collective-permute-start.3 = (bf16[128,512]{1,0:T(8,128)(2,1)S(1)}, bf16[128,512]{1,0:T(8,128)(2,1)S(1)}, u32[]{:S(2)}, u32[]{:S(2)}) collective-permute-start(bf16[128,512]{1,0:T(8,128)(2,1)S(1)} %collective-permute-done.1.refs_2_), channel_id=1, source_target_pairs={{0,1},{1,0},{2,3},{3,2},{4,5},{5,4},{6,7},{7,6},{8,9},{9,8},{10,11... | collective-permute-start | bytes 393224 | tf_op jit(solution)/shard_map/ppermute | solution.py:323
  28.1 16.2 %collective-permute-start.10 = (bf16[320,1024]{1,0:T(8,128)(2,1)S(1)}, bf16[320,1024]{1,0:T(8,128)(2,1)S(1)}, u32[]{:S(2)}, u32[]{:S(2)}) collective-permute-start(bf16[320,1024]{1,0:T(8,128)(2,1)S(1)} %get-tuple-element.167), channel_id=1, source_target_pairs={{0,16},{1,17},{2,18},{3,19},{4,20},{5,21},{6,22},{7,23},{8,24},{9,... | collective-permute-start | bytes 1966088 | tf_op jit(solution)/shard_map/ppermute | solution.py:323
  32.2 8.3 %collective-permute-start.11 = (bf16[128,1024]{1,0:T(8,128)(2,1)S(1)}, bf16[128,1024]{1,0:T(8,128)(2,1)S(1)}, u32[]{:S(2)}, u32[]{:S(2)}) collective-permute-start(bf16[128,1024]{1,0:T(8,128)(2,1)S(1)} %get-tuple-element.169.refs_0_), channel_id=1, source_target_pairs={{0,4},{1,5},{2,6},{3,7},{4,0},{5,1},{6,2},{7,3},{8,12},{9,13},{10,... | collective-permute-start | bytes 786440 | tf_op jit(solution)/shard_map/ppermute | solution.py:323
  49.9 17.7 %collective-permute-start.15 = (bf16[2,64,1024]{2,1,0:T(8,128)(2,1)S(1)}, bf16[2,64,1024]{2,1,0:T(8,128)(2,1)S(1)}, u32[]{:S(2)}, u32[]{:S(2)}) collective-permute-start(bf16[2,64,1024]{2,1,0:T(8,128)(2,1)S(1)} %get-tuple-element.177), channel_id=1, source_target_pairs={{0,1},{1,0},{2,3},{3,2},{4,5},{5,4},{6,7},{7,6},{8,9},{9,8},{10,11... | collective-permute-start | bytes 786440 | tf_op jit(solution)/shard_map/ppermute | solution.py:323
  51.5 16.1 %collective-permute-start.16 = (bf16[2,64,1024]{2,1,0:T(8,128)(2,1)S(1)}, bf16[2,64,1024]{2,1,0:T(8,128)(2,1)S(1)}, u32[]{:S(2)}, u32[]{:S(2)}) collective-permute-start(bf16[2,64,1024]{2,1,0:T(8,128)(2,1)S(1)} %get-tuple-element.178), channel_id=1, source_target_pairs={{0,16},{1,17},{2,18},{3,19},{4,20},{5,21},{6,22},{7,23},{8,24},{9,... | collective-permute-start | bytes 786440 | tf_op jit(solution)/shard_map/ppermute | solution.py:323
  52.0 15.6 %collective-permute-start.17 = (bf16[2,64,1024]{2,1,0:T(8,128)(2,1)S(1)}, bf16[2,64,1024]{2,1,0:T(8,128)(2,1)S(1)}, u32[]{:S(2)}, u32[]{:S(2)}) collective-permute-start(bf16[2,64,1024]{2,1,0:T(8,128)(2,1)S(1)} %get-tuple-element.179), channel_id=1, source_target_pairs={{0,17},{1,16},{2,19},{3,18},{4,21},{5,20},{6,23},{7,22},{8,25},{9,... | collective-permute-start | bytes 786440 | tf_op jit(solution)/shard_map/ppermute | solution.py:323
  53.5 8.1 %collective-permute-start.14 = (bf16[128,512]{1,0:T(8,128)(2,1)S(1)}, bf16[128,512]{1,0:T(8,128)(2,1)S(1)}, u32[]{:S(2)}, u32[]{:S(2)}) collective-permute-start(bf16[128,512]{1,0:T(8,128)(2,1)S(1)} %get-tuple-element.175), channel_id=1, source_target_pairs={{0,12},{1,13},{2,14},{3,15},{4,8},{5,9},{6,10},{7,11},{8,4},{9,5},... | collective-permute-start | bytes 393224 | tf_op jit(solution)/shard_map/ppermute | solution.py:323
  57.1 10.5 %collective-permute-start.13 = (bf16[128,512]{1,0:T(8,128)(2,1)S(1)}, bf16[128,512]{1,0:T(8,128)(2,1)S(1)}, u32[]{:S(2)}, u32[]{:S(2)}) collective-permute-start(bf16[128,512]{1,0:T(8,128)(2,1)S(1)} %get-tuple-element.175), channel_id=1, source_target_pairs={{0,8},{1,9},{2,10},{3,11},{4,12},{5,13},{6,14},{7,15},{8,0},{9,1},... | collective-permute-start | bytes 393224 | tf_op jit(solution)/shard_map/ppermute | solution.py:323
  79.0 9.0 %collective-permute-start.24 = (bf16[2,64,1024]{2,1,0:T(8,128)(2,1)S(1)}, bf16[2,64,1024]{2,1,0:T(8,128)(2,1)S(1)}, u32[]{:S(2)}, u32[]{:S(2)}) collective-permute-start(bf16[2,64,1024]{2,1,0:T(8,128)(2,1)S(1)} %pad_maximum_fusion.1.refs_0_), channel_id=1, source_target_pairs={{0,17},{1,16},{2,19},{3,18},{4,21},{5,20},{6,23},{7,22},{8,25},{9,... | collective-permute-start | bytes 786440 | tf_op jit(solution)/shard_map/ppermute | solution.py:323
  80.6 10.3 %collective-permute-start.23 = (bf16[2,64,1024]{2,1,0:T(8,128)(2,1)S(1)}, bf16[2,64,1024]{2,1,0:T(8,128)(2,1)S(1)}, u32[]{:S(2)}, u32[]{:S(2)}) collective-permute-start(bf16[2,64,1024]{2,1,0:T(8,128)(2,1)S(1)} %pad_maximum_fusion.1.refs_0_), channel_id=1, source_target_pairs={{0,16},{1,17},{2,18},{3,19},{4,20},{5,21},{6,22},{7,23},{8,24},{9,... | collective-permute-start | bytes 786440 | tf_op jit(solution)/shard_map/ppermute | solution.py:323
  82.0 8.8 %collective-permute-start.22 = (bf16[2,64,1024]{2,1,0:T(8,128)(2,1)S(1)}, bf16[2,64,1024]{2,1,0:T(8,128)(2,1)S(1)}, u32[]{:S(2)}, u32[]{:S(2)}) collective-permute-start(bf16[2,64,1024]{2,1,0:T(8,128)(2,1)S(1)} %pad_maximum_fusion.1.refs_0_), channel_id=1, source_target_pairs={{0,1},{1,0},{2,3},{3,2},{4,5},{5,4},{6,7},{7,6},{8,9},{9,8},{10,11... | collective-permute-start | bytes 786440 | tf_op jit(solution)/shard_map/ppermute | solution.py:323
  108.9 6.7 %collective-permute-start.34 = (bf16[2,2,384,128]{3,2,1,0:T(8,128)(2,1)S(1)}, bf16[2,2,384,128]{3,2,1,0:T(8,128)(2,1)S(1)}, u32[]{:S(2)}, u32[]{:S(2)}) collective-permute-start(bf16[2,2,384,128]{3,2,1,0:T(8,128)(2,1)S(1)} %get-tuple-element.213), channel_id=1, source_target_pairs={{0,2},{1,3},{2,0},{3,1},{4,6},{5,7},{6,4},{7,5},{8,10},{9,11},{10,... | collective-permute-start | bytes 1179656 | tf_op jit(solution)/shard_map/ppermute | solution.py:323
  109.7 16.1 %collective-permute-start.28 = (bf16[1152,128]{1,0:T(8,128)(2,1)S(1)}, bf16[1152,128]{1,0:T(8,128)(2,1)S(1)}, u32[]{:S(2)}, u32[]{:S(2)}) collective-permute-start(bf16[1152,128]{1,0:T(8,128)(2,1)S(1)} %get-tuple-element.301), channel_id=1, source_target_pairs={{0,8},{1,9},{2,10},{3,11},{4,12},{5,13},{6,14},{7,15},{8,0},{9,1},... | collective-permute-start | bytes 884744 | tf_op jit(solution)/shard_map/ppermute | solution.py:323
  110.5 15.3 %collective-permute-start.29 = (bf16[2,64,1024]{2,1,0:T(8,128)(2,1)S(1)}, bf16[2,64,1024]{2,1,0:T(8,128)(2,1)S(1)}, u32[]{:S(2)}, u32[]{:S(2)}) collective-permute-start(bf16[2,64,1024]{2,1,0:T(8,128)(2,1)S(1)} %get-tuple-element.215), channel_id=1, source_target_pairs={{0,1},{1,0},{2,3},{3,2},{4,5},{5,4},{6,7},{7,6},{8,9},{9,8},{10,11... | collective-permute-start | bytes 786440 | tf_op jit(solution)/shard_map/ppermute | solution.py:323
  111.9 13.9 %collective-permute-start.30 = (bf16[2,64,1024]{2,1,0:T(8,128)(2,1)S(1)}, bf16[2,64,1024]{2,1,0:T(8,128)(2,1)S(1)}, u32[]{:S(2)}, u32[]{:S(2)}) collective-permute-start(bf16[2,64,1024]{2,1,0:T(8,128)(2,1)S(1)} %get-tuple-element.216), channel_id=1, source_target_pairs={{0,16},{1,17},{2,18},{3,19},{4,20},{5,21},{6,22},{7,23},{8,24},{9,... | collective-permute-start | bytes 786440 | tf_op jit(solution)/shard_map/ppermute | solution.py:323
  112.4 13.3 %collective-permute-start.31 = (bf16[2,64,1024]{2,1,0:T(8,128)(2,1)S(1)}, bf16[2,64,1024]{2,1,0:T(8,128)(2,1)S(1)}, u32[]{:S(2)}, u32[]{:S(2)}) collective-permute-start(bf16[2,64,1024]{2,1,0:T(8,128)(2,1)S(1)} %get-tuple-element.217), channel_id=1, source_target_pairs={{0,17},{1,16},{2,19},{3,18},{4,21},{5,20},{6,23},{7,22},{8,25},{9,... | collective-permute-start | bytes 786440 | tf_op jit(solution)/shard_map/ppermute | solution.py:323
  127.5 13.7 %collective-permute-start.36 = (bf16[2,64,1024]{2,1,0:T(8,128)(2,1)S(1)}, bf16[2,64,1024]{2,1,0:T(8,128)(2,1)S(1)}, u32[]{:S(2)}, u32[]{:S(2)}) collective-permute-start(bf16[2,64,1024]{2,1,0:T(8,128)(2,1)S(1)} %get-tuple-element.224), channel_id=1, source_target_pairs={{0,1},{1,0},{2,3},{3,2},{4,5},{5,4},{6,7},{7,6},{8,9},{9,8},{10,11... | collective-permute-start | bytes 786440 | tf_op jit(solution)/shard_map/ppermute | solution.py:323
  128.9 12.4 %collective-permute-start.37 = (bf16[2,64,1024]{2,1,0:T(8,128)(2,1)S(1)}, bf16[2,64,1024]{2,1,0:T(8,128)(2,1)S(1)}, u32[]{:S(2)}, u32[]{:S(2)}) collective-permute-start(bf16[2,64,1024]{2,1,0:T(8,128)(2,1)S(1)} %get-tuple-element.226), channel_id=1, source_target_pairs={{0,16},{1,17},{2,18},{3,19},{4,20},{5,21},{6,22},{7,23},{8,24},{9,... | collective-permute-start | bytes 786440 | tf_op jit(solution)/shard_map/ppermute | solution.py:323
  129.4 12.2 %collective-permute-start.38 = (bf16[2,64,1024]{2,1,0:T(8,128)(2,1)S(1)}, bf16[2,64,1024]{2,1,0:T(8,128)(2,1)S(1)}, u32[]{:S(2)}, u32[]{:S(2)}) collective-permute-start(bf16[2,64,1024]{2,1,0:T(8,128)(2,1)S(1)} %get-tuple-element.228), channel_id=1, source_target_pairs={{0,17},{1,16},{2,19},{3,18},{4,21},{5,20},{6,23},{7,22},{8,25},{9,... | collective-permute-start | bytes 786440 | tf_op jit(solution)/shard_map/ppermute | solution.py:323
  131.0 10.2 %collective-permute-start.35 = (bf16[2,384,128]{2,1,0:T(8,128)(2,1)S(1)}, bf16[2,384,128]{2,1,0:T(8,128)(2,1)S(1)}, u32[]{:S(2)}, u32[]{:S(2)}) collective-permute-start(bf16[2,384,128]{2,1,0:T(8,128)(2,1)S(1)} %pad_maximum_fusion.5), channel_id=1, source_target_pairs={{0,8},{1,9},{2,10},{3,11},{4,12},{5,13},{6,14},{7,15},{8,0},{9,1},... | collective-permute-start | bytes 589832 | tf_op jit(solution)/shard_map/ppermute | solution.py:323
  133.3 8.0 %collective-permute-start.33 = (bf16[64,1024]{1,0:T(8,128)(2,1)S(1)}, bf16[64,1024]{1,0:T(8,128)(2,1)S(1)}, u32[]{:S(2)}, u32[]{:S(2)}) collective-permute-start(bf16[64,1024]{1,0:T(8,128)(2,1)S(1)} %join_backward.2.g), channel_id=1, source_target_pairs={{0,4},{1,5},{2,6},{3,7},{4,0},{5,1},{6,2},{7,3},{8,12},{9,13},{10,... | collective-permute-start | bytes 393224 | tf_op jit(solution)/shard_map/ppermute | solution.py:323
  141.6 14.7 %collective-permute-start.39 = (bf16[1152,128]{1,0:T(8,128)(2,1)S(1)}, bf16[1152,128]{1,0:T(8,128)(2,1)S(1)}, u32[]{:S(2)}, u32[]{:S(2)}) collective-permute-start(bf16[1152,128]{1,0:T(8,128)(2,1)S(1)} %get-tuple-element.230), channel_id=1, source_target_pairs={{0,8},{1,9},{2,10},{3,11},{4,12},{5,13},{6,14},{7,15},{8,0},{9,1},... | collective-permute-start | bytes 884744 | tf_op jit(solution)/shard_map/ppermute | solution.py:323
  143.6 12.7 %collective-permute-start.42 = (bf16[2,64,1024]{2,1,0:T(8,128)(2,1)S(1)}, bf16[2,64,1024]{2,1,0:T(8,128)(2,1)S(1)}, u32[]{:S(2)}, u32[]{:S(2)}) collective-permute-start(bf16[2,64,1024]{2,1,0:T(8,128)(2,1)S(1)} %pad_maximum_fusion.2.refs_0_), channel_id=1, source_target_pairs={{0,17},{1,16},{2,19},{3,18},{4,21},{5,20},{6,23},{7,22},{8,25},{9,... | collective-permute-start | bytes 786440 | tf_op jit(solution)/shard_map/ppermute | solution.py:323
  145.1 11.6 %collective-permute-start.41 = (bf16[2,64,1024]{2,1,0:T(8,128)(2,1)S(1)}, bf16[2,64,1024]{2,1,0:T(8,128)(2,1)S(1)}, u32[]{:S(2)}, u32[]{:S(2)}) collective-permute-start(bf16[2,64,1024]{2,1,0:T(8,128)(2,1)S(1)} %pad_maximum_fusion.2.refs_0_), channel_id=1, source_target_pairs={{0,16},{1,17},{2,18},{3,19},{4,20},{5,21},{6,22},{7,23},{8,24},{9,... | collective-permute-start | bytes 786440 | tf_op jit(solution)/shard_map/ppermute | solution.py:323
  146.5 10.2 %collective-permute-start.40 = (bf16[2,64,1024]{2,1,0:T(8,128)(2,1)S(1)}, bf16[2,64,1024]{2,1,0:T(8,128)(2,1)S(1)}, u32[]{:S(2)}, u32[]{:S(2)}) collective-permute-start(bf16[2,64,1024]{2,1,0:T(8,128)(2,1)S(1)} %pad_maximum_fusion.2.refs_0_), channel_id=1, source_target_pairs={{0,1},{1,0},{2,3},{3,2},{4,5},{5,4},{6,7},{7,6},{8,9},{9,8},{10,11... | collective-permute-start | bytes 786440 | tf_op jit(solution)/shard_map/ppermute | solution.py:323
  165.3 7.4 %collective-permute-start.45 = (bf16[64,1024]{1,0:T(8,128)(2,1)S(1)}, bf16[64,1024]{1,0:T(8,128)(2,1)S(1)}, u32[]{:S(2)}, u32[]{:S(2)}) collective-permute-start(bf16[64,1024]{1,0:T(8,128)(2,1)S(1)} %get-tuple-element.249), channel_id=1, source_target_pairs={{0,4},{1,5},{2,6},{3,7},{4,0},{5,1},{6,2},{7,3},{8,12},{9,13},{10,... | collective-permute-start | bytes 393224 | tf_op jit(solution)/shard_map/ppermute | solution.py:323
  165.9 16.0 %collective-permute-start.46 = (bf16[1152,128]{1,0:T(8,128)(2,1)S(1)}, bf16[1152,128]{1,0:T(8,128)(2,1)S(1)}, u32[]{:S(2)}, u32[]{:S(2)}) collective-permute-start(bf16[1152,128]{1,0:T(8,128)(2,1)S(1)} %get-tuple-element.298), channel_id=1, source_target_pairs={{0,8},{1,9},{2,10},{3,11},{4,12},{5,13},{6,14},{7,15},{8,0},{9,1},... | collective-permute-start | bytes 884744 | tf_op jit(solution)/shard_map/ppermute | solution.py:323
  172.7 10.2 %collective-permute-start.49 = (bf16[2,64,1024]{2,1,0:T(8,128)(2,1)S(1)}, bf16[2,64,1024]{2,1,0:T(8,128)(2,1)S(1)}, u32[]{:S(2)}, u32[]{:S(2)}) collective-permute-start(bf16[2,64,1024]{2,1,0:T(8,128)(2,1)S(1)} %get-tuple-element.257), channel_id=1, source_target_pairs={{0,17},{1,16},{2,19},{3,18},{4,21},{5,20},{6,23},{7,22},{8,25},{9,... | collective-permute-start | bytes 786440 | tf_op jit(solution)/shard_map/ppermute | solution.py:323
  174.1 12.1 %collective-permute-start.48 = (bf16[2,64,1024]{2,1,0:T(8,128)(2,1)S(1)}, bf16[2,64,1024]{2,1,0:T(8,128)(2,1)S(1)}, u32[]{:S(2)}, u32[]{:S(2)}) collective-permute-start(bf16[2,64,1024]{2,1,0:T(8,128)(2,1)S(1)} %get-tuple-element.255), channel_id=1, source_target_pairs={{0,16},{1,17},{2,18},{3,19},{4,20},{5,21},{6,22},{7,23},{8,24},{9,... | collective-permute-start | bytes 786440 | tf_op jit(solution)/shard_map/ppermute | solution.py:323
  175.7 10.6 %collective-permute-start.47 = (bf16[2,64,1024]{2,1,0:T(8,128)(2,1)S(1)}, bf16[2,64,1024]{2,1,0:T(8,128)(2,1)S(1)}, u32[]{:S(2)}, u32[]{:S(2)}) collective-permute-start(bf16[2,64,1024]{2,1,0:T(8,128)(2,1)S(1)} %get-tuple-element.253), channel_id=1, source_target_pairs={{0,1},{1,0},{2,3},{3,2},{4,5},{5,4},{6,7},{7,6},{8,9},{9,8},{10,11... | collective-permute-start | bytes 786440 | tf_op jit(solution)/shard_map/ppermute | solution.py:323
  178.5 13.5 %collective-permute-start.55 = (bf16[2,2,512,128]{3,2,1,0:T(8,128)(2,1)S(1)}, bf16[2,2,512,128]{3,2,1,0:T(8,128)(2,1)S(1)}, u32[]{:S(2)}, u32[]{:S(2)}) collective-permute-start(bf16[2,2,512,128]{3,2,1,0:T(8,128)(2,1)S(1)} %get-tuple-element.270), channel_id=1, source_target_pairs={{0,2},{1,3},{2,0},{3,1},{4,6},{5,7},{6,4},{7,5},{8,10},{9,11},{10,... | collective-permute-start | bytes 1572872 | tf_op jit(solution)/shard_map/ppermute | solution.py:323
  186.9 18.4 %collective-permute-start.50 = (bf16[64,1024]{1,0:T(8,128)(2,1)S(1)}, bf16[64,1024]{1,0:T(8,128)(2,1)S(1)}, u32[]{:S(2)}, u32[]{:S(2)}) collective-permute-start(bf16[64,1024]{1,0:T(8,128)(2,1)S(1)} %get-tuple-element.259), channel_id=1, source_target_pairs={{0,4},{1,5},{2,6},{3,7},{4,0},{5,1},{6,2},{7,3},{8,12},{9,13},{10,... | collective-permute-start | bytes 393224 | tf_op jit(solution)/shard_map/ppermute | solution.py:323
  187.3 34.9 %collective-permute-start.60 = (bf16[1152,128]{1,0:T(8,128)(2,1)S(1)}, bf16[1152,128]{1,0:T(8,128)(2,1)S(1)}, u32[]{:S(2)}, u32[]{:S(2)}) collective-permute-start(bf16[1152,128]{1,0:T(8,128)(2,1)S(1)} %get-tuple-element.294), channel_id=1, source_target_pairs={{0,20},{1,21},{2,22},{3,23},{4,16},{5,17},{6,18},{7,19},{8,28},{9,... | collective-permute-start | bytes 884744 | tf_op jit(solution)/shard_map/ppermute | solution.py:323
  189.3 32.8 %collective-permute-start.59 = (bf16[1152,128]{1,0:T(8,128)(2,1)S(1)}, bf16[1152,128]{1,0:T(8,128)(2,1)S(1)}, u32[]{:S(2)}, u32[]{:S(2)}) collective-permute-start(bf16[1152,128]{1,0:T(8,128)(2,1)S(1)} %get-tuple-element.295), channel_id=1, source_target_pairs={{0,4},{1,5},{2,6},{3,7},{4,0},{5,1},{6,2},{7,3},{8,12},{9,13},{10,... | collective-permute-start | bytes 884744 | tf_op jit(solution)/shard_map/ppermute | solution.py:323
  189.4 20.3 %collective-permute-start.51 = (bf16[1152,128]{1,0:T(8,128)(2,1)S(1)}, bf16[1152,128]{1,0:T(8,128)(2,1)S(1)}, u32[]{:S(2)}, u32[]{:S(2)}) collective-permute-start(bf16[1152,128]{1,0:T(8,128)(2,1)S(1)} %get-tuple-element.260), channel_id=1, source_target_pairs={{0,8},{1,9},{2,10},{3,11},{4,12},{5,13},{6,14},{7,15},{8,0},{9,1},... | collective-permute-start | bytes 884744 | tf_op jit(solution)/shard_map/ppermute | solution.py:323
  192.1 28.6 %collective-permute-start.56 = (bf16[2,512,128]{2,1,0:T(8,128)(2,1)S(1)}, bf16[2,512,128]{2,1,0:T(8,128)(2,1)S(1)}, u32[]{:S(2)}, u32[]{:S(2)}) collective-permute-start(bf16[2,512,128]{2,1,0:T(8,128)(2,1)S(1)} %pad_maximum_fusion.4), channel_id=1, source_target_pairs={{0,8},{1,9},{2,10},{3,11},{4,12},{5,13},{6,14},{7,15},{8,0},{9,1},... | collective-permute-start | bytes 786440 | tf_op jit(solution)/shard_map/ppermute | solution.py:323
  210.6 6.5 %collective-permute-start.52 = (bf16[64,1024]{1,0:T(8,128)(2,1)S(1)}, bf16[64,1024]{1,0:T(8,128)(2,1)S(1)}, u32[]{:S(2)}, u32[]{:S(2)}) collective-permute-start(bf16[64,1024]{1,0:T(8,128)(2,1)S(1)} %broadcast_select_fusion.4), channel_id=1, source_target_pairs={{0,16},{1,17},{2,18},{3,19},{4,20},{5,21},{6,22},{7,23},{8,24},{9,... | collective-permute-start | bytes 393224 | tf_op jit(solution)/shard_map/ppermute | solution.py:323
  212.2 10.0 %collective-permute-start.58 = (bf16[1152,128]{1,0:T(8,128)(2,1)S(1)}, bf16[1152,128]{1,0:T(8,128)(2,1)S(1)}, u32[]{:S(2)}, u32[]{:S(2)}) collective-permute-start(bf16[1152,128]{1,0:T(8,128)(2,1)S(1)} %get-tuple-element.296), channel_id=1, source_target_pairs={{0,16},{1,17},{2,18},{3,19},{4,20},{5,21},{6,22},{7,23},{8,24},{9,... | collective-permute-start | bytes 884744 | tf_op jit(solution)/shard_map/ppermute | solution.py:323
  217.2 11.5 %collective-permute-start.53 = (bf16[2,64,1024]{2,1,0:T(8,128)(2,1)S(1)}, bf16[2,64,1024]{2,1,0:T(8,128)(2,1)S(1)}, u32[]{:S(2)}, u32[]{:S(2)}) collective-permute-start(bf16[2,64,1024]{2,1,0:T(8,128)(2,1)S(1)} %pad_maximum_fusion.3), channel_id=1, source_target_pairs={{0,8},{1,9},{2,10},{3,11},{4,12},{5,13},{6,14},{7,15},{8,0},{9,1},... | collective-permute-start | bytes 786440 | tf_op jit(solution)/shard_map/ppermute | solution.py:323
  220.8 9.5 %collective-permute-start.57 = (bf16[448,128]{1,0:T(8,128)(2,1)S(1)}, bf16[448,128]{1,0:T(8,128)(2,1)S(1)}, u32[]{:S(2)}, u32[]{:S(2)}) collective-permute-start(bf16[448,128]{1,0:T(8,128)(2,1)S(1)} %get-tuple-element.314), channel_id=1, source_target_pairs={{0,16},{1,17},{2,18},{3,19},{4,20},{5,21},{6,22},{7,23},{8,24},{9,... | collective-permute-start | bytes 344072 | tf_op jit(solution)/shard_map/ppermute | solution.py:323
  222.3 8.1 %collective-permute-start.62 = (bf16[448,128]{1,0:T(8,128)(2,1)S(1)}, bf16[448,128]{1,0:T(8,128)(2,1)S(1)}, u32[]{:S(2)}, u32[]{:S(2)}) collective-permute-start(bf16[448,128]{1,0:T(8,128)(2,1)S(1)} %get-tuple-element.316), channel_id=1, source_target_pairs={{0,20},{1,21},{2,22},{3,23},{4,16},{5,17},{6,18},{7,19},{8,28},{9,... | collective-permute-start | bytes 344072 | tf_op jit(solution)/shard_map/ppermute | solution.py:323
  228.8 8.8 %collective-permute-start.54 = (bf16[3,64,1024]{2,1,0:T(8,128)(2,1)S(1)}, bf16[3,64,1024]{2,1,0:T(8,128)(2,1)S(1)}, u32[]{:S(2)}, u32[]{:S(2)}) collective-permute-start(bf16[3,64,1024]{2,1,0:T(8,128)(2,1)S(1)} %pad_maximum_fusion), channel_id=1, source_target_pairs={{0,1},{1,0},{2,3},{3,2},{4,5},{5,4},{6,7},{7,6},{8,9},{9,8},{10,11... | collective-permute-start | bytes 1179656 | tf_op jit(solution)/shard_map/ppermute | solution.py:323
  (23 other events, 159.9 us)
